TPU v7x, 32 devices: a whole 2x2x4 slice. The times are simulated.
32 devices in a mesh: frame: 8 (over y, x, core), tensor: 4 (over z).
Axes of the slice: x: 2, y: 2, z: 4, core: 2. Of those that a mesh axis runs over, the one named last changes fastest.
Arguments:
- queue_state: float32 [6144, 3072], P('frame', 'tensor'), may hold values from -6 to 6
- fresh_noise: float32 [768, 3072], P(None, 'tensor'), may hold values from -6 to 6
- levels: int32 [8], P('frame'), may hold values from 0 to 49
- reach_slot: int32 [8], P('frame'), may hold values from 1 to 3, as said below
- mod_table: float32 [50, 9216], replicated, may hold values from -3 to 3
- step_table: float32 [50], replicated, may hold values from -0.5 to -0.2
- norm_gain: float32 [2, 128], replicated, may hold values from 1 to 2.5
- input_weight: bfloat16 [3072, 3, 3072], P(None, None, 'tensor'), may hold values from -0.109375 to 0.109375
- output_weight: bfloat16 [3072, 3072], P('tensor'), may hold values from -0.109375 to 0.109375
Outputs:
- advanced: float32 [6144, 3072], P('frame', 'tensor')
Inputs may be any that keep to these rules, and one draw needn't show every extreme that they name: `reach_slot`: some slot with index 3 or more attends to 3 frames on each side.
All inputs are finite; a program needn't handle non-finite values.
Results may differ from a plain program's by a relative error of at most 0.014.
Values may be sent and summed in bfloat16 or wider, within the bound.
No kernel may reach another device: no remote copies, remote signals or barrier semaphores. Data moves between devices by JAX's collectives and lax.ppermute only.
A program may use at most 192 MiB of HBM per device.

v0:
```python
import jax
import jax.numpy as jnp
from jax import lax
from jax.sharding import PartitionSpec as P

REACH = 3
STEPS = 2


epsilon = 1e-06


def passed_along(block, axis, distance):
    devices = range(lax.axis_size(axis))
    route = [(i - distance, i) for i in devices if i - distance in devices]
    return lax.ppermute(block, axis, route)


def head_norm(values, gain):
    scale = lax.rsqrt(jnp.mean(values * values, axis=-1, keepdims=True) + epsilon)
    return values * scale * gain


def absorb(running, block, usable, queries, head_count, head_dim):
    weight_sum, weighted = running
    rows_here = block.shape[0]
    column_count = head_count * head_dim
    key_part = block[:, :column_count].reshape(rows_here, head_count, head_dim)
    value_part = block[:, column_count:].reshape(rows_here, head_count, head_dim)
    scores = jnp.einsum(
        "qhd,khd->hqk", queries, key_part, preferred_element_type=jnp.float32
    ) / jnp.sqrt(jnp.float32(head_dim))
    probs = jnp.where(usable, jnp.exp(scores), jnp.float32(0.0))
    weight_sum = weight_sum + jnp.sum(probs, axis=-1)
    weighted = weighted + jnp.einsum(
        "hqk,khd->hqd", probs.astype(jnp.bfloat16), value_part, preferred_element_type=jnp.float32
    )
    return (weight_sum, weighted)


def on_device(
    queue_state,
    fresh_noise,
    levels,
    reach_slot,
    mod_table,
    step_table,
    norm_gain,
    input_weight,
    output_weight,
):
    rows_here, column_count = queue_state.shape
    tensor_count = lax.axis_size("tensor")
    full_width = column_count * tensor_count
    frames = lax.axis_size("frame")
    slot_index = lax.axis_index("frame")
    tensor_index = lax.axis_index("tensor")
    level = levels[0]
    window_reach = reach_slot[0]
    head_dim = norm_gain.shape[1]
    head_count = column_count // head_dim
    modulation = lax.dynamic_index_in_dim(mod_table, level, 0, keepdims=False)
    step_size = lax.dynamic_index_in_dim(step_table, level, 0, keepdims=False)
    shift_full = modulation[:full_width]
    scale_full = modulation[full_width : 2 * full_width]
    gate_full = modulation[2 * full_width :]

    def own_columns(vector):
        return lax.dynamic_slice_in_dim(vector, tensor_index * column_count, column_count)

    wide_weight = input_weight.reshape(full_width, 3 * column_count)
    latent = queue_state
    advanced = queue_state
    for step_number in range(STEPS):
        if step_number > 0:
            moved = passed_along(advanced.astype(jnp.bfloat16), "frame", 1).astype(advanced.dtype)
            latent = jnp.where(slot_index == 0, fresh_noise, moved)
        row_sums = lax.psum((jnp.sum(latent, axis=1), jnp.sum(latent * latent, axis=1)), "tensor")
        row_mean = row_sums[0] / full_width
        row_var = row_sums[1] / full_width - row_mean * row_mean
        normed = (
            (latent - row_mean[:, None])
            * lax.rsqrt(row_var + epsilon)[:, None]
            * (1.0 + own_columns(scale_full))
            + own_columns(shift_full)
        ).astype(jnp.bfloat16)
        projected = jnp.dot(
            lax.all_gather(normed, "tensor", axis=1, tiled=True),
            wide_weight,
            preferred_element_type=jnp.float32,
        )
        reshaped = projected.reshape(rows_here, 3, head_count, head_dim)
        queries = head_norm(reshaped[:, 0], norm_gain[0]).astype(jnp.bfloat16)
        key_block = head_norm(reshaped[:, 1], norm_gain[1]).astype(jnp.bfloat16)
        values = reshaped[:, 2].astype(jnp.bfloat16)
        packed = jnp.concatenate(
            [key_block.reshape(rows_here, column_count), values.reshape(rows_here, column_count)],
            axis=1,
        )
        running = (
            jnp.zeros((head_count, rows_here), jnp.float32),
            jnp.zeros((head_count, rows_here, head_dim), jnp.float32),
        )
        running = absorb(running, packed, True, queries, head_count, head_dim)
        lower_keys = packed
        upper_keys = packed
        for offset in range(1, REACH + 1):
            lower_keys = passed_along(lower_keys, "frame", 1)
            upper_keys = passed_along(upper_keys, "frame", -1)
            running = absorb(
                running,
                lower_keys,
                (slot_index - offset >= 0) & (offset <= window_reach),
                queries,
                head_count,
                head_dim,
            )
            running = absorb(
                running,
                upper_keys,
                (slot_index + offset < frames) & (offset <= window_reach),
                queries,
                head_count,
                head_dim,
            )
        attended = (running[1] / running[0][..., None]).astype(jnp.bfloat16)
        attended = jnp.transpose(attended, (1, 0, 2)).reshape(rows_here, column_count)
        mixed = lax.psum_scatter(
            lax.dot_general(
                output_weight,
                attended,
                (((0,), (1,)), ((), ())),
                preferred_element_type=jnp.float32,
            ).astype(jnp.bfloat16),
            "tensor",
            scatter_dimension=0,
            tiled=True,
        ).astype(jnp.float32)
        branch = jnp.transpose(mixed)
        advanced = latent + step_size * (latent + own_columns(gate_full) * branch)
    return advanced


def solution(mesh):
    return jax.shard_map(
        on_device,
        mesh=mesh,
        in_specs=(
            P("frame", "tensor"),
            P(None, "tensor"),
            P("frame"),
            P("frame"),
            P(),
            P(),
            P(),
            P(None, None, "tensor"),
            P("tensor", None),
        ),
        out_specs=P("frame", "tensor"),
        check_vma=False,
    )
```

profile of v0, /device:TPU:0, one launch (start us, length us, event | category | flops | bytes accessed | tf_op | source)
XLA Modules:
  0.0 846.4 jit_solution(6395381106011574791)
XLA Ops:
  7.3 2.0 fusion.161
  9.4 13.7 %all-reduce.1 = (f32[768]{0:T(1024)S(1)}, f32[768]{0:T(1024)S(1)}) all-reduce(f32[768]{0:T(1024)S(1)} %get-tuple-element.12, f32[768]{0:T(1024)S(1)} %get-tuple-element.11), channel_id=1, replica_groups=mesh['frame'=8,'tensor'=4] {'tensor'}, use_global_device_ids=true, to_apply=%region_3.4 | all-reduce | flops 1536 | bytes 12288 | tf_op jit(solution)/shard_map/psum | solution.py:78
  25.6 18.8 %copy.40 = bf16[3072,3,768]{0,2,1:T(8,128)(2,1)} copy(bf16[3072,3,768]{2,0,1:T(8,128)(2,1)} %param.16) | data formatting | bytes 28311552 | tf_op args[7]
  44.4 68.9 %all-gather.3.cloned.1.call-done = bf16[768,3072]{1,0:T(8,128)(2,1)} async-done(((bf16[768,768]{1,0:T(8,128)(2,1)}), bf16[768,3072]{1,0:T(8,128)(2,1)}) %all-gather.3.cloned.1.call-update) | async-done | bytes 4718608 | tf_op jit(solution)/shard_map/all_gather | solution.py:88
  113.3 15.4 %fusion.96 = f32[768,3,6,128]{0,3,2,1:T(8,128)S(1)} fusion(bf16[3,6,128,3072]{3,2,1,0:T(8,128)(2,1)} %bitcast.189, bf16[768,3072]{1,0:T(8,128)(2,1)} %all-gather.3.cloned.1.call-done), kind=kOutput, calls=%fused_computation.98 | convolution fusion | flops 10871635968 | bytes 25952256 | tf_op jit(solution)/shard_map/dot_general | solution.py:87
  129.7 1.8 copy-done
  135.0 3.2 collective-permute-start
  138.2 2.0 multiply_convert_fusion.1
  140.3 4.4 fusion
  144.7 5.7 fusion.54
  151.6 1.8 fusion.170
  153.4 3.7 fusion.6
  157.1 38.2 %collective-permute-start.2 = (bf16[768,1536]{0,1:T(8,128)(2,1)S(1)}, bf16[768,1536]{0,1:T(8,128)(2,1)}, u32[]{:S(2)}, u32[]{:S(2)}) collective-permute-start(bf16[768,1536]{0,1:T(8,128)(2,1)S(1)} %collective-permute-done), channel_id=1, source_target_pairs={{0,4},{4,8},{8,12},{12,16},{16,20},{20,24},{24,28},{1,5},{5,9},{9,... | collective-permute-start | bytes 7077896 | tf_op jit(solution)/shard_map/ppermute | solution.py:16
  195.4 3.4 fusion.48
  198.8 3.7 fusion.4
  202.5 3.4 fusion.50
  205.9 2.8 fusion.172
  208.7 3.7 fusion.10
  212.3 25.6 %collective-permute-start.4 = (bf16[768,1536]{0,1:T(8,128)(2,1)}, bf16[768,1536]{0,1:T(8,128)(2,1)}, u32[]{:S(2)}, u32[]{:S(2)}) collective-permute-start(bf16[768,1536]{0,1:T(8,128)(2,1)} %collective-permute-done.2), channel_id=1, source_target_pairs={{0,4},{4,8},{8,12},{12,16},{16,20},{20,24},{24,28},{1,5},{5,9},{9,... | collective-permute-start | bytes 7077896 | tf_op jit(solution)/shard_map/ppermute | solution.py:16
  238.0 2.8 fusion.171
  242.1 3.7 fusion.8
  245.8 4.6 fusion.44
  250.4 4.6 fusion.46
  255.1 1.8 fusion.173
  256.9 3.7 fusion.12
  260.6 3.3 fusion.42
  263.9 2.9 fusion.168
  266.8 3.7 fusion.14
  270.5 8.1 fusion.111
  278.6 8.7 %fusion.98 = bf16[3072,768]{0,1:T(8,128)(2,1)} fusion(bf16[768,768]{0,1:T(8,128)(2,1)} %bitcast.206, bf16[768,3072]{1,0:T(8,128)(2,1)} %param.17), kind=kOutput, calls=%fused_computation.100 | convolution fusion | flops 3626237952 | bytes 10616832 | tf_op jit(solution)/shard_map/dot_general | solution.py:129
  288.6 122.0 %reduce-scatter.3.cloned.1.call-done = bf16[768,768]{0,1:T(8,128)(2,1)} async-done(((bf16[3072,768]{0,1:T(8,128)(2,1)}), bf16[768,768]{0,1:T(8,128)(2,1)}) %reduce-scatter.3.cloned.1.call-update) | async-done | bytes 1179664 | tf_op jit(solution)/shard_map/reduce_scatter | solution.py:128
  410.7 4.2 fusion.110
  414.9 1.8 collective-permute-start.6
  416.7 2.6 collective-permute-done.6
  420.4 11.9 %all-reduce = (f32[768]{0:T(1024)}, f32[768]{0:T(1024)}) all-reduce(f32[768]{0:T(1024)} %get-tuple-element.10, f32[768]{0:T(1024)} %get-tuple-element.9), channel_id=1, replica_groups=mesh['frame'=8,'tensor'=4] {'tensor'}, use_global_device_ids=true, to_apply=%region_17.18 | all-reduce | flops 1536 | bytes 12288 | tf_op jit(solution)/shard_map/psum | solution.py:78
  433.0 1.6 add_convert_fusion
  434.7 101.0 %all-gather.5.cloned.1.call-done = bf16[768,3072]{1,0:T(8,128)(2,1)} async-done(((bf16[768,768]{1,0:T(8,128)(2,1)}), bf16[768,3072]{1,0:T(8,128)(2,1)}) %all-gather.5.cloned.1.call-update) | async-done | bytes 4718608 | tf_op jit(solution)/shard_map/all_gather | solution.py:88
  535.7 15.4 %fusion.94 = f32[768,3,6,128]{0,3,2,1:T(8,128)S(1)} fusion(bf16[3,6,128,3072]{3,2,1,0:T(8,128)(2,1)} %bitcast.190, bf16[768,3072]{1,0:T(8,128)(2,1)} %all-gather.5.cloned.1.call-done), kind=kOutput, calls=%fused_computation.96 | convolution fusion | flops 10871635968 | bytes 25952256 | tf_op jit(solution)/shard_map/dot_general | solution.py:87
  555.1 4.6 collective-permute-start.7
  560.1 2.4 fusion.2
  562.6 2.6 fusion.52
  566.7 1.8 fusion.164
  568.5 3.7 fusion.18
  572.2 44.3 %collective-permute-start.9 = (bf16[768,1536]{0,1:T(8,128)(2,1)}, bf16[768,1536]{0,1:T(8,128)(2,1)}, u32[]{:S(2)}, u32[]{:S(2)}) collective-permute-start(bf16[768,1536]{0,1:T(8,128)(2,1)} %collective-permute-done.7), channel_id=1, source_target_pairs={{0,4},{4,8},{8,12},{12,16},{16,20},{20,24},{24,28},{1,5},{5,9},{9,... | collective-permute-start | bytes 7077896 | tf_op jit(solution)/shard_map/ppermute | solution.py:16
  616.4 1.8 fusion.163
  618.2 2.3 fusion.36
  620.5 3.7 fusion.16
  624.2 2.3 fusion.38
  626.4 1.8 fusion.166
  628.2 3.7 fusion.22
  631.9 26.4 %collective-permute-start.11 = (bf16[768,1536]{0,1:T(8,128)(2,1)}, bf16[768,1536]{0,1:T(8,128)(2,1)}, u32[]{:S(2)}, u32[]{:S(2)}) collective-permute-start(bf16[768,1536]{0,1:T(8,128)(2,1)} %collective-permute-done.9), channel_id=1, source_target_pairs={{0,4},{4,8},{8,12},{12,16},{16,20},{20,24},{24,28},{1,5},{5,9},{9,... | collective-permute-start | bytes 7077896 | tf_op jit(solution)/shard_map/ppermute | solution.py:16
  658.3 3.2 fusion.165
  662.9 2.3 fusion.32
  665.2 4.3 fusion.20
  669.6 3.4 fusion.34
  672.9 1.8 fusion.167
  674.7 3.7 fusion.24
  678.4 2.8 fusion.162
  681.2 6.5 fusion.26
  687.8 3.5 fusion.30
  691.3 10.3 %fusion.102 = bf16[768,6,128]{0,2,1:T(8,128)(2,1)} fusion(f32[6,768,128]{1,2,0:T(8,128)} %fusion.30, f32[6,768,128]{1,2,0:T(8,128)S(1)} %fusion.32, f32[6,768,128]{1,2,0:T(8,128)} %fusion.34, f32[6,768,128]{1,2,0:T(8,128)S(1)} %fusion.36, f32[6,768,128]{1,2,0:T(8,128)S(1)} %fusion.52, f32[6,768,128]{1,2,0:T(8,128)S(1)} %fusion.38, ...), kind=kOutput, calls=%fused_computation.112 | convolution fusion | flops 921305088 | bytes 30689280 | tf_op jit(solution)/shard_map/hqk,khd->hqd/dot_general | solution.py:35
  701.6 8.7 %fusion.99 = bf16[3072,768]{0,1:T(8,128)(2,1)} fusion(bf16[768,768]{0,1:T(8,128)(2,1)} %bitcast.205, bf16[768,3072]{1,0:T(8,128)(2,1)} %param.17), kind=kOutput, calls=%fused_computation.101 | convolution fusion | flops 3626237952 | bytes 10616832 | tf_op jit(solution)/shard_map/dot_general | solution.py:129
  710.3 125.3 %reduce-scatter.5.cloned.1.call-done = bf16[768,768]{0,1:T(8,128)(2,1)} async-done(((bf16[3072,768]{0,1:T(8,128)(2,1)}), bf16[768,768]{0,1:T(8,128)(2,1)}) %reduce-scatter.5.cloned.1.call-update) | async-done | bytes 1179664 | tf_op jit(solution)/shard_map/reduce_scatter | solution.py:128
  835.6 3.8 fusion.101
  (81 shorter events, 19.5 us)
Async XLA Ops:
  6.5 17.5 %copy-start.2 = (f32[768,768]{1,0:T(8,128)S(1)}, f32[768,768]{1,0:T(8,128)}, u32[]{:S(2)}) copy-start(f32[768,768]{1,0:T(8,128)} %param.9) | copy-start | bytes 7077892
  6.5 106.7 %all-gather.3.cloned.1.call-start = ((), (), s32[]{:S(2)}) async-start(), calls=%async_computation.2 | async-start | bytes 5898240 | tf_op jit(solution)/shard_map/all_gather | solution.py:88
  25.5 18.9 %copy-start.13 = (f32[2,128]{1,0:T(2,128)S(1)}, f32[2,128]{1,0:T(2,128)}, u32[]{:S(2)}) copy-start(f32[2,128]{1,0:T(2,128)} %param.15) | copy-start | bytes 3076
  25.5 385.2 %reduce-scatter.3.cloned.1.call-start = ((), (), s32[]{:S(2)}) async-start(), calls=%async_computation.3 | async-start | bytes 5898240 | tf_op jit(solution)/shard_map/reduce_scatter | solution.py:128
  44.4 93.9 %copy-start.11 = (f32[128]{0:T(128)}, f32[128]{0:T(128)S(1)}, u32[]{:S(2)}) copy-start(f32[128]{0:T(128)S(1)} %get-tuple-element.48) | copy-start | bytes 1540
  44.4 95.9 %copy-start.9 = (f32[128]{0:T(128)}, f32[128]{0:T(128)S(1)}, u32[]{:S(2)}) copy-start(f32[128]{0:T(128)S(1)} %get-tuple-element.49) | copy-start | bytes 1540
  128.7 2.8 copy-start
  133.0 17.3 %collective-permute-start.1 = (bf16[768,1536]{0,1:T(8,128)(2,1)}, bf16[768,1536]{0,1:T(8,128)(2,1)}, u32[]{:S(2)}, u32[]{:S(2)}) collective-permute-start(bf16[768,1536]{0,1:T(8,128)(2,1)} %pad_maximum_fusion), channel_id=1, source_target_pairs={{4,0},{8,4},{12,8},{16,12},{20,16},{24,20},{28,24},{5,1},{9,5},{13... | collective-permute-start | bytes 7077896 | tf_op jit(solution)/shard_map/ppermute | solution.py:16
  135.0 22.1 %collective-permute-start = (bf16[768,1536]{0,1:T(8,128)(2,1)}, bf16[768,1536]{0,1:T(8,128)(2,1)S(1)}, u32[]{:S(2)}, u32[]{:S(2)}) collective-permute-start(bf16[768,1536]{0,1:T(8,128)(2,1)} %pad_maximum_fusion), channel_id=1, source_target_pairs={{0,4},{4,8},{8,12},{12,16},{16,20},{20,24},{24,28},{1,5},{5,9},{9,... | collective-permute-start | bytes 7077896 | tf_op jit(solution)/shard_map/ppermute | solution.py:16
  140.3 116.6 %copy-start.5 = (bf16[768,6,128]{0,2,1:T(8,128)(2,1)}, bf16[768,6,128]{0,2,1:T(8,128)(2,1)S(1)}, u32[]{:S(2)}) copy-start(bf16[768,6,128]{0,2,1:T(8,128)(2,1)S(1)} %multiply_convert_fusion.1) | copy-start | bytes 3538948
  150.3 55.5 %collective-permute-start.3 = (bf16[768,1536]{0,1:T(8,128)(2,1)}, bf16[768,1536]{0,1:T(8,128)(2,1)}, u32[]{:S(2)}, u32[]{:S(2)}) collective-permute-start(bf16[768,1536]{0,1:T(8,128)(2,1)} %collective-permute-done.1), channel_id=1, source_target_pairs={{4,0},{8,4},{12,8},{16,12},{20,16},{24,20},{28,24},{5,1},{9,5},{13... | collective-permute-start | bytes 7077896 | tf_op jit(solution)/shard_map/ppermute | solution.py:16
  157.1 55.2 %collective-permute-start.2 = (bf16[768,1536]{0,1:T(8,128)(2,1)S(1)}, bf16[768,1536]{0,1:T(8,128)(2,1)}, u32[]{:S(2)}, u32[]{:S(2)}) collective-permute-start(bf16[768,1536]{0,1:T(8,128)(2,1)S(1)} %collective-permute-done), channel_id=1, source_target_pairs={{0,4},{4,8},{8,12},{12,16},{16,20},{20,24},{24,28},{1,5},{5,9},{9,... | collective-permute-start | bytes 7077896 | tf_op jit(solution)/shard_map/ppermute | solution.py:16
  212.3 42.7 %collective-permute-start.4 = (bf16[768,1536]{0,1:T(8,128)(2,1)}, bf16[768,1536]{0,1:T(8,128)(2,1)}, u32[]{:S(2)}, u32[]{:S(2)}) collective-permute-start(bf16[768,1536]{0,1:T(8,128)(2,1)} %collective-permute-done.2), channel_id=1, source_target_pairs={{0,4},{4,8},{8,12},{12,16},{16,20},{20,24},{24,28},{1,5},{5,9},{9,... | collective-permute-start | bytes 7077896 | tf_op jit(solution)/shard_map/ppermute | solution.py:16
  240.8 23.1 %collective-permute-start.5 = (bf16[768,1536]{0,1:T(8,128)(2,1)}, bf16[768,1536]{0,1:T(8,128)(2,1)}, u32[]{:S(2)}, u32[]{:S(2)}) collective-permute-start(bf16[768,1536]{0,1:T(8,128)(2,1)} %collective-permute-done.3), channel_id=1, source_target_pairs={{4,0},{8,4},{12,8},{16,12},{20,16},{24,20},{28,24},{5,1},{9,5},{13... | collective-permute-start | bytes 7077896 | tf_op jit(solution)/shard_map/ppermute | solution.py:16
  263.9 2.9 copy-start.6
  287.3 0.7 copy-start.14
  287.4 248.3 %all-gather.5.cloned.1.call-start = ((), (), s32[]{:S(2)}) async-start(), calls=%async_computation.4 | async-start | bytes 5898240 | tf_op jit(solution)/shard_map/all_gather | solution.py:88
  410.7 8.7 %copy-start.1 = (f32[768,768]{1,0:T(8,128)S(1)}, f32[768,768]{1,0:T(8,128)}, u32[]{:S(2)}) copy-start(f32[768,768]{1,0:T(8,128)} %param.10) | copy-start | bytes 7077892
  414.9 4.4 collective-permute-start.6
  434.6 401.0 %reduce-scatter.5.cloned.1.call-start = ((), (), s32[]{:S(2)}) async-start(), calls=%async_computation.5 | async-start | bytes 5898240 | tf_op jit(solution)/shard_map/reduce_scatter | solution.py:128
  552.1 7.6 copy-start.12
  553.6 6.5 copy-start.10
  553.6 11.6 %collective-permute-start.8 = (bf16[768,1536]{0,1:T(8,128)(2,1)}, bf16[768,1536]{0,1:T(8,128)(2,1)}, u32[]{:S(2)}, u32[]{:S(2)}) collective-permute-start(bf16[768,1536]{0,1:T(8,128)(2,1)} %pad_maximum_fusion.1), channel_id=1, source_target_pairs={{4,0},{8,4},{12,8},{16,12},{20,16},{24,20},{28,24},{5,1},{9,5},{13... | collective-permute-start | bytes 7077896 | tf_op jit(solution)/shard_map/ppermute | solution.py:16
  555.1 17.1 %collective-permute-start.7 = (bf16[768,1536]{0,1:T(8,128)(2,1)}, bf16[768,1536]{0,1:T(8,128)(2,1)}, u32[]{:S(2)}, u32[]{:S(2)}) collective-permute-start(bf16[768,1536]{0,1:T(8,128)(2,1)} %pad_maximum_fusion.1), channel_id=1, source_target_pairs={{0,4},{4,8},{8,12},{12,16},{16,20},{20,24},{24,28},{1,5},{5,9},{9,... | collective-permute-start | bytes 7077896 | tf_op jit(solution)/shard_map/ppermute | solution.py:16
  560.1 2.4 copy-start.3
  565.2 3.2 copy-start.4
  565.2 61.2 %collective-permute-start.10 = (bf16[768,1536]{0,1:T(8,128)(2,1)}, bf16[768,1536]{0,1:T(8,128)(2,1)}, u32[]{:S(2)}, u32[]{:S(2)}) collective-permute-start(bf16[768,1536]{0,1:T(8,128)(2,1)} %collective-permute-done.8), channel_id=1, source_target_pairs={{4,0},{8,4},{12,8},{16,12},{20,16},{24,20},{28,24},{5,1},{9,5},{13... | collective-permute-start | bytes 7077896 | tf_op jit(solution)/shard_map/ppermute | solution.py:16
  572.2 59.7 %collective-permute-start.9 = (bf16[768,1536]{0,1:T(8,128)(2,1)}, bf16[768,1536]{0,1:T(8,128)(2,1)}, u32[]{:S(2)}, u32[]{:S(2)}) collective-permute-start(bf16[768,1536]{0,1:T(8,128)(2,1)} %collective-permute-done.7), channel_id=1, source_target_pairs={{0,4},{4,8},{8,12},{12,16},{16,20},{20,24},{24,28},{1,5},{5,9},{9,... | collective-permute-start | bytes 7077896 | tf_op jit(solution)/shard_map/ppermute | solution.py:16
  631.9 41.0 %collective-permute-start.11 = (bf16[768,1536]{0,1:T(8,128)(2,1)}, bf16[768,1536]{0,1:T(8,128)(2,1)}, u32[]{:S(2)}, u32[]{:S(2)}) collective-permute-start(bf16[768,1536]{0,1:T(8,128)(2,1)} %collective-permute-done.9), channel_id=1, source_target_pairs={{0,4},{4,8},{8,12},{12,16},{16,20},{20,24},{24,28},{1,5},{5,9},{9,... | collective-permute-start | bytes 7077896 | tf_op jit(solution)/shard_map/ppermute | solution.py:16
  661.4 17.0 %collective-permute-start.12 = (bf16[768,1536]{0,1:T(8,128)(2,1)}, bf16[768,1536]{0,1:T(8,128)(2,1)}, u32[]{:S(2)}, u32[]{:S(2)}) collective-permute-start(bf16[768,1536]{0,1:T(8,128)(2,1)} %collective-permute-done.10), channel_id=1, source_target_pairs={{4,0},{8,4},{12,8},{16,12},{20,16},{24,20},{28,24},{5,1},{9,5},{13... | collective-permute-start | bytes 7077896 | tf_op jit(solution)/shard_map/ppermute | solution.py:16
  665.2 4.4 copy-start.8
  687.8 3.5 copy-start.7
Sparse Core Ops, SparseCore 0:
  25.6 87.6 all-gather.2
  287.5 123.1 reduce-scatter.2
  434.7 100.8 all-gather.4
  710.4 125.1 reduce-scatter.4
where the time goes:
time: 856 us; the launch traced here: 846 us
  waiting for transfers between devices  420 us (49%)
  matrix products  162 us (19%)
  starting transfers between devices  152 us (18%)
  local copies, waits for them, and re-layouts  47.9 us (6%)
  blocking collectives  25.7 us (3%)
  other arithmetic  22.7 us (3%)
  between operations  15.7 us (2%)
    reduce_scatter x2, waiting for transfers between devices, on_device(): lax.psum_scatter(lax.dot_general(output_weight, attended, (((0,), (1,)),...  247 us
    all_gather x2, waiting for transfers between devices, on_device(): lax.all_gather(normed, 'tensor', axis=1, tiled=True)  170 us
    ppermute x13, starting transfers between devices, passed_along(): return lax.ppermute(block, axis, route)  152 us
    dot_general x14, matrix products, absorb(): jnp.einsum('hqk,khd->hqd', probs.astype(jnp.bfloat16), value_part, prefer...  59.7 us
    dot_general x14, matrix products, absorb(): jnp.einsum('qhd,khd->hqk', queries, key_part, preferred_element_type=jnp....  54.5 us
    dot_general x2, matrix products, on_device(): jnp.dot(lax.all_gather(normed, 'tensor', axis=1, tiled=True), wide_weight...  30.8 us
    psum x2, blocking collectives, on_device(): lax.psum((jnp.sum(latent, axis=1), jnp.sum(latent * latent, axis=1)), 'te...  25.7 us
    unnamed x31, local copies, waits for them, and re-layouts  21.2 us
  transfers between devices with their start and end apart: 17, of which 5 were waited for; matrix products, arithmetic and copies ran while one was open for 15% of the time, Pallas kernels for 0%

commit v1 on v0

v1 whole, which is shorter than its diff:
```python
import functools
import math

import jax
import jax.numpy as jnp
from jax import lax
from jax.experimental import pallas as pl
from jax.experimental.pallas import tpu as pltpu
from jax.sharding import PartitionSpec as P

STEPS = 2
QUAD = 4
CHUNKS = 3
TILE = 256
VMEM = 56 * 1024 * 1024

epsilon = 1e-06


def permute(block, axis, route):
    size = lax.axis_size(axis)
    pairs = [(i, j) for i, j in ((i, route(i)) for i in range(size)) if 0 <= j < size]
    return lax.ppermute(block, axis, pairs)


def ring(block):
    size = lax.axis_size("tensor")
    return permute(block, "tensor", lambda i: (i + 1) % size)


def qkv_kernel(parts, heads, head_dim, order_ref, gain_ref, *refs):
    inputs, weights = refs[:parts], refs[parts : 2 * parts]
    query_ref, pair_ref = refs[2 * parts :]
    step = pl.program_id(0)
    total = jnp.dot(inputs[0][...], weights[0][...], preferred_element_type=jnp.float32)
    for part in range(1, parts):
        total += jnp.dot(inputs[part][...], weights[part][...], preferred_element_type=jnp.float32)

    def normed(row, factor):
        pieces = []
        for head in range(heads):
            piece = total[:, head * head_dim : (head + 1) * head_dim]
            scale = lax.rsqrt(jnp.mean(piece * piece, axis=-1, keepdims=True) + epsilon)
            pieces.append((piece * scale * (gain_ref[row : row + 1, :] * factor)).astype(jnp.bfloat16))
        return jnp.concatenate(pieces, axis=1) if heads > 1 else pieces[0]

    @pl.when(step == 0)
    def _():
        pair_ref[...] = normed(1, 1.0)

    @pl.when(step == 1)
    def _():
        pair_ref[...] = total.astype(jnp.bfloat16)

    @pl.when(step == 2)
    def _():
        query_ref[...] = normed(0, math.log2(math.e) / math.sqrt(head_dim))


def project(inputs, weight, order, norm_gain):
    parts = len(inputs)
    rows, columns = inputs[0].shape
    head_dim = norm_gain.shape[1]

    def weight_spec(part):
        return pl.BlockSpec((None, columns, columns), lambda j, order: ((j + 1) % 3, order[part], 0))

    return pl.pallas_call(
        functools.partial(qkv_kernel, parts, columns // head_dim, head_dim),
        grid_spec=pltpu.PrefetchScalarGridSpec(
            num_scalar_prefetch=1,
            grid=(3,),
            in_specs=[pl.BlockSpec(norm_gain.shape, lambda j, order: (0, 0))]
            + [pl.BlockSpec((rows, columns), lambda j, order: (0, 0)) for _ in range(parts)]
            + [weight_spec(part) for part in range(parts)],
            out_specs=[
                pl.BlockSpec((rows, columns), lambda j, order: (0, 0)),
                pl.BlockSpec((rows, columns), lambda j, order: (0, jnp.minimum(j, 1))),
            ],
        ),
        out_shape=[
            jax.ShapeDtypeStruct((rows, columns), jnp.bfloat16),
            jax.ShapeDtypeStruct((rows, 2 * columns), jnp.bfloat16),
        ],
        compiler_params=pltpu.CompilerParams(vmem_limit_bytes=VMEM),
        cost_estimate=pl.CostEstimate(
            flops=2 * rows * columns * parts * 3 * columns,
            bytes_accessed=2 * (columns * parts * 3 * columns + rows * columns * (parts + 3)),
            transcendentals=0,
        ),
        name="qkv",
    )(order, norm_gain, *inputs, *([weight] * parts))


def attend_kernel(chunks, pieces, first, last, tile, usable_ref, *refs):
    queries, refs = refs[:chunks], refs[chunks:]
    keys, values = refs[:pieces], refs[pieces : 2 * pieces]
    rest = refs[2 * pieces :]
    total_in = None
    if not first:
        total_in, rest = rest[0], rest[1:]
    (out_ref,) = rest
    height, head_dim = queries[0].shape
    wide = []
    for piece in range(pieces):
        value = values[piece][...]
        usable = usable_ref[piece].astype(jnp.float32).astype(value.dtype)
        wide.append(jnp.concatenate([value, jnp.ones_like(value)], axis=1) * usable)
    for chunk in range(chunks):
        for start in range(0, height, tile):
            query = queries[chunk][start : start + tile, :]
            at = pl.ds(chunk * height + start, tile)
            total = None if first else total_in[at, :]
            for piece in range(pieces):
                scores = lax.dot_general(
                    query, keys[piece][...], (((1,), (1,)), ((), ())), preferred_element_type=jnp.float32
                )
                probs = jnp.exp2(scores).astype(jnp.bfloat16)
                added = jnp.dot(probs, wide[piece], preferred_element_type=jnp.float32)
                total = added if total is None else total + added
            if last:
                out_ref[at, :] = (total[:, :head_dim] / total[:, head_dim:]).astype(out_ref.dtype)
            else:
                out_ref[at, :] = total


def attend(queries, blocks, usable, running, last, head_dim):
    height, columns = queries[0].shape
    chunks = len(queries)
    rows = height * chunks
    heads = columns // head_dim
    pieces = len(blocks)
    first = running is None
    tile = TILE if height % TILE == 0 else height

    def key_spec(block):
        return pl.BlockSpec((block.shape[0], head_dim), lambda h, usable: (0, h))

    def value_spec(block):
        return pl.BlockSpec((block.shape[0], head_dim), lambda h, usable: (0, heads + h))

    running_spec = pl.BlockSpec((None, rows, 2 * head_dim), lambda h, usable: (h, 0, 0))
    key_rows = sum(block.shape[0] for block in blocks)
    return pl.pallas_call(
        functools.partial(attend_kernel, chunks, pieces, first, last, tile),
        grid_spec=pltpu.PrefetchScalarGridSpec(
            num_scalar_prefetch=1,
            grid=(heads,),
            in_specs=[pl.BlockSpec((height, head_dim), lambda h, usable: (0, h)) for _ in queries]
            + [key_spec(block) for block in blocks]
            + [value_spec(block) for block in blocks]
            + ([] if first else [running_spec]),
            out_specs=pl.BlockSpec((rows, head_dim), lambda h, usable: (0, h)) if last else running_spec,
        ),
        out_shape=jax.ShapeDtypeStruct((rows, columns), jnp.bfloat16)
        if last
        else jax.ShapeDtypeStruct((heads, rows, 2 * head_dim), jnp.float32),
        compiler_params=pltpu.CompilerParams(vmem_limit_bytes=VMEM),
        cost_estimate=pl.CostEstimate(
            flops=8 * rows * key_rows * columns,
            bytes_accessed=4 * key_rows * columns + 12 * rows * columns,
            transcendentals=rows * key_rows * heads,
        ),
        name="attend",
    )(usable, *queries, *blocks, *blocks, *([] if first else [running]))


def first_share_kernel(order_ref, attended_ref, weight_ref, *out_refs):
    share = jnp.dot(
        attended_ref[...], weight_ref[...], preferred_element_type=jnp.float32
    ).astype(jnp.bfloat16)
    height = out_refs[0].shape[0]
    for index, out_ref in enumerate(out_refs):
        out_ref[...] = share[index * height : (index + 1) * height]


def share_kernel(order_ref, attended_ref, weight_ref, out_ref):
    out_ref[...] = jnp.dot(
        attended_ref[...], weight_ref[...], preferred_element_type=jnp.float32
    ).astype(out_ref.dtype)


def shares(attended, weight, order, chunks):
    rows, depth = attended.shape
    count = order.shape[0]
    columns = weight.shape[1] // lax.axis_size("tensor")
    if chunks:
        kernel = first_share_kernel
        out_specs = [pl.BlockSpec((rows // chunks, columns), lambda j, order: (0, 0))] * chunks
        out_shape = [jax.ShapeDtypeStruct((rows // chunks, columns), jnp.bfloat16)] * chunks
    else:
        kernel = share_kernel
        out_specs = pl.BlockSpec((None, rows, columns), lambda j, order: (j, 0, 0))
        out_shape = jax.ShapeDtypeStruct((count, rows, columns), jnp.bfloat16)
    return pl.pallas_call(
        kernel,
        grid_spec=pltpu.PrefetchScalarGridSpec(
            num_scalar_prefetch=1,
            grid=(count,),
            in_specs=[
                pl.BlockSpec((rows, depth), lambda j, order: (0, 0)),
                pl.BlockSpec((depth, columns), lambda j, order: (0, order[j])),
            ],
            out_specs=out_specs,
        ),
        out_shape=out_shape,
        compiler_params=pltpu.CompilerParams(vmem_limit_bytes=VMEM),
        cost_estimate=pl.CostEstimate(
            flops=2 * rows * depth * columns * count,
            bytes_accessed=2 * (rows * depth + count * columns * (rows + depth)),
            transcendentals=0,
        ),
        name="shares",
    )(order, attended, weight)


def summed(block):
    size = lax.axis_size("tensor")
    total = block
    for distance in range(1, size):
        total = total + permute(block, "tensor", lambda i: (i + distance) % size)
    return total


def sums_of(block):
    return jnp.stack([jnp.sum(block, axis=1), jnp.sum(block * block, axis=1)])


def chunk_sums(sums, index, height):
    return sums[:, index * height : (index + 1) * height]


def normalize(block, sums, full_width, shift, scale):
    mean = sums[0] / full_width
    var = sums[1] / full_width - mean * mean
    return (
        (block - mean[:, None]) * lax.rsqrt(var + epsilon)[:, None] * (1.0 + scale) + shift
    ).astype(jnp.bfloat16)


def sibling(block):
    return permute(block, "frame", lambda i: i ^ 1)


def halo(pair):
    across = permute(pair, "frame", lambda i: i ^ 2)
    near = sibling(pair)
    third = permute(pair, "frame", lambda i: i + (3 if i % 2 else -3))
    second = permute(across, "frame", lambda i: i + (QUAD if i % QUAD < 2 else -QUAD))
    return dict(
        own=pair, near=near, across=across, beyond=sibling(across), third=third, second=second, other=sibling(second)
    )


SOURCES = ("own", "near", "across", "beyond", "third", "second", "other")


def usable_sources(slot, frames, reach):
    place = slot % QUAD
    held = dict(
        own=slot,
        near=slot ^ 1,
        across=slot ^ 2,
        beyond=slot ^ 3,
        third=jnp.where(place % 2 == 0, slot - 3, slot + 3),
        second=jnp.where(place < 2, slot - 2, slot + 2),
        other=slot + jnp.where(place == 0, -1, jnp.where(place == 1, -3, jnp.where(place == 2, 3, 1))),
    )
    return {
        name: ((jnp.abs(g - slot) <= reach) & (g >= 0) & (g < frames)).astype(jnp.int32) for name, g in held.items()
    }


def on_device(
    queue_state,
    fresh_noise,
    levels,
    reach_slot,
    mod_table,
    step_table,
    norm_gain,
    input_weight,
    output_weight,
):
    rows, columns = queue_state.shape
    tensor_count = lax.axis_size("tensor")
    full_width = columns * tensor_count
    frames = lax.axis_size("frame")
    slot = lax.axis_index("frame")
    place = lax.axis_index("tensor")
    head_dim = norm_gain.shape[1]
    height = rows // CHUNKS

    def pieces_of(vector_level):
        row = lax.dynamic_index_in_dim(mod_table, vector_level, 0, keepdims=False)
        return [
            lax.dynamic_slice_in_dim(row, part * full_width + place * columns, columns) for part in range(3)
        ]

    level = levels[0]
    shift, scale, gate = pieces_of(level)
    step_size = lax.dynamic_index_in_dim(step_table, level, 0, keepdims=False)
    next_level = permute(levels, "frame", lambda i: i - 1)[0]
    next_shift, next_scale, _ = pieces_of(next_level)
    usable = usable_sources(slot, frames, reach_slot[0])
    gather_order = (place - jnp.arange(tensor_count, dtype=jnp.int32)) % tensor_count
    scatter_order = (place - 1 - jnp.arange(tensor_count, dtype=jnp.int32)) % tensor_count
    weights = jnp.transpose(input_weight, (1, 0, 2))

    def chunk(array, index):
        return array[index * height : (index + 1) * height]

    first_sums = summed(jnp.concatenate([sums_of(queue_state), sums_of(fresh_noise)]))
    normed = [
        normalize(chunk(queue_state, i), chunk_sums(first_sums[:2], i, height), full_width, shift, scale)
        for i in range(CHUNKS)
    ]
    latents = [chunk(queue_state, i) for i in range(CHUNKS)]
    fresh_normed = normalize(fresh_noise, first_sums[2:], full_width, shift, scale)
    advanced = None

    for step_number in range(STEPS):
        queries, sources = [], []
        waiting = None
        for i in range(CHUNKS):
            own = normed[i]
            if waiting is not None:
                gathered_before, own = lax.optimization_barrier((waiting[-1], own))
                waiting[-1] = gathered_before
                waiting.append(ring(waiting[-1]))
                query, pair = project(waiting, weights, gather_order, norm_gain)
                queries.append(query)
                sources.append(halo(pair))
            waiting = [own]
            for _ in range(tensor_count - 2):
                waiting.append(ring(waiting[-1]))
        waiting.append(ring(waiting[-1]))
        query, pair = project(waiting, weights, gather_order, norm_gain)
        queries.append(query)
        sources.append(halo(pair))

        def flags(names):
            return jnp.stack([usable[name] for _, name in names])

        final = CHUNKS - 1
        late_names = ("second", "other")
        early = [(i, name) for i in range(final - 1) for name in SOURCES]
        early += [(final - 1, name) for name in SOURCES if name not in late_names]
        middle = [(final - 1, name) for name in late_names]
        middle += [(final, name) for name in SOURCES if name not in late_names]
        late = [(final, name) for name in late_names]
        running = None
        for names in (early, middle, late):
            running = attend(
                queries,
                [sources[i][name] for i, name in names],
                flags(names),
                running,
                names is late,
                head_dim,
            )

        if step_number > 0:
            advanced, running = lax.optimization_barrier((advanced, running))
            moved = [permute(done, "frame", lambda i: i + 1) for done in advanced]
            latents = [jnp.where(slot == 0, chunk(fresh_noise, j), moved[j]) for j in range(CHUNKS)]

        totals = list(shares(running, output_weight, scatter_order[:1], CHUNKS))
        others = shares(running, output_weight, scatter_order[1:], 0)
        for hop in range(tensor_count - 1):
            for j in range(CHUNKS):
                total = ring(totals[j]).astype(jnp.float32) + chunk(others[hop], j).astype(jnp.float32)
                totals[j] = total.astype(jnp.bfloat16) if hop < tensor_count - 2 else total
        advanced = [
            latents[j] + step_size * (latents[j] + gate * totals[j]) for j in range(CHUNKS)
        ]
        if step_number < STEPS - 1:
            normed = []
            for j in range(CHUNKS):
                sums = summed(sums_of(advanced[j]))
                ready = permute(
                    normalize(advanced[j], sums, full_width, next_shift, next_scale), "frame", lambda i: i + 1
                )
                normed.append(jnp.where(slot == 0, chunk(fresh_normed, j), ready))
    return jnp.concatenate(advanced, axis=0)


def solution(mesh):
    return jax.shard_map(
        on_device,
        mesh=mesh,
        in_specs=(
            P("frame", "tensor"),
            P(None, "tensor"),
            P("frame"),
            P("frame"),
            P(),
            P(),
            P(),
            P(None, None, "tensor"),
            P("tensor", None),
        ),
        out_specs=P("frame", "tensor"),
        check_vma=False,
    )
```

time: 856 us -> 662 us (0.77)
  Pallas kernels: 0 us -> 172 us
  matrix products: 162 us -> 0 us
  waiting for transfers between devices: 420 us -> 325 us
  local copies, waits for them, and re-layouts: 47.9 us -> 12.2 us
  starting transfers between devices: 152 us -> 120 us
  blocking collectives: 25.7 us -> 0 us
  between operations: 15.7 us -> 4.93 us
    ppermute x13 -> x91, waiting for transfers between devices: 2.62 us -> 325 us  [permute(): return lax.ppermute(block, axis, pairs)]
    reduce_scatter x2 -> x0, waiting for transfers between devices: 247 us -> none  [on_device(): lax.psum_scatter(lax.dot_general(output_weight, attended, (((0,), (1,)),...]
    pallas_call x0 -> x16, Pallas kernels: none -> 172 us  [the longest x6 85.7 us: attend(): pl.pallas_call(functools.partial(attend_kernel, chunks, pieces, first, la...]
    all_gather x2 -> x0, waiting for transfers between devices: 170 us -> none  [on_device(): lax.all_gather(normed, 'tensor', axis=1, tiled=True)]
    dot_general x32 -> x0, matrix products: 162 us -> none  [the longest x14 59.7 us: absorb(): jnp.einsum('hqk,khd->hqd', probs.astype(jnp.bfloat16), value_part, prefer...]
    ppermute x13 -> x91, starting transfers between devices: 152 us -> 120 us  [permute(): return lax.ppermute(block, axis, pairs)]
    psum x2 -> x0, blocking collectives: 25.7 us -> none  [on_device(): lax.psum((jnp.sum(latent, axis=1), jnp.sum(latent * latent, axis=1)), 'te...]
    slice x16 -> x1, local copies, waits for them, and re-layouts: 26.1 us -> 0.66 us  [on_device(): others = shares(running, output_weight, scatter_order[1:], 0)]
  transfers between devices with their start and end apart: 17 -> 91, of which waited for: 5 -> 43; matrix products, arithmetic and copies ran while one was open for 15% -> 1% of each run, Pallas kernels for 0% -> 22%
where the time goes in v1:
time: 662 us; the launch traced here: 653 us
  waiting for transfers between devices  325 us (49%)
  Pallas kernels  172 us (26%)
  starting transfers between devices  120 us (18%)
  other arithmetic  19.3 us (3%)
  local copies, waits for them, and re-layouts  12.2 us (2%)
    ppermute x91, waiting for transfers between devices, permute(): return lax.ppermute(block, axis, pairs)  325 us
    ppermute x91, starting transfers between devices, permute(): return lax.ppermute(block, axis, pairs)  120 us
    pallas_call x6, Pallas kernels, attend(): pl.pallas_call(functools.partial(attend_kernel, chunks, pieces, first, la...  85.7 us
    pallas_call x6, Pallas kernels, project(): pl.pallas_call(functools.partial(qkv_kernel, parts, columns // head_dim,...  63.6 us
    pallas_call x4, Pallas kernels, shares(): pl.pallas_call(kernel, grid_spec=pltpu.PrefetchScalarGridSpec(num_scalar_...  23.1 us
  transfers between devices with their start and end apart: 91, of which 43 were waited for; matrix products, arithmetic and copies ran while one was open for 1% of the time, Pallas kernels for 22%

profile of v1, /device:TPU:0, one launch (start us, length us, event | category | flops | bytes accessed | tf_op | source)
XLA Modules:
  0.0 653.1 jit_solution(16058215630156861238)
XLA Ops:
  0.0 3.1 fusion.40
  3.2 3.1 collective-permute-start
  18.3 12.3 %collective-permute-done.3.refs_1_ = bf16[256,768]{1,0:T(8,128)(2,1)S(1)} collective-permute-done((bf16[256,768]{1,0:T(8,128)(2,1)S(1)}, bf16[256,768]{1,0:T(8,128)(2,1)S(1)}, u32[]{:S(2)}, u32[]{:S(2)}) %collective-permute-start.3) | collective-permute-done | bytes 393248 | tf_op jit(solution)/shard_map/ppermute | solution.py:23
  30.5 13.5 %collective-permute-done.4.refs_2_ = bf16[256,768]{1,0:T(8,128)(2,1)S(1)} collective-permute-done((bf16[256,768]{1,0:T(8,128)(2,1)S(1)}, bf16[256,768]{1,0:T(8,128)(2,1)S(1)}, u32[]{:S(2)}, u32[]{:S(2)}) %collective-permute-start.4) | collective-permute-done | bytes 393248 | tf_op jit(solution)/shard_map/ppermute | solution.py:23
  44.0 12.6 %collective-permute-done.6.refs_1_ = bf16[256,768]{1,0:T(8,128)(2,1)S(1)} collective-permute-done((bf16[256,768]{1,0:T(8,128)(2,1)S(1)}, bf16[256,768]{1,0:T(8,128)(2,1)S(1)}, u32[]{:S(2)}, u32[]{:S(2)}) %collective-permute-start.6) | collective-permute-done | bytes 393248 | tf_op jit(solution)/shard_map/ppermute | solution.py:23
  56.6 13.8 %collective-permute-done.7.refs_2_ = bf16[256,768]{1,0:T(8,128)(2,1)S(1)} collective-permute-done((bf16[256,768]{1,0:T(8,128)(2,1)S(1)}, bf16[256,768]{1,0:T(8,128)(2,1)S(1)}, u32[]{:S(2)}, u32[]{:S(2)}) %collective-permute-start.7) | collective-permute-done | bytes 393248 | tf_op jit(solution)/shard_map/ppermute | solution.py:23
  71.1 7.8 %collective-permute-done.5.refs_3_ = bf16[256,768]{1,0:T(8,128)(2,1)S(1)} collective-permute-done((bf16[256,768]{1,0:T(8,128)(2,1)S(1)}, bf16[256,768]{1,0:T(8,128)(2,1)S(1)}, u32[]{:S(2)}, u32[]{:S(2)}) %collective-permute-start.5) | collective-permute-done | bytes 393248 | tf_op jit(solution)/shard_map/ppermute | solution.py:23
  79.7 10.6 %qkv.6 = (bf16[256,768]{1,0:T(8,128)(2,1)}, bf16[256,1536]{1,0:T(8,128)(2,1)}) custom-call(s32[4]{0:T(128)} %and_select_fusion.order_ref, f32[2,128]{1,0:T(2,128)} %gain_ref.11, bf16[256,768]{1,0:T(8,128)(2,1)} %copy-done.13, bf16[256,768]{1,0:T(8,128)(2,1)} %copy-done.25, bf16[256,768]{1,0:T(8,128)(2,1)} %copy-done.27, bf16[256,768]{1,0:T(8,128)(2,1)} %copy-done.31, ...), custom_call_target="tpu_custom_call" | custom-call | flops 3623878656 | bytes 16908288 | tf_op jit(solution)/shard_map/qkv/pallas_call | solution.py:68
  92.0 13.6 %collective-permute-done.10.refs_2_ = bf16[256,768]{1,0:T(8,128)(2,1)S(1)} collective-permute-done((bf16[256,768]{1,0:T(8,128)(2,1)S(1)}, bf16[256,768]{1,0:T(8,128)(2,1)S(1)}, u32[]{:S(2)}, u32[]{:S(2)}) %collective-permute-start.10) | collective-permute-done | bytes 393248 | tf_op jit(solution)/shard_map/ppermute | solution.py:23
  106.4 7.7 %collective-permute-done.8.refs_3_ = bf16[256,768]{1,0:T(8,128)(2,1)S(1)} collective-permute-done((bf16[256,768]{1,0:T(8,128)(2,1)S(1)}, bf16[256,768]{1,0:T(8,128)(2,1)S(1)}, u32[]{:S(2)}, u32[]{:S(2)}) %collective-permute-start.8) | collective-permute-done | bytes 393248 | tf_op jit(solution)/shard_map/ppermute | solution.py:23
  114.9 10.6 %qkv.7 = (bf16[256,768]{1,0:T(8,128)(2,1)}, bf16[256,1536]{1,0:T(8,128)(2,1)}) custom-call(s32[4]{0:T(128)} %and_select_fusion.order_ref, f32[2,128]{1,0:T(2,128)} %gain_ref.11, bf16[256,768]{1,0:T(8,128)(2,1)} %copy-done.11, bf16[256,768]{1,0:T(8,128)(2,1)} %copy-done.17, bf16[256,768]{1,0:T(8,128)(2,1)} %copy-done.19, bf16[256,768]{1,0:T(8,128)(2,1)} %copy-done.29, ...), custom_call_target="tpu_custom_call" | custom-call | flops 3623878656 | bytes 16908288 | tf_op jit(solution)/shard_map/qkv/pallas_call | solution.py:68
  126.1 4.4 collective-permute-start.25
  131.2 10.6 %qkv.8 = (bf16[256,768]{1,0:T(8,128)(2,1)}, bf16[256,1536]{1,0:T(8,128)(2,1)}) custom-call(s32[4]{0:T(128)} %and_select_fusion.order_ref, f32[2,128]{1,0:T(2,128)} %gain_ref.11, bf16[256,768]{1,0:T(8,128)(2,1)} %copy-done.9, bf16[256,768]{1,0:T(8,128)(2,1)} %copy-done.15, bf16[256,768]{1,0:T(8,128)(2,1)} %copy-done.22, bf16[256,768]{1,0:T(8,128)(2,1)} %copy-done.24, ...), custom_call_target="tpu_custom_call" | custom-call | flops 3623878656 | bytes 16908288 | tf_op jit(solution)/shard_map/qkv/pallas_call | solution.py:68
  148.4 13.3 %collective-permute-start.16 = (bf16[256,1536]{1,0:T(8,128)(2,1)}, bf16[256,1536]{1,0:T(8,128)(2,1)}, u32[]{:S(2)}, u32[]{:S(2)}) collective-permute-start(bf16[256,1536]{1,0:T(8,128)(2,1)} %collective-permute-done.15.refs_12_.refs_24_), channel_id=1, source_target_pairs={{0,16},{4,20},{24,8},{28,12},{1,17},{5,21},{25,9},{29,13},{2,18},{... | collective-permute-start | bytes 2359304 | tf_op jit(solution)/shard_map/ppermute | solution.py:23
  167.3 3.8 collective-permute-start.13
  171.1 8.0 %collective-permute-done.16.refs_3_.refs_10_ = bf16[256,1536]{1,0:T(8,128)(2,1)} collective-permute-done((bf16[256,1536]{1,0:T(8,128)(2,1)}, bf16[256,1536]{1,0:T(8,128)(2,1)}, u32[]{:S(2)}, u32[]{:S(2)}) %collective-permute-start.16) | collective-permute-done | bytes 786464 | tf_op jit(solution)/shard_map/ppermute | solution.py:23
  179.0 20.4 %attend.6.refs_17_ = f32[6,768,256]{2,1,0:T(8,128)} custom-call(s32[12]{0:T(128)} %stack.148.usable_ref, bf16[256,768]{1,0:T(8,128)(2,1)} %get-tuple-element.36.refs_0_, bf16[256,768]{1,0:T(8,128)(2,1)} %get-tuple-element.39.refs_1_, bf16[256,768]{1,0:T(8,128)(2,1)} %get-tuple-element.41.refs_2_, bf16[256,1536]{1,0:T(8,128)(2,1)} %get-tuple-element.44.refs_3_.refs_15_, ...), custom_call_target="tpu_custom_call" | custom-call | flops 14495514624 | bytes 16515072 | tf_op jit(solution)/shard_map/attend/pallas_call | solution.py:144
  203.1 13.9 %attend.7.refs_7_ = f32[6,768,256]{2,1,0:T(8,128)} custom-call(s32[7]{0:T(128)} %stack.147.usable_ref, bf16[256,768]{1,0:T(8,128)(2,1)} %get-tuple-element.36.refs_0_, bf16[256,768]{1,0:T(8,128)(2,1)} %get-tuple-element.39.refs_1_, bf16[256,768]{1,0:T(8,128)(2,1)} %get-tuple-element.41.refs_2_, bf16[256,1536]{1,0:T(8,128)(2,1)} %collective-permute-done.16.refs_3_.refs_10_, ...), custom_call_target="tpu_custom_call" | custom-call | flops 8455716864 | bytes 12582912 | tf_op jit(solution)/shard_map/attend/pallas_call | solution.py:144
  217.9 8.5 %attend.8.attended_ref = bf16[768,768]{1,0:T(8,128)(2,1)} custom-call(s32[2]{0:T(128)} %pad_add_fusion.usable_ref, bf16[256,768]{1,0:T(8,128)(2,1)} %get-tuple-element.36.refs_0_, bf16[256,768]{1,0:T(8,128)(2,1)} %get-tuple-element.39.refs_1_, bf16[256,768]{1,0:T(8,128)(2,1)} %get-tuple-element.41.refs_2_, bf16[256,1536]{1,0:T(8,128)(2,1)} %copy-done.4, ...), custom_call_target="tpu_custom_call" | custom-call | flops 2415919104 | bytes 8650752 | tf_op jit(solution)/shard_map/attend/pallas_call | solution.py:144
  226.4 4.3 shares.4
  232.0 7.2 %shares.5 = bf16[3,768,768]{2,1,0:T(8,128)(2,1)} custom-call(s32[3]{0:T(128)} %slice.217.order_ref, bf16[768,768]{1,0:T(8,128)(2,1)} %attend.8.attended_ref, bf16[768,3072]{1,0:T(8,128)(2,1)} %weight_ref.7), custom_call_target="tpu_custom_call" | custom-call | flops 2717908992 | bytes 8257536 | tf_op jit(solution)/shard_map/shares/pallas_call | solution.py:195
  239.2 5.4 collective-permute-done.30
  244.7 8.4 %collective-permute-done.33 = bf16[256,768]{1,0:T(8,128)(2,1)S(1)} collective-permute-done((bf16[256,768]{1,0:T(8,128)(2,1)}, bf16[256,768]{1,0:T(8,128)(2,1)S(1)}, u32[]{:S(2)}, u32[]{:S(2)}) %collective-permute-start.33) | collective-permute-done | bytes 393248 | tf_op jit(solution)/shard_map/ppermute | solution.py:23
  253.1 7.5 %collective-permute-done.36 = bf16[256,768]{1,0:T(8,128)(2,1)S(1)} collective-permute-done((bf16[256,768]{1,0:T(8,128)(2,1)}, bf16[256,768]{1,0:T(8,128)(2,1)S(1)}, u32[]{:S(2)}, u32[]{:S(2)}) %collective-permute-start.36) | collective-permute-done | bytes 393248 | tf_op jit(solution)/shard_map/ppermute | solution.py:23
  262.9 13.1 %collective-permute-done.31 = bf16[256,768]{1,0:T(8,128)(2,1)S(1)} collective-permute-done((bf16[256,768]{1,0:T(8,128)(2,1)S(1)}, bf16[256,768]{1,0:T(8,128)(2,1)S(1)}, u32[]{:S(2)}, u32[]{:S(2)}) %collective-permute-start.31) | collective-permute-done | bytes 393248 | tf_op jit(solution)/shard_map/ppermute | solution.py:23
  276.0 8.4 %collective-permute-done.34 = bf16[256,768]{1,0:T(8,128)(2,1)S(1)} collective-permute-done((bf16[256,768]{1,0:T(8,128)(2,1)S(1)}, bf16[256,768]{1,0:T(8,128)(2,1)S(1)}, u32[]{:S(2)}, u32[]{:S(2)}) %collective-permute-start.34) | collective-permute-done | bytes 393248 | tf_op jit(solution)/shard_map/ppermute | solution.py:23
  284.4 6.6 %collective-permute-done.37 = bf16[256,768]{1,0:T(8,128)(2,1)S(1)} collective-permute-done((bf16[256,768]{1,0:T(8,128)(2,1)S(1)}, bf16[256,768]{1,0:T(8,128)(2,1)S(1)}, u32[]{:S(2)}, u32[]{:S(2)}) %collective-permute-start.37) | collective-permute-done | bytes 393248 | tf_op jit(solution)/shard_map/ppermute | solution.py:23
  295.3 12.1 %collective-permute-done.32 = bf16[256,768]{1,0:T(8,128)(2,1)S(1)} collective-permute-done((bf16[256,768]{1,0:T(8,128)(2,1)}, bf16[256,768]{1,0:T(8,128)(2,1)S(1)}, u32[]{:S(2)}, u32[]{:S(2)}) %collective-permute-start.32) | collective-permute-done | bytes 393248 | tf_op jit(solution)/shard_map/ppermute | solution.py:23
  307.5 8.4 %collective-permute-done.35 = bf16[256,768]{1,0:T(8,128)(2,1)S(1)} collective-permute-done((bf16[256,768]{1,0:T(8,128)(2,1)}, bf16[256,768]{1,0:T(8,128)(2,1)S(1)}, u32[]{:S(2)}, u32[]{:S(2)}) %collective-permute-start.35) | collective-permute-done | bytes 393248 | tf_op jit(solution)/shard_map/ppermute | solution.py:23
  315.9 5.7 collective-permute-done.38
  324.6 3.6 collective-permute-start.41
  330.3 2.9 collective-permute-start.48
  334.2 2.9 collective-permute-start.55
  341.1 7.0 %collective-permute-start.49 = (bf16[256,768]{1,0:T(8,128)(2,1)S(1)}, bf16[256,768]{1,0:T(8,128)(2,1)S(1)}, u32[]{:S(2)}, u32[]{:S(2)}) collective-permute-start(bf16[256,768]{1,0:T(8,128)(2,1)S(1)} %get-tuple-element.119), channel_id=1, source_target_pairs={{0,4},{4,8},{8,12},{12,16},{16,20},{20,24},{24,28},{1,5},{5,9},{9,... | collective-permute-start | bytes 1179656 | tf_op jit(solution)/shard_map/ppermute | solution.py:23
  353.6 7.6 %collective-permute-done.44.refs_1_ = bf16[256,768]{1,0:T(8,128)(2,1)S(1)} collective-permute-done((bf16[256,768]{1,0:T(8,128)(2,1)S(1)}, bf16[256,768]{1,0:T(8,128)(2,1)S(1)}, u32[]{:S(2)}, u32[]{:S(2)}) %collective-permute-start.44) | collective-permute-done | bytes 393248 | tf_op jit(solution)/shard_map/ppermute | solution.py:23
  361.4 11.0 %collective-permute-done.45.refs_2_ = bf16[256,768]{1,0:T(8,128)(2,1)S(1)} collective-permute-done((bf16[256,768]{1,0:T(8,128)(2,1)S(1)}, bf16[256,768]{1,0:T(8,128)(2,1)S(1)}, u32[]{:S(2)}, u32[]{:S(2)}) %collective-permute-start.45) | collective-permute-done | bytes 393248 | tf_op jit(solution)/shard_map/ppermute | solution.py:23
  372.6 10.1 %collective-permute-done.51.refs_1_ = bf16[256,768]{1,0:T(8,128)(2,1)S(1)} collective-permute-done((bf16[256,768]{1,0:T(8,128)(2,1)S(1)}, bf16[256,768]{1,0:T(8,128)(2,1)S(1)}, u32[]{:S(2)}, u32[]{:S(2)}) %collective-permute-start.51) | collective-permute-done | bytes 393248 | tf_op jit(solution)/shard_map/ppermute | solution.py:23
  383.5 8.8 %collective-permute-done.52.refs_2_ = bf16[256,768]{1,0:T(8,128)(2,1)S(1)} collective-permute-done((bf16[256,768]{1,0:T(8,128)(2,1)S(1)}, bf16[256,768]{1,0:T(8,128)(2,1)S(1)}, u32[]{:S(2)}, u32[]{:S(2)}) %collective-permute-start.52) | collective-permute-done | bytes 393248 | tf_op jit(solution)/shard_map/ppermute | solution.py:23
  392.4 8.4 %collective-permute-done.50.refs_3_ = bf16[256,768]{1,0:T(8,128)(2,1)S(1)} collective-permute-done((bf16[256,768]{1,0:T(8,128)(2,1)S(1)}, bf16[256,768]{1,0:T(8,128)(2,1)S(1)}, u32[]{:S(2)}, u32[]{:S(2)}) %collective-permute-start.50) | collective-permute-done | bytes 393248 | tf_op jit(solution)/shard_map/ppermute | solution.py:23
  401.5 10.6 %qkv.9 = (bf16[256,768]{1,0:T(8,128)(2,1)}, bf16[256,1536]{1,0:T(8,128)(2,1)}) custom-call(s32[4]{0:T(128)} %and_select_fusion.order_ref, f32[2,128]{1,0:T(2,128)} %gain_ref.11, bf16[256,768]{1,0:T(8,128)(2,1)} %copy-done.14, bf16[256,768]{1,0:T(8,128)(2,1)} %copy-done.26, bf16[256,768]{1,0:T(8,128)(2,1)} %copy-done.28, bf16[256,768]{1,0:T(8,128)(2,1)} %copy-done.32, ...), custom_call_target="tpu_custom_call" | custom-call | flops 3623878656 | bytes 16908288 | tf_op jit(solution)/shard_map/qkv/pallas_call | solution.py:68
  412.1 12.1 %collective-permute-start.71 = (bf16[256,1536]{1,0:T(8,128)(2,1)}, bf16[256,1536]{1,0:T(8,128)(2,1)S(1)}, u32[]{:S(2)}, u32[]{:S(2)}) collective-permute-start(bf16[256,1536]{1,0:T(8,128)(2,1)} %get-tuple-element.57.refs_3_.refs_15_), channel_id=1, source_target_pairs={{0,8},{4,12},{8,0},{12,4},{16,24},{20,28},{24,16},{28,20},{1,9},{5... | collective-permute-start | bytes 2359304 | tf_op jit(solution)/shard_map/ppermute | solution.py:23
  424.4 13.6 %collective-permute-done.59.refs_2_ = bf16[256,768]{1,0:T(8,128)(2,1)S(1)} collective-permute-done((bf16[256,768]{1,0:T(8,128)(2,1)S(1)}, bf16[256,768]{1,0:T(8,128)(2,1)S(1)}, u32[]{:S(2)}, u32[]{:S(2)}) %collective-permute-start.59) | collective-permute-done | bytes 393248 | tf_op jit(solution)/shard_map/ppermute | solution.py:23
  438.7 7.7 %collective-permute-done.57.refs_3_ = bf16[256,768]{1,0:T(8,128)(2,1)S(1)} collective-permute-done((bf16[256,768]{1,0:T(8,128)(2,1)S(1)}, bf16[256,768]{1,0:T(8,128)(2,1)S(1)}, u32[]{:S(2)}, u32[]{:S(2)}) %collective-permute-start.57) | collective-permute-done | bytes 393248 | tf_op jit(solution)/shard_map/ppermute | solution.py:23
  447.2 10.6 %qkv.10 = (bf16[256,768]{1,0:T(8,128)(2,1)}, bf16[256,1536]{1,0:T(8,128)(2,1)}) custom-call(s32[4]{0:T(128)} %and_select_fusion.order_ref, f32[2,128]{1,0:T(2,128)} %gain_ref.11, bf16[256,768]{1,0:T(8,128)(2,1)} %copy-done.12, bf16[256,768]{1,0:T(8,128)(2,1)} %copy-done.18, bf16[256,768]{1,0:T(8,128)(2,1)} %copy-done.20, bf16[256,768]{1,0:T(8,128)(2,1)} %copy-done.30, ...), custom_call_target="tpu_custom_call" | custom-call | flops 3623878656 | bytes 16908288 | tf_op jit(solution)/shard_map/qkv/pallas_call | solution.py:68
  458.0 5.5 collective-permute-start.74
  464.3 10.7 %qkv.11 = (bf16[256,768]{1,0:T(8,128)(2,1)}, bf16[256,1536]{1,0:T(8,128)(2,1)}) custom-call(s32[4]{0:T(128)} %and_select_fusion.order_ref, f32[2,128]{1,0:T(2,128)} %gain_ref.11, bf16[256,768]{1,0:T(8,128)(2,1)} %copy-done.10, bf16[256,768]{1,0:T(8,128)(2,1)} %copy-done.16, bf16[256,768]{1,0:T(8,128)(2,1)} %copy-done.21, bf16[256,768]{1,0:T(8,128)(2,1)} %copy-done.23, ...), custom_call_target="tpu_custom_call" | custom-call | flops 3623878656 | bytes 16908288 | tf_op jit(solution)/shard_map/qkv/pallas_call | solution.py:68
  480.5 13.3 %collective-permute-start.65 = (bf16[256,1536]{1,0:T(8,128)(2,1)}, bf16[256,1536]{1,0:T(8,128)(2,1)}, u32[]{:S(2)}, u32[]{:S(2)}) collective-permute-start(bf16[256,1536]{1,0:T(8,128)(2,1)} %collective-permute-done.64.refs_12_.refs_24_), channel_id=1, source_target_pairs={{0,16},{4,20},{24,8},{28,12},{1,17},{5,21},{25,9},{29,13},{2,18},{... | collective-permute-start | bytes 2359304 | tf_op jit(solution)/shard_map/ppermute | solution.py:23
  497.1 3.5 collective-permute-start.62
  500.6 10.6 %collective-permute-done.65.refs_3_.refs_10_ = bf16[256,1536]{1,0:T(8,128)(2,1)} collective-permute-done((bf16[256,1536]{1,0:T(8,128)(2,1)}, bf16[256,1536]{1,0:T(8,128)(2,1)}, u32[]{:S(2)}, u32[]{:S(2)}) %collective-permute-start.65) | collective-permute-done | bytes 786464 | tf_op jit(solution)/shard_map/ppermute | solution.py:23
  511.2 20.4 %attend.9.refs_17_ = f32[6,768,256]{2,1,0:T(8,128)} custom-call(s32[12]{0:T(128)} %stack.148.usable_ref, bf16[256,768]{1,0:T(8,128)(2,1)} %get-tuple-element.49.refs_0_, bf16[256,768]{1,0:T(8,128)(2,1)} %get-tuple-element.52.refs_1_, bf16[256,768]{1,0:T(8,128)(2,1)} %get-tuple-element.54.refs_2_, bf16[256,1536]{1,0:T(8,128)(2,1)} %get-tuple-element.57.refs_3_.refs_15_, ...), custom_call_target="tpu_custom_call" | custom-call | flops 14495514624 | bytes 16515072 | tf_op jit(solution)/shard_map/attend/pallas_call | solution.py:144
  533.8 13.9 %attend.10.refs_7_ = f32[6,768,256]{2,1,0:T(8,128)} custom-call(s32[7]{0:T(128)} %stack.147.usable_ref, bf16[256,768]{1,0:T(8,128)(2,1)} %get-tuple-element.49.refs_0_, bf16[256,768]{1,0:T(8,128)(2,1)} %get-tuple-element.52.refs_1_, bf16[256,768]{1,0:T(8,128)(2,1)} %get-tuple-element.54.refs_2_, bf16[256,1536]{1,0:T(8,128)(2,1)} %collective-permute-done.65.refs_3_.refs_10_, ...), custom_call_target="tpu_custom_call" | custom-call | flops 8455716864 | bytes 12582912 | tf_op jit(solution)/shard_map/attend/pallas_call | solution.py:144
  548.6 8.5 %attend.11.attended_ref = bf16[768,768]{1,0:T(8,128)(2,1)} custom-call(s32[2]{0:T(128)} %pad_add_fusion.usable_ref, bf16[256,768]{1,0:T(8,128)(2,1)} %get-tuple-element.49.refs_0_, bf16[256,768]{1,0:T(8,128)(2,1)} %get-tuple-element.52.refs_1_, bf16[256,768]{1,0:T(8,128)(2,1)} %get-tuple-element.54.refs_2_, bf16[256,1536]{1,0:T(8,128)(2,1)} %copy-done.3, ...), custom_call_target="tpu_custom_call" | custom-call | flops 2415919104 | bytes 8650752 | tf_op jit(solution)/shard_map/attend/pallas_call | solution.py:144
  557.1 4.2 shares.6
  562.0 7.3 %shares.7 = bf16[3,768,768]{2,1,0:T(8,128)(2,1)} custom-call(s32[3]{0:T(128)} %slice.217.order_ref, bf16[768,768]{1,0:T(8,128)(2,1)} %attend.11.attended_ref, bf16[768,3072]{1,0:T(8,128)(2,1)} %weight_ref.7), custom_call_target="tpu_custom_call" | custom-call | flops 2717908992 | bytes 8257536 | tf_op jit(solution)/shard_map/shares/pallas_call | solution.py:195
  569.3 6.0 collective-permute-done.80
  575.3 8.4 %collective-permute-done.84 = bf16[256,768]{1,0:T(8,128)(2,1)S(1)} collective-permute-done((bf16[256,768]{1,0:T(8,128)(2,1)}, bf16[256,768]{1,0:T(8,128)(2,1)S(1)}, u32[]{:S(2)}, u32[]{:S(2)}) %collective-permute-start.84) | collective-permute-done | bytes 393248 | tf_op jit(solution)/shard_map/ppermute | solution.py:23
  583.7 7.5 %collective-permute-done.88 = bf16[256,768]{1,0:T(8,128)(2,1)S(1)} collective-permute-done((bf16[256,768]{1,0:T(8,128)(2,1)}, bf16[256,768]{1,0:T(8,128)(2,1)S(1)}, u32[]{:S(2)}, u32[]{:S(2)}) %collective-permute-start.88) | collective-permute-done | bytes 393248 | tf_op jit(solution)/shard_map/ppermute | solution.py:23
  595.0 4.7 collective-permute-start.83
  599.7 7.0 %collective-permute-done.81 = bf16[256,768]{1,0:T(8,128)(2,1)S(1)} collective-permute-done((bf16[256,768]{1,0:T(8,128)(2,1)S(1)}, bf16[256,768]{1,0:T(8,128)(2,1)S(1)}, u32[]{:S(2)}, u32[]{:S(2)}) %collective-permute-start.81) | collective-permute-done | bytes 393248 | tf_op jit(solution)/shard_map/ppermute | solution.py:23
  608.0 7.1 %collective-permute-done.85 = bf16[256,768]{1,0:T(8,128)(2,1)S(1)} collective-permute-done((bf16[256,768]{1,0:T(8,128)(2,1)S(1)}, bf16[256,768]{1,0:T(8,128)(2,1)S(1)}, u32[]{:S(2)}, u32[]{:S(2)}) %collective-permute-start.85) | collective-permute-done | bytes 393248 | tf_op jit(solution)/shard_map/ppermute | solution.py:23
  615.1 6.6 %collective-permute-done.89 = bf16[256,768]{1,0:T(8,128)(2,1)S(1)} collective-permute-done((bf16[256,768]{1,0:T(8,128)(2,1)S(1)}, bf16[256,768]{1,0:T(8,128)(2,1)S(1)}, u32[]{:S(2)}, u32[]{:S(2)}) %collective-permute-start.89) | collective-permute-done | bytes 393248 | tf_op jit(solution)/shard_map/ppermute | solution.py:23
  622.7 13.2 %collective-permute-done.82 = bf16[256,768]{1,0:T(8,128)(2,1)S(1)} collective-permute-done((bf16[256,768]{1,0:T(8,128)(2,1)S(1)}, bf16[256,768]{1,0:T(8,128)(2,1)S(1)}, u32[]{:S(2)}, u32[]{:S(2)}) %collective-permute-start.82) | collective-permute-done | bytes 393248 | tf_op jit(solution)/shard_map/ppermute | solution.py:23
  635.9 8.4 %collective-permute-done.86 = bf16[256,768]{1,0:T(8,128)(2,1)S(1)} collective-permute-done((bf16[256,768]{1,0:T(8,128)(2,1)S(1)}, bf16[256,768]{1,0:T(8,128)(2,1)S(1)}, u32[]{:S(2)}, u32[]{:S(2)}) %collective-permute-start.86) | collective-permute-done | bytes 393248 | tf_op jit(solution)/shard_map/ppermute | solution.py:23
  644.3 5.7 collective-permute-done.90
  (296 shorter events, 80.1 us)
Async XLA Ops:
  56.6 22.3 %collective-permute-start.5 = (bf16[256,768]{1,0:T(8,128)(2,1)S(1)}, bf16[256,768]{1,0:T(8,128)(2,1)S(1)}, u32[]{:S(2)}, u32[]{:S(2)}) collective-permute-start(bf16[256,768]{1,0:T(8,128)(2,1)S(1)} %collective-permute-done.4.refs_2_), channel_id=1, source_target_pairs={{0,1},{1,2},{2,3},{3,0},{4,5},{5,6},{6,7},{7,4},{8,9},{9,10},{10,1... | collective-permute-start | bytes 1179656 | tf_op jit(solution)/shard_map/ppermute | solution.py:23
  70.5 21.4 %collective-permute-start.9 = (bf16[256,768]{1,0:T(8,128)(2,1)S(1)}, bf16[256,768]{1,0:T(8,128)(2,1)S(1)}, u32[]{:S(2)}, u32[]{:S(2)}) collective-permute-start(bf16[256,768]{1,0:T(8,128)(2,1)S(1)} %get-tuple-element.40.refs_0_), channel_id=1, source_target_pairs={{0,1},{1,2},{2,3},{3,0},{4,5},{5,6},{6,7},{7,4},{8,9},{9,10},{10,1... | collective-permute-start | bytes 1179656 | tf_op jit(solution)/shard_map/ppermute | solution.py:23
  90.3 35.8 %collective-permute-start.22 = (bf16[256,1536]{1,0:T(8,128)(2,1)}, bf16[256,1536]{1,0:T(8,128)(2,1)S(1)}, u32[]{:S(2)}, u32[]{:S(2)}) collective-permute-start(bf16[256,1536]{1,0:T(8,128)(2,1)} %get-tuple-element.44.refs_3_.refs_15_), channel_id=1, source_target_pairs={{0,8},{4,12},{8,0},{12,4},{16,24},{20,28},{24,16},{28,20},{1,9},{5... | collective-permute-start | bytes 2359304 | tf_op jit(solution)/shard_map/ppermute | solution.py:23
  91.9 34.2 %collective-permute-start.21 = (bf16[256,1536]{1,0:T(8,128)(2,1)}, bf16[256,1536]{1,0:T(8,128)(2,1)S(1)}, u32[]{:S(2)}, u32[]{:S(2)}) collective-permute-start(bf16[256,1536]{1,0:T(8,128)(2,1)} %get-tuple-element.44.refs_3_.refs_15_), channel_id=1, source_target_pairs={{0,4},{4,0},{8,12},{12,8},{16,20},{20,16},{24,28},{28,24},{1,5},{5... | collective-permute-start | bytes 2359304 | tf_op jit(solution)/shard_map/ppermute | solution.py:23
  92.0 22.1 %collective-permute-start.8 = (bf16[256,768]{1,0:T(8,128)(2,1)S(1)}, bf16[256,768]{1,0:T(8,128)(2,1)S(1)}, u32[]{:S(2)}, u32[]{:S(2)}) collective-permute-start(bf16[256,768]{1,0:T(8,128)(2,1)S(1)} %collective-permute-done.7.refs_2_), channel_id=1, source_target_pairs={{0,1},{1,2},{2,3},{3,0},{4,5},{5,6},{6,7},{7,4},{8,9},{9,10},{10,1... | collective-permute-start | bytes 1179656 | tf_op jit(solution)/shard_map/ppermute | solution.py:23
  105.7 24.8 %collective-permute-start.11 = (bf16[256,768]{1,0:T(8,128)(2,1)S(1)}, bf16[256,768]{1,0:T(8,128)(2,1)S(1)}, u32[]{:S(2)}, u32[]{:S(2)}) collective-permute-start(bf16[256,768]{1,0:T(8,128)(2,1)S(1)} %collective-permute-done.10.refs_2_), channel_id=1, source_target_pairs={{0,1},{1,2},{2,3},{3,0},{4,5},{5,6},{6,7},{7,4},{8,9},{9,10},{10,1... | collective-permute-start | bytes 1179656 | tf_op jit(solution)/shard_map/ppermute | solution.py:23
  105.7 36.2 %collective-permute-start.24 = (bf16[256,1536]{1,0:T(8,128)(2,1)}, bf16[256,1536]{1,0:T(8,128)(2,1)S(1)}, u32[]{:S(2)}, u32[]{:S(2)}) collective-permute-start(bf16[256,1536]{1,0:T(8,128)(2,1)} %get-tuple-element.44.refs_3_.refs_15_), channel_id=1, source_target_pairs={{4,16},{12,24},{16,4},{24,12},{5,17},{13,25},{17,5},{25,13},{6,18}... | collective-permute-start | bytes 2359304 | tf_op jit(solution)/shard_map/ppermute | solution.py:23
  125.5 19.0 %collective-permute-start.15 = (bf16[256,1536]{1,0:T(8,128)(2,1)}, bf16[256,1536]{1,0:T(8,128)(2,1)}, u32[]{:S(2)}, u32[]{:S(2)}) collective-permute-start(bf16[256,1536]{1,0:T(8,128)(2,1)} %get-tuple-element.43.refs_10_.refs_22_), channel_id=1, source_target_pairs={{0,8},{4,12},{8,0},{12,4},{16,24},{20,28},{24,16},{28,20},{1,9},{5... | collective-permute-start | bytes 2359304 | tf_op jit(solution)/shard_map/ppermute | solution.py:23
  126.0 18.5 %collective-permute-start.27 = (bf16[256,1536]{1,0:T(8,128)(2,1)}, bf16[256,1536]{1,0:T(8,128)(2,1)S(1)}, u32[]{:S(2)}, u32[]{:S(2)}) collective-permute-start(bf16[256,1536]{1,0:T(8,128)(2,1)} %get-tuple-element.43.refs_10_.refs_22_), channel_id=1, source_target_pairs={{0,4},{4,0},{8,12},{12,8},{16,20},{20,16},{24,28},{28,24},{1,5},{5... | collective-permute-start | bytes 2359304 | tf_op jit(solution)/shard_map/ppermute | solution.py:23
  126.1 21.4 %collective-permute-start.25 = (bf16[256,1536]{1,0:T(8,128)(2,1)S(1)}, bf16[256,1536]{1,0:T(8,128)(2,1)}, u32[]{:S(2)}, u32[]{:S(2)}) collective-permute-start(bf16[256,1536]{1,0:T(8,128)(2,1)S(1)} %collective-permute-done.22.refs_5_.refs_17_), channel_id=1, source_target_pairs={{0,16},{4,20},{24,8},{28,12},{1,17},{5,21},{25,9},{29,13},{2,18},{... | collective-permute-start | bytes 2359304 | tf_op jit(solution)/shard_map/ppermute | solution.py:23
  130.5 17.0 %collective-permute-start.29 = (bf16[256,1536]{1,0:T(8,128)(2,1)}, bf16[256,1536]{1,0:T(8,128)(2,1)S(1)}, u32[]{:S(2)}, u32[]{:S(2)}) collective-permute-start(bf16[256,1536]{1,0:T(8,128)(2,1)} %get-tuple-element.43.refs_10_.refs_22_), channel_id=1, source_target_pairs={{4,16},{12,24},{16,4},{24,12},{5,17},{13,25},{17,5},{25,13},{6,18}... | collective-permute-start | bytes 2359304 | tf_op jit(solution)/shard_map/ppermute | solution.py:23
  141.9 22.9 %collective-permute-start.23 = (bf16[256,1536]{1,0:T(8,128)(2,1)S(1)}, bf16[256,1536]{1,0:T(8,128)(2,1)}, u32[]{:S(2)}, u32[]{:S(2)}) collective-permute-start(bf16[256,1536]{1,0:T(8,128)(2,1)S(1)} %collective-permute-done.22.refs_5_.refs_17_), channel_id=1, source_target_pairs={{0,4},{4,0},{8,12},{12,8},{16,20},{20,16},{24,28},{28,24},{1,5},{5... | collective-permute-start | bytes 2359304 | tf_op jit(solution)/shard_map/ppermute | solution.py:23
  144.6 20.2 %collective-permute-start.28 = (bf16[256,1536]{1,0:T(8,128)(2,1)}, bf16[256,1536]{1,0:T(8,128)(2,1)}, u32[]{:S(2)}, u32[]{:S(2)}) collective-permute-start(bf16[256,1536]{1,0:T(8,128)(2,1)} %collective-permute-done.15.refs_12_.refs_24_), channel_id=1, source_target_pairs={{0,4},{4,0},{8,12},{12,8},{16,20},{20,16},{24,28},{28,24},{1,5},{5... | collective-permute-start | bytes 2359304 | tf_op jit(solution)/shard_map/ppermute | solution.py:23
  144.6 20.9 %collective-permute-start.12 = (bf16[256,1536]{1,0:T(8,128)(2,1)}, bf16[256,1536]{1,0:T(8,128)(2,1)}, u32[]{:S(2)}, u32[]{:S(2)}) collective-permute-start(bf16[256,1536]{1,0:T(8,128)(2,1)} %get-tuple-element.42.refs_5_.refs_12_), channel_id=1, source_target_pairs={{0,8},{4,12},{8,0},{12,4},{16,24},{20,28},{24,16},{28,20},{1,9},{5... | collective-permute-start | bytes 2359304 | tf_op jit(solution)/shard_map/ppermute | solution.py:23
  147.4 19.8 %collective-permute-start.26 = (bf16[256,1536]{1,0:T(8,128)(2,1)}, bf16[256,1536]{1,0:T(8,128)(2,1)}, u32[]{:S(2)}, u32[]{:S(2)}) collective-permute-start(bf16[256,1536]{1,0:T(8,128)(2,1)} %collective-permute-done.25.refs_8_.refs_20_), channel_id=1, source_target_pairs={{0,4},{4,0},{8,12},{12,8},{16,20},{20,16},{24,28},{28,24},{1,5},{5... | collective-permute-start | bytes 2359304 | tf_op jit(solution)/shard_map/ppermute | solution.py:23
  148.4 30.7 %collective-permute-start.16 = (bf16[256,1536]{1,0:T(8,128)(2,1)}, bf16[256,1536]{1,0:T(8,128)(2,1)}, u32[]{:S(2)}, u32[]{:S(2)}) collective-permute-start(bf16[256,1536]{1,0:T(8,128)(2,1)} %collective-permute-done.15.refs_12_.refs_24_), channel_id=1, source_target_pairs={{0,16},{4,20},{24,8},{28,12},{1,17},{5,21},{25,9},{29,13},{2,18},{... | collective-permute-start | bytes 2359304 | tf_op jit(solution)/shard_map/ppermute | solution.py:23
  164.8 36.0 %collective-permute-start.18 = (bf16[256,1536]{1,0:T(8,128)(2,1)}, bf16[256,1536]{1,0:T(8,128)(2,1)S(1)}, u32[]{:S(2)}, u32[]{:S(2)}) collective-permute-start(bf16[256,1536]{1,0:T(8,128)(2,1)} %get-tuple-element.42.refs_5_.refs_12_), channel_id=1, source_target_pairs={{0,4},{4,0},{8,12},{12,8},{16,20},{20,16},{24,28},{28,24},{1,5},{5... | collective-permute-start | bytes 2359304 | tf_op jit(solution)/shard_map/ppermute | solution.py:23
  164.8 36.0 %collective-permute-start.20 = (bf16[256,1536]{1,0:T(8,128)(2,1)}, bf16[256,1536]{1,0:T(8,128)(2,1)S(1)}, u32[]{:S(2)}, u32[]{:S(2)}) collective-permute-start(bf16[256,1536]{1,0:T(8,128)(2,1)} %get-tuple-element.42.refs_5_.refs_12_), channel_id=1, source_target_pairs={{4,16},{12,24},{16,4},{24,12},{5,17},{13,25},{17,5},{25,13},{6,18}... | collective-permute-start | bytes 2359304 | tf_op jit(solution)/shard_map/ppermute | solution.py:23
  165.5 35.3 %collective-permute-start.19 = (bf16[256,1536]{1,0:T(8,128)(2,1)}, bf16[256,1536]{1,0:T(8,128)(2,1)S(1)}, u32[]{:S(2)}, u32[]{:S(2)}) collective-permute-start(bf16[256,1536]{1,0:T(8,128)(2,1)} %collective-permute-done.12.refs_7_.refs_14_), channel_id=1, source_target_pairs={{0,4},{4,0},{8,12},{12,8},{16,20},{20,16},{24,28},{28,24},{1,5},{5... | collective-permute-start | bytes 2359304 | tf_op jit(solution)/shard_map/ppermute | solution.py:23
  167.3 32.2 %collective-permute-start.13 = (bf16[256,1536]{1,0:T(8,128)(2,1)}, bf16[256,1536]{1,0:T(8,128)(2,1)S(1)}, u32[]{:S(2)}, u32[]{:S(2)}) collective-permute-start(bf16[256,1536]{1,0:T(8,128)(2,1)} %collective-permute-done.12.refs_7_.refs_14_), channel_id=1, source_target_pairs={{0,16},{4,20},{24,8},{28,12},{1,17},{5,21},{25,9},{29,13},{2,18},{... | collective-permute-start | bytes 2359304 | tf_op jit(solution)/shard_map/ppermute | solution.py:23
  179.0 21.8 %collective-permute-start.17 = (bf16[256,1536]{1,0:T(8,128)(2,1)}, bf16[256,1536]{1,0:T(8,128)(2,1)S(1)}, u32[]{:S(2)}, u32[]{:S(2)}) collective-permute-start(bf16[256,1536]{1,0:T(8,128)(2,1)} %collective-permute-done.16.refs_3_.refs_10_), channel_id=1, source_target_pairs={{0,4},{4,0},{8,12},{12,8},{16,20},{20,16},{24,28},{28,24},{1,5},{5... | collective-permute-start | bytes 2359304 | tf_op jit(solution)/shard_map/ppermute | solution.py:23
  199.5 17.5 %collective-permute-start.14 = (bf16[256,1536]{1,0:T(8,128)(2,1)S(1)}, bf16[256,1536]{1,0:T(8,128)(2,1)S(1)}, u32[]{:S(2)}, u32[]{:S(2)}) collective-permute-start(bf16[256,1536]{1,0:T(8,128)(2,1)S(1)} %collective-permute-done.13.refs_3_.refs_5_), channel_id=1, source_target_pairs={{0,4},{4,0},{8,12},{12,8},{16,20},{20,16},{24,28},{28,24},{1,5},{5... | collective-permute-start | bytes 2359304 | tf_op jit(solution)/shard_map/ppermute | solution.py:23
  230.7 14.0 %collective-permute-start.30 = (bf16[256,768]{1,0:T(8,128)(2,1)}, bf16[256,768]{1,0:T(8,128)(2,1)S(1)}, u32[]{:S(2)}, u32[]{:S(2)}) collective-permute-start(bf16[256,768]{1,0:T(8,128)(2,1)} %get-tuple-element.45), channel_id=1, source_target_pairs={{0,1},{1,2},{2,3},{3,0},{4,5},{5,6},{6,7},{7,4},{8,9},{9,10},{10,1... | collective-permute-start | bytes 1179656 | tf_op jit(solution)/shard_map/ppermute | solution.py:23
  230.7 22.4 %collective-permute-start.33 = (bf16[256,768]{1,0:T(8,128)(2,1)}, bf16[256,768]{1,0:T(8,128)(2,1)S(1)}, u32[]{:S(2)}, u32[]{:S(2)}) collective-permute-start(bf16[256,768]{1,0:T(8,128)(2,1)} %get-tuple-element.46), channel_id=1, source_target_pairs={{0,1},{1,2},{2,3},{3,0},{4,5},{5,6},{6,7},{7,4},{8,9},{9,10},{10,1... | collective-permute-start | bytes 1179656 | tf_op jit(solution)/shard_map/ppermute | solution.py:23
  230.7 29.9 %collective-permute-start.36 = (bf16[256,768]{1,0:T(8,128)(2,1)}, bf16[256,768]{1,0:T(8,128)(2,1)S(1)}, u32[]{:S(2)}, u32[]{:S(2)}) collective-permute-start(bf16[256,768]{1,0:T(8,128)(2,1)} %get-tuple-element.47), channel_id=1, source_target_pairs={{0,1},{1,2},{2,3},{3,0},{4,5},{5,6},{6,7},{7,4},{8,9},{9,10},{10,1... | collective-permute-start | bytes 1179656 | tf_op jit(solution)/shard_map/ppermute | solution.py:23
  262.2 22.3 %collective-permute-start.34 = (bf16[256,768]{1,0:T(8,128)(2,1)S(1)}, bf16[256,768]{1,0:T(8,128)(2,1)S(1)}, u32[]{:S(2)}, u32[]{:S(2)}) collective-permute-start(bf16[256,768]{1,0:T(8,128)(2,1)S(1)} %get-tuple-element.104), channel_id=1, source_target_pairs={{0,1},{1,2},{2,3},{3,0},{4,5},{5,6},{6,7},{7,4},{8,9},{9,10},{10,1... | collective-permute-start | bytes 1179656 | tf_op jit(solution)/shard_map/ppermute | solution.py:23
  262.2 28.8 %collective-permute-start.37 = (bf16[256,768]{1,0:T(8,128)(2,1)S(1)}, bf16[256,768]{1,0:T(8,128)(2,1)S(1)}, u32[]{:S(2)}, u32[]{:S(2)}) collective-permute-start(bf16[256,768]{1,0:T(8,128)(2,1)S(1)} %get-tuple-element.103), channel_id=1, source_target_pairs={{0,1},{1,2},{2,3},{3,0},{4,5},{5,6},{6,7},{7,4},{8,9},{9,10},{10,1... | collective-permute-start | bytes 1179656 | tf_op jit(solution)/shard_map/ppermute | solution.py:23
  293.4 14.1 %collective-permute-start.32 = (bf16[256,768]{1,0:T(8,128)(2,1)}, bf16[256,768]{1,0:T(8,128)(2,1)S(1)}, u32[]{:S(2)}, u32[]{:S(2)}) collective-permute-start(bf16[256,768]{1,0:T(8,128)(2,1)} %get-tuple-element.102), channel_id=1, source_target_pairs={{0,1},{1,2},{2,3},{3,0},{4,5},{5,6},{6,7},{7,4},{8,9},{9,10},{10,1... | collective-permute-start | bytes 1179656 | tf_op jit(solution)/shard_map/ppermute | solution.py:23
  293.4 22.5 %collective-permute-start.35 = (bf16[256,768]{1,0:T(8,128)(2,1)}, bf16[256,768]{1,0:T(8,128)(2,1)S(1)}, u32[]{:S(2)}, u32[]{:S(2)}) collective-permute-start(bf16[256,768]{1,0:T(8,128)(2,1)} %get-tuple-element.101), channel_id=1, source_target_pairs={{0,1},{1,2},{2,3},{3,0},{4,5},{5,6},{6,7},{7,4},{8,9},{9,10},{10,1... | collective-permute-start | bytes 1179656 | tf_op jit(solution)/shard_map/ppermute | solution.py:23
  293.4 28.1 %collective-permute-start.38 = (bf16[256,768]{1,0:T(8,128)(2,1)}, bf16[256,768]{1,0:T(8,128)(2,1)S(1)}, u32[]{:S(2)}, u32[]{:S(2)}) collective-permute-start(bf16[256,768]{1,0:T(8,128)(2,1)} %get-tuple-element.100), channel_id=1, source_target_pairs={{0,1},{1,2},{2,3},{3,0},{4,5},{5,6},{6,7},{7,4},{8,9},{9,10},{10,1... | collective-permute-start | bytes 1179656 | tf_op jit(solution)/shard_map/ppermute | solution.py:23
  382.9 17.8 %collective-permute-start.50 = (bf16[256,768]{1,0:T(8,128)(2,1)S(1)}, bf16[256,768]{1,0:T(8,128)(2,1)S(1)}, u32[]{:S(2)}, u32[]{:S(2)}) collective-permute-start(bf16[256,768]{1,0:T(8,128)(2,1)S(1)} %collective-permute-done.45.refs_2_), channel_id=1, source_target_pairs={{0,1},{1,2},{2,3},{3,0},{4,5},{5,6},{6,7},{7,4},{8,9},{9,10},{10,1... | collective-permute-start | bytes 1179656 | tf_op jit(solution)/shard_map/ppermute | solution.py:23
  392.3 31.9 %collective-permute-start.58 = (bf16[256,768]{1,0:T(8,128)(2,1)S(1)}, bf16[256,768]{1,0:T(8,128)(2,1)S(1)}, u32[]{:S(2)}, u32[]{:S(2)}) collective-permute-start(bf16[256,768]{1,0:T(8,128)(2,1)S(1)} %get-tuple-element.53.refs_0_), channel_id=1, source_target_pairs={{0,1},{1,2},{2,3},{3,0},{4,5},{5,6},{6,7},{7,4},{8,9},{9,10},{10,1... | collective-permute-start | bytes 1179656 | tf_op jit(solution)/shard_map/ppermute | solution.py:23
  412.1 45.9 %collective-permute-start.71 = (bf16[256,1536]{1,0:T(8,128)(2,1)}, bf16[256,1536]{1,0:T(8,128)(2,1)S(1)}, u32[]{:S(2)}, u32[]{:S(2)}) collective-permute-start(bf16[256,1536]{1,0:T(8,128)(2,1)} %get-tuple-element.57.refs_3_.refs_15_), channel_id=1, source_target_pairs={{0,8},{4,12},{8,0},{12,4},{16,24},{20,28},{24,16},{28,20},{1,9},{5... | collective-permute-start | bytes 2359304 | tf_op jit(solution)/shard_map/ppermute | solution.py:23
  424.2 33.8 %collective-permute-start.70 = (bf16[256,1536]{1,0:T(8,128)(2,1)}, bf16[256,1536]{1,0:T(8,128)(2,1)S(1)}, u32[]{:S(2)}, u32[]{:S(2)}) collective-permute-start(bf16[256,1536]{1,0:T(8,128)(2,1)} %get-tuple-element.57.refs_3_.refs_15_), channel_id=1, source_target_pairs={{0,4},{4,0},{8,12},{12,8},{16,20},{20,16},{24,28},{28,24},{1,5},{5... | collective-permute-start | bytes 2359304 | tf_op jit(solution)/shard_map/ppermute | solution.py:23
  424.3 22.1 %collective-permute-start.57 = (bf16[256,768]{1,0:T(8,128)(2,1)S(1)}, bf16[256,768]{1,0:T(8,128)(2,1)S(1)}, u32[]{:S(2)}, u32[]{:S(2)}) collective-permute-start(bf16[256,768]{1,0:T(8,128)(2,1)S(1)} %collective-permute-done.52.refs_2_), channel_id=1, source_target_pairs={{0,1},{1,2},{2,3},{3,0},{4,5},{5,6},{6,7},{7,4},{8,9},{9,10},{10,1... | collective-permute-start | bytes 1179656 | tf_op jit(solution)/shard_map/ppermute | solution.py:23
  438.0 25.5 %collective-permute-start.60 = (bf16[256,768]{1,0:T(8,128)(2,1)S(1)}, bf16[256,768]{1,0:T(8,128)(2,1)S(1)}, u32[]{:S(2)}, u32[]{:S(2)}) collective-permute-start(bf16[256,768]{1,0:T(8,128)(2,1)S(1)} %collective-permute-done.59.refs_2_), channel_id=1, source_target_pairs={{0,1},{1,2},{2,3},{3,0},{4,5},{5,6},{6,7},{7,4},{8,9},{9,10},{10,1... | collective-permute-start | bytes 1179656 | tf_op jit(solution)/shard_map/ppermute | solution.py:23
  438.0 36.9 %collective-permute-start.73 = (bf16[256,1536]{1,0:T(8,128)(2,1)}, bf16[256,1536]{1,0:T(8,128)(2,1)S(1)}, u32[]{:S(2)}, u32[]{:S(2)}) collective-permute-start(bf16[256,1536]{1,0:T(8,128)(2,1)} %get-tuple-element.57.refs_3_.refs_15_), channel_id=1, source_target_pairs={{4,16},{12,24},{16,4},{24,12},{5,17},{13,25},{17,5},{25,13},{6,18}... | collective-permute-start | bytes 2359304 | tf_op jit(solution)/shard_map/ppermute | solution.py:23
  457.8 19.0 %collective-permute-start.64 = (bf16[256,1536]{1,0:T(8,128)(2,1)}, bf16[256,1536]{1,0:T(8,128)(2,1)}, u32[]{:S(2)}, u32[]{:S(2)}) collective-permute-start(bf16[256,1536]{1,0:T(8,128)(2,1)} %get-tuple-element.56.refs_10_.refs_22_), channel_id=1, source_target_pairs={{0,8},{4,12},{8,0},{12,4},{16,24},{20,28},{24,16},{28,20},{1,9},{5... | collective-permute-start | bytes 2359304 | tf_op jit(solution)/shard_map/ppermute | solution.py:23
  458.0 18.9 %collective-permute-start.76 = (bf16[256,1536]{1,0:T(8,128)(2,1)}, bf16[256,1536]{1,0:T(8,128)(2,1)S(1)}, u32[]{:S(2)}, u32[]{:S(2)}) collective-permute-start(bf16[256,1536]{1,0:T(8,128)(2,1)} %get-tuple-element.56.refs_10_.refs_22_), channel_id=1, source_target_pairs={{0,4},{4,0},{8,12},{12,8},{16,20},{20,16},{24,28},{28,24},{1,5},{5... | collective-permute-start | bytes 2359304 | tf_op jit(solution)/shard_map/ppermute | solution.py:23
  458.0 22.5 %collective-permute-start.74 = (bf16[256,1536]{1,0:T(8,128)(2,1)S(1)}, bf16[256,1536]{1,0:T(8,128)(2,1)}, u32[]{:S(2)}, u32[]{:S(2)}) collective-permute-start(bf16[256,1536]{1,0:T(8,128)(2,1)S(1)} %collective-permute-done.71.refs_5_.refs_17_), channel_id=1, source_target_pairs={{0,16},{4,20},{24,8},{28,12},{1,17},{5,21},{25,9},{29,13},{2,18},{... | collective-permute-start | bytes 2359304 | tf_op jit(solution)/shard_map/ppermute | solution.py:23
  463.6 17.0 %collective-permute-start.78 = (bf16[256,1536]{1,0:T(8,128)(2,1)}, bf16[256,1536]{1,0:T(8,128)(2,1)S(1)}, u32[]{:S(2)}, u32[]{:S(2)}) collective-permute-start(bf16[256,1536]{1,0:T(8,128)(2,1)} %get-tuple-element.56.refs_10_.refs_22_), channel_id=1, source_target_pairs={{4,16},{12,24},{16,4},{24,12},{5,17},{13,25},{17,5},{25,13},{6,18}... | collective-permute-start | bytes 2359304 | tf_op jit(solution)/shard_map/ppermute | solution.py:23
  475.0 18.9 %collective-permute-start.72 = (bf16[256,1536]{1,0:T(8,128)(2,1)S(1)}, bf16[256,1536]{1,0:T(8,128)(2,1)S(1)}, u32[]{:S(2)}, u32[]{:S(2)}) collective-permute-start(bf16[256,1536]{1,0:T(8,128)(2,1)S(1)} %collective-permute-done.71.refs_5_.refs_17_), channel_id=1, source_target_pairs={{0,4},{4,0},{8,12},{12,8},{16,20},{20,16},{24,28},{28,24},{1,5},{5... | collective-permute-start | bytes 2359304 | tf_op jit(solution)/shard_map/ppermute | solution.py:23
  476.9 17.0 %collective-permute-start.77 = (bf16[256,1536]{1,0:T(8,128)(2,1)}, bf16[256,1536]{1,0:T(8,128)(2,1)S(1)}, u32[]{:S(2)}, u32[]{:S(2)}) collective-permute-start(bf16[256,1536]{1,0:T(8,128)(2,1)} %collective-permute-done.64.refs_12_.refs_24_), channel_id=1, source_target_pairs={{0,4},{4,0},{8,12},{12,8},{16,20},{20,16},{24,28},{28,24},{1,5},{5... | collective-permute-start | bytes 2359304 | tf_op jit(solution)/shard_map/ppermute | solution.py:23
  476.9 20.2 %collective-permute-start.61 = (bf16[256,1536]{1,0:T(8,128)(2,1)}, bf16[256,1536]{1,0:T(8,128)(2,1)S(1)}, u32[]{:S(2)}, u32[]{:S(2)}) collective-permute-start(bf16[256,1536]{1,0:T(8,128)(2,1)} %get-tuple-element.55.refs_5_.refs_12_), channel_id=1, source_target_pairs={{0,8},{4,12},{8,0},{12,4},{16,24},{20,28},{24,16},{28,20},{1,9},{5... | collective-permute-start | bytes 2359304 | tf_op jit(solution)/shard_map/ppermute | solution.py:23
  480.5 16.6 %collective-permute-start.75 = (bf16[256,1536]{1,0:T(8,128)(2,1)}, bf16[256,1536]{1,0:T(8,128)(2,1)S(1)}, u32[]{:S(2)}, u32[]{:S(2)}) collective-permute-start(bf16[256,1536]{1,0:T(8,128)(2,1)} %collective-permute-done.74.refs_8_.refs_20_), channel_id=1, source_target_pairs={{0,4},{4,0},{8,12},{12,8},{16,20},{20,16},{24,28},{28,24},{1,5},{5... | collective-permute-start | bytes 2359304 | tf_op jit(solution)/shard_map/ppermute | solution.py:23
  480.5 30.7 %collective-permute-start.65 = (bf16[256,1536]{1,0:T(8,128)(2,1)}, bf16[256,1536]{1,0:T(8,128)(2,1)}, u32[]{:S(2)}, u32[]{:S(2)}) collective-permute-start(bf16[256,1536]{1,0:T(8,128)(2,1)} %collective-permute-done.64.refs_12_.refs_24_), channel_id=1, source_target_pairs={{0,16},{4,20},{24,8},{28,12},{1,17},{5,21},{25,9},{29,13},{2,18},{... | collective-permute-start | bytes 2359304 | tf_op jit(solution)/shard_map/ppermute | solution.py:23
  493.9 39.0 %collective-permute-start.67 = (bf16[256,1536]{1,0:T(8,128)(2,1)}, bf16[256,1536]{1,0:T(8,128)(2,1)S(1)}, u32[]{:S(2)}, u32[]{:S(2)}) collective-permute-start(bf16[256,1536]{1,0:T(8,128)(2,1)} %get-tuple-element.55.refs_5_.refs_12_), channel_id=1, source_target_pairs={{0,4},{4,0},{8,12},{12,8},{16,20},{20,16},{24,28},{28,24},{1,5},{5... | collective-permute-start | bytes 2359304 | tf_op jit(solution)/shard_map/ppermute | solution.py:23
  493.9 39.0 %collective-permute-start.69 = (bf16[256,1536]{1,0:T(8,128)(2,1)}, bf16[256,1536]{1,0:T(8,128)(2,1)}, u32[]{:S(2)}, u32[]{:S(2)}) collective-permute-start(bf16[256,1536]{1,0:T(8,128)(2,1)} %get-tuple-element.55.refs_5_.refs_12_), channel_id=1, source_target_pairs={{4,16},{12,24},{16,4},{24,12},{5,17},{13,25},{17,5},{25,13},{6,18}... | collective-permute-start | bytes 2359304 | tf_op jit(solution)/shard_map/ppermute | solution.py:23
  497.1 35.8 %collective-permute-start.68 = (bf16[256,1536]{1,0:T(8,128)(2,1)S(1)}, bf16[256,1536]{1,0:T(8,128)(2,1)}, u32[]{:S(2)}, u32[]{:S(2)}) collective-permute-start(bf16[256,1536]{1,0:T(8,128)(2,1)S(1)} %collective-permute-done.61.refs_7_.refs_14_), channel_id=1, source_target_pairs={{0,4},{4,0},{8,12},{12,8},{16,20},{20,16},{24,28},{28,24},{1,5},{5... | collective-permute-start | bytes 2359304 | tf_op jit(solution)/shard_map/ppermute | solution.py:23
  497.1 34.6 %collective-permute-start.62 = (bf16[256,1536]{1,0:T(8,128)(2,1)S(1)}, bf16[256,1536]{1,0:T(8,128)(2,1)S(1)}, u32[]{:S(2)}, u32[]{:S(2)}) collective-permute-start(bf16[256,1536]{1,0:T(8,128)(2,1)S(1)} %collective-permute-done.61.refs_7_.refs_14_), channel_id=1, source_target_pairs={{0,16},{4,20},{24,8},{28,12},{1,17},{5,21},{25,9},{29,13},{2,18},{... | collective-permute-start | bytes 2359304 | tf_op jit(solution)/shard_map/ppermute | solution.py:23
  511.2 21.7 %collective-permute-start.66 = (bf16[256,1536]{1,0:T(8,128)(2,1)}, bf16[256,1536]{1,0:T(8,128)(2,1)}, u32[]{:S(2)}, u32[]{:S(2)}) collective-permute-start(bf16[256,1536]{1,0:T(8,128)(2,1)} %collective-permute-done.65.refs_3_.refs_10_), channel_id=1, source_target_pairs={{0,4},{4,0},{8,12},{12,8},{16,20},{20,16},{24,28},{28,24},{1,5},{5... | collective-permute-start | bytes 2359304 | tf_op jit(solution)/shard_map/ppermute | solution.py:23
  531.7 16.0 %collective-permute-start.63 = (bf16[256,1536]{1,0:T(8,128)(2,1)S(1)}, bf16[256,1536]{1,0:T(8,128)(2,1)S(1)}, u32[]{:S(2)}, u32[]{:S(2)}) collective-permute-start(bf16[256,1536]{1,0:T(8,128)(2,1)S(1)} %collective-permute-done.62.refs_3_.refs_5_), channel_id=1, source_target_pairs={{0,4},{4,0},{8,12},{12,8},{16,20},{20,16},{24,28},{28,24},{1,5},{5... | collective-permute-start | bytes 2359304 | tf_op jit(solution)/shard_map/ppermute | solution.py:23
  561.3 14.0 %collective-permute-start.80 = (bf16[256,768]{1,0:T(8,128)(2,1)}, bf16[256,768]{1,0:T(8,128)(2,1)S(1)}, u32[]{:S(2)}, u32[]{:S(2)}) collective-permute-start(bf16[256,768]{1,0:T(8,128)(2,1)} %get-tuple-element.60), channel_id=1, source_target_pairs={{0,1},{1,2},{2,3},{3,0},{4,5},{5,6},{6,7},{7,4},{8,9},{9,10},{10,1... | collective-permute-start | bytes 1179656 | tf_op jit(solution)/shard_map/ppermute | solution.py:23
  561.3 22.4 %collective-permute-start.84 = (bf16[256,768]{1,0:T(8,128)(2,1)}, bf16[256,768]{1,0:T(8,128)(2,1)S(1)}, u32[]{:S(2)}, u32[]{:S(2)}) collective-permute-start(bf16[256,768]{1,0:T(8,128)(2,1)} %get-tuple-element.62), channel_id=1, source_target_pairs={{0,1},{1,2},{2,3},{3,0},{4,5},{5,6},{6,7},{7,4},{8,9},{9,10},{10,1... | collective-permute-start | bytes 1179656 | tf_op jit(solution)/shard_map/ppermute | solution.py:23
  561.3 29.9 %collective-permute-start.88 = (bf16[256,768]{1,0:T(8,128)(2,1)}, bf16[256,768]{1,0:T(8,128)(2,1)S(1)}, u32[]{:S(2)}, u32[]{:S(2)}) collective-permute-start(bf16[256,768]{1,0:T(8,128)(2,1)} %get-tuple-element.64), channel_id=1, source_target_pairs={{0,1},{1,2},{2,3},{3,0},{4,5},{5,6},{6,7},{7,4},{8,9},{9,10},{10,1... | collective-permute-start | bytes 1179656 | tf_op jit(solution)/shard_map/ppermute | solution.py:23
  592.8 13.9 %collective-permute-start.81 = (bf16[256,768]{1,0:T(8,128)(2,1)S(1)}, bf16[256,768]{1,0:T(8,128)(2,1)S(1)}, u32[]{:S(2)}, u32[]{:S(2)}) collective-permute-start(bf16[256,768]{1,0:T(8,128)(2,1)S(1)} %get-tuple-element.97), channel_id=1, source_target_pairs={{0,1},{1,2},{2,3},{3,0},{4,5},{5,6},{6,7},{7,4},{8,9},{9,10},{10,1... | collective-permute-start | bytes 1179656 | tf_op jit(solution)/shard_map/ppermute | solution.py:23
  592.8 29.3 %collective-permute-start.79 = (f32[256,768]{1,0:T(8,128)S(1)}, f32[256,768]{1,0:T(8,128)S(1)}, u32[]{:S(2)}, u32[]{:S(2)}) collective-permute-start(f32[256,768]{1,0:T(8,128)S(1)} %copy-done.8), channel_id=1, source_target_pairs={{0,4},{4,8},{8,12},{12,16},{16,20},{20,24},{24,28},{1,5},{5,9},{9,... | collective-permute-start | bytes 2359304 | tf_op jit(solution)/shard_map/ppermute | solution.py:23
  594.2 20.9 %collective-permute-start.85 = (bf16[256,768]{1,0:T(8,128)(2,1)S(1)}, bf16[256,768]{1,0:T(8,128)(2,1)S(1)}, u32[]{:S(2)}, u32[]{:S(2)}) collective-permute-start(bf16[256,768]{1,0:T(8,128)(2,1)S(1)} %get-tuple-element.99), channel_id=1, source_target_pairs={{0,1},{1,2},{2,3},{3,0},{4,5},{5,6},{6,7},{7,4},{8,9},{9,10},{10,1... | collective-permute-start | bytes 1179656 | tf_op jit(solution)/shard_map/ppermute | solution.py:23
  594.2 27.4 %collective-permute-start.89 = (bf16[256,768]{1,0:T(8,128)(2,1)S(1)}, bf16[256,768]{1,0:T(8,128)(2,1)S(1)}, u32[]{:S(2)}, u32[]{:S(2)}) collective-permute-start(bf16[256,768]{1,0:T(8,128)(2,1)S(1)} %get-tuple-element.98), channel_id=1, source_target_pairs={{0,1},{1,2},{2,3},{3,0},{4,5},{5,6},{6,7},{7,4},{8,9},{9,10},{10,1... | collective-permute-start | bytes 1179656 | tf_op jit(solution)/shard_map/ppermute | solution.py:23
  595.0 27.7 %collective-permute-start.83 = (f32[256,768]{1,0:T(8,128)S(1)}, f32[256,768]{1,0:T(8,128)S(1)}, u32[]{:S(2)}, u32[]{:S(2)}) collective-permute-start(f32[256,768]{1,0:T(8,128)S(1)} %get-tuple-element.61), channel_id=1, source_target_pairs={{0,4},{4,8},{8,12},{12,16},{16,20},{20,24},{24,28},{1,5},{5,9},{9,... | collective-permute-start | bytes 2359304 | tf_op jit(solution)/shard_map/ppermute | solution.py:23
  606.7 16.1 %collective-permute-start.87 = (f32[256,768]{1,0:T(8,128)S(1)}, f32[256,768]{1,0:T(8,128)S(1)}, u32[]{:S(2)}, u32[]{:S(2)}) collective-permute-start(f32[256,768]{1,0:T(8,128)S(1)} %get-tuple-element.63), channel_id=1, source_target_pairs={{0,4},{4,8},{8,12},{12,16},{16,20},{20,24},{24,28},{1,5},{5,9},{9,... | collective-permute-start | bytes 2359304 | tf_op jit(solution)/shard_map/ppermute | solution.py:23
  622.0 13.9 %collective-permute-start.82 = (bf16[256,768]{1,0:T(8,128)(2,1)S(1)}, bf16[256,768]{1,0:T(8,128)(2,1)S(1)}, u32[]{:S(2)}, u32[]{:S(2)}) collective-permute-start(bf16[256,768]{1,0:T(8,128)(2,1)S(1)} %get-tuple-element.94), channel_id=1, source_target_pairs={{0,1},{1,2},{2,3},{3,0},{4,5},{5,6},{6,7},{7,4},{8,9},{9,10},{10,1... | collective-permute-start | bytes 1179656 | tf_op jit(solution)/shard_map/ppermute | solution.py:23
  622.0 22.3 %collective-permute-start.86 = (bf16[256,768]{1,0:T(8,128)(2,1)S(1)}, bf16[256,768]{1,0:T(8,128)(2,1)S(1)}, u32[]{:S(2)}, u32[]{:S(2)}) collective-permute-start(bf16[256,768]{1,0:T(8,128)(2,1)S(1)} %get-tuple-element.96), channel_id=1, source_target_pairs={{0,1},{1,2},{2,3},{3,0},{4,5},{5,6},{6,7},{7,4},{8,9},{9,10},{10,1... | collective-permute-start | bytes 1179656 | tf_op jit(solution)/shard_map/ppermute | solution.py:23
  622.1 27.8 %collective-permute-start.90 = (bf16[256,768]{1,0:T(8,128)(2,1)S(1)}, bf16[256,768]{1,0:T(8,128)(2,1)S(1)}, u32[]{:S(2)}, u32[]{:S(2)}) collective-permute-start(bf16[256,768]{1,0:T(8,128)(2,1)S(1)} %get-tuple-element.95), channel_id=1, source_target_pairs={{0,1},{1,2},{2,3},{3,0},{4,5},{5,6},{6,7},{7,4},{8,9},{9,10},{10,1... | collective-permute-start | bytes 1179656 | tf_op jit(solution)/shard_map/ppermute | solution.py:23
  (86 other events, 1572.3 us)

commit v2 on v1

--- a/solution.py
+++ b/solution.py
@@ -15,6 +15,7 @@
 VMEM = 56 * 1024 * 1024
 
 epsilon = 1e-06
+QUICK = pl.CostEstimate(flops=1000, bytes_accessed=1000, transcendentals=0)
 
 
 def permute(block, axis, route):
@@ -83,11 +84,7 @@
             jax.ShapeDtypeStruct((rows, 2 * columns), jnp.bfloat16),
         ],
         compiler_params=pltpu.CompilerParams(vmem_limit_bytes=VMEM),
-        cost_estimate=pl.CostEstimate(
-            flops=2 * rows * columns * parts * 3 * columns,
-            bytes_accessed=2 * (columns * parts * 3 * columns + rows * columns * (parts + 3)),
-            transcendentals=0,
-        ),
+        cost_estimate=QUICK,
         name="qkv",
     )(order, norm_gain, *inputs, *([weight] * parts))
 
@@ -124,7 +121,7 @@
                 out_ref[at, :] = total
 
 
-def attend(queries, blocks, usable, running, last, head_dim):
+def attend(queries, blocks, parts, usable, running, last, head_dim):
     height, columns = queries[0].shape
     chunks = len(queries)
     rows = height * chunks
@@ -133,22 +130,21 @@
     first = running is None
     tile = TILE if height % TILE == 0 else height
 
-    def key_spec(block):
-        return pl.BlockSpec((block.shape[0], head_dim), lambda h, usable: (0, h))
-
-    def value_spec(block):
-        return pl.BlockSpec((block.shape[0], head_dim), lambda h, usable: (0, heads + h))
+    def key_spec(part):
+        return pl.BlockSpec((height, head_dim), lambda h, usable: (part, h))
+
+    def value_spec(part):
+        return pl.BlockSpec((height, head_dim), lambda h, usable: (part, heads + h))
 
     running_spec = pl.BlockSpec((None, rows, 2 * head_dim), lambda h, usable: (h, 0, 0))
-    key_rows = sum(block.shape[0] for block in blocks)
     return pl.pallas_call(
         functools.partial(attend_kernel, chunks, pieces, first, last, tile),
         grid_spec=pltpu.PrefetchScalarGridSpec(
             num_scalar_prefetch=1,
             grid=(heads,),
             in_specs=[pl.BlockSpec((height, head_dim), lambda h, usable: (0, h)) for _ in queries]
-            + [key_spec(block) for block in blocks]
-            + [value_spec(block) for block in blocks]
+            + [key_spec(part) for part in parts]
+            + [value_spec(part) for part in parts]
             + ([] if first else [running_spec]),
             out_specs=pl.BlockSpec((rows, head_dim), lambda h, usable: (0, h)) if last else running_spec,
         ),
@@ -156,11 +152,7 @@
         if last
         else jax.ShapeDtypeStruct((heads, rows, 2 * head_dim), jnp.float32),
         compiler_params=pltpu.CompilerParams(vmem_limit_bytes=VMEM),
-        cost_estimate=pl.CostEstimate(
-            flops=8 * rows * key_rows * columns,
-            bytes_accessed=4 * key_rows * columns + 12 * rows * columns,
-            transcendentals=rows * key_rows * heads,
-        ),
+        cost_estimate=QUICK,
         name="attend",
     )(usable, *queries, *blocks, *blocks, *([] if first else [running]))
 
@@ -205,13 +197,102 @@
         ),
         out_shape=out_shape,
         compiler_params=pltpu.CompilerParams(vmem_limit_bytes=VMEM),
-        cost_estimate=pl.CostEstimate(
-            flops=2 * rows * depth * columns * count,
-            bytes_accessed=2 * (rows * depth + count * columns * (rows + depth)),
-            transcendentals=0,
-        ),
+        cost_estimate=QUICK,
         name="shares",
     )(order, attended, weight)
+
+
+def add_kernel(total_ref, share_ref, out_ref):
+    out_ref[...] = (total_ref[...].astype(jnp.float32) + share_ref[...].astype(jnp.float32)).astype(out_ref.dtype)
+
+
+def add_share(total, others, hop, index, dtype):
+    rows, columns = total.shape
+    return pl.pallas_call(
+        add_kernel,
+        grid=(1,),
+        in_specs=[
+            pl.BlockSpec((rows, columns), lambda j: (0, 0)),
+            pl.BlockSpec((None, rows, columns), lambda j: (hop, index, 0)),
+        ],
+        out_specs=pl.BlockSpec((rows, columns), lambda j: (0, 0)),
+        out_shape=jax.ShapeDtypeStruct((rows, columns), dtype),
+        compiler_params=pltpu.CompilerParams(vmem_limit_bytes=VMEM),
+        cost_estimate=QUICK,
+        name="add_share",
+    )(total, others)
+
+
+def turn_kernel(full_width, leaves_ref, total_ref, share_ref, latent_ref, fresh_ref, rows_ref, out_ref, sums_ref):
+    total = total_ref[...].astype(jnp.float32) + share_ref[...].astype(jnp.float32)
+    latent = latent_ref[...]
+    advanced = latent + rows_ref[1:2, :] * (latent + rows_ref[0:1, :] * total)
+    kept = jnp.where(leaves_ref[0] != 0, fresh_ref[...], advanced)
+    out_ref[...] = kept
+    lane = lax.broadcasted_iota(jnp.int32, (kept.shape[0], 128), 1)
+    first = jnp.sum(kept, axis=1, keepdims=True)
+    second = jnp.sum(kept * kept, axis=1, keepdims=True)
+    both = jnp.where(lane == 0, first, jnp.where(lane == 1, second, 0.0))
+    sums_ref[...] = jnp.transpose(both)[: sums_ref.shape[0]]
+
+
+def turn(total, others, hop, index, latent, fresh, rows, leaves, full_width):
+    height, columns = total.shape
+    whole = pl.BlockSpec((height, columns), lambda j, leaves: (0, 0))
+    return pl.pallas_call(
+        functools.partial(turn_kernel, full_width),
+        grid_spec=pltpu.PrefetchScalarGridSpec(
+            num_scalar_prefetch=1,
+            grid=(1,),
+            in_specs=[
+                whole,
+                pl.BlockSpec((None, height, columns), lambda j, leaves: (hop, index, 0)),
+                pl.BlockSpec((height, columns), lambda j, leaves: (index, 0)),
+                pl.BlockSpec((height, columns), lambda j, leaves: (index, 0)),
+                pl.BlockSpec((2, columns), lambda j, leaves: (0, 0)),
+            ],
+            out_specs=[whole, pl.BlockSpec((8, height), lambda j, leaves: (0, 0))],
+        ),
+        out_shape=[
+            jax.ShapeDtypeStruct((height, columns), jnp.float32),
+            jax.ShapeDtypeStruct((8, height), jnp.float32),
+        ],
+        compiler_params=pltpu.CompilerParams(vmem_limit_bytes=VMEM),
+        cost_estimate=QUICK,
+        name="turn",
+    )(leaves, total, others, latent, fresh, rows)
+
+
+def normalize_kernel(full_width, count, block_ref, rows_ref, *refs):
+    sums = refs[0][...]
+    for part in range(1, count):
+        sums = sums + refs[part][...]
+    upright = jnp.transpose(sums)
+    mean = upright[:, 0:1] / full_width
+    var = upright[:, 1:2] / full_width - mean * mean
+    out_ref = refs[count]
+    out_ref[...] = (
+        (block_ref[...] - mean) * lax.rsqrt(var + epsilon) * (1.0 + rows_ref[1:2, :]) + rows_ref[0:1, :]
+    ).astype(out_ref.dtype)
+
+
+def normalize_turned(block, sums, rows, full_width):
+    size = lax.axis_size("tensor")
+    everyone = [sums]
+    for distance in range(1, size):
+        everyone.append(permute(sums, "tensor", lambda i: (i + distance) % size))
+    return pl.pallas_call(
+        functools.partial(normalize_kernel, full_width, size),
+        out_shape=jax.ShapeDtypeStruct(block.shape, jnp.bfloat16),
+        compiler_params=pltpu.CompilerParams(vmem_limit_bytes=VMEM),
+        cost_estimate=QUICK,
+        name="normalize",
+    )(block, rows, *everyone)
+
+
+def onward(block):
+    size = lax.axis_size("frame")
+    return permute(block, "frame", lambda i: (i + 1) % size)
 
 
 def summed(block):
@@ -243,13 +324,26 @@
 
 
 def halo(pair):
-    across = permute(pair, "frame", lambda i: i ^ 2)
-    near = sibling(pair)
-    third = permute(pair, "frame", lambda i: i + (3 if i % 2 else -3))
-    second = permute(across, "frame", lambda i: i + (QUAD if i % QUAD < 2 else -QUAD))
     return dict(
-        own=pair, near=near, across=across, beyond=sibling(across), third=third, second=second, other=sibling(second)
+        own=pair,
+        across=permute(pair, "frame", lambda i: i ^ 2),
+        third=permute(pair, "frame", lambda i: i + (3 if i % 2 else -3)),
     )
+
+
+def halo_second(held):
+    held["second"] = permute(held["across"], "frame", lambda i: i + (QUAD if i % QUAD < 2 else -QUAD))
+
+
+def halo_sibling(held):
+    held["sibling"] = sibling(jnp.concatenate([held["own"], held["across"], held["second"]]))
+
+
+SIBLING = dict(near=0, beyond=1, other=2)
+
+
+def tie(*arrays):
+    return lax.optimization_barrier(arrays)
 
 
 SOURCES = ("own", "near", "across", "beyond", "third", "second", "other")
@@ -300,8 +394,10 @@
     level = levels[0]
     shift, scale, gate = pieces_of(level)
     step_size = lax.dynamic_index_in_dim(step_table, level, 0, keepdims=False)
-    next_level = permute(levels, "frame", lambda i: i - 1)[0]
-    next_shift, next_scale, _ = pieces_of(next_level)
+    next_level = permute(levels, "frame", lambda i: (i - 1) % frames)[0]
+    next_rows = jnp.stack(pieces_of(next_level)[:2])
+    update_rows = jnp.stack([gate, jnp.full_like(gate, step_size)])
+    leaves = (slot == frames - 1).astype(jnp.int32).reshape(1)
     usable = usable_sources(slot, frames, reach_slot[0])
     gather_order = (place - jnp.arange(tensor_count, dtype=jnp.int32)) % tensor_count
     scatter_order = (place - 1 - jnp.arange(tensor_count, dtype=jnp.int32)) % tensor_count
@@ -310,78 +406,101 @@
     def chunk(array, index):
         return array[index * height : (index + 1) * height]
 
-    first_sums = summed(jnp.concatenate([sums_of(queue_state), sums_of(fresh_noise)]))
+    first_sums = summed(sums_of(queue_state))
     normed = [
-        normalize(chunk(queue_state, i), chunk_sums(first_sums[:2], i, height), full_width, shift, scale)
+        normalize(chunk(queue_state, i), chunk_sums(first_sums, i, height), full_width, shift, scale)
         for i in range(CHUNKS)
     ]
-    latents = [chunk(queue_state, i) for i in range(CHUNKS)]
-    fresh_normed = normalize(fresh_noise, first_sums[2:], full_width, shift, scale)
-    advanced = None
+    latents = None
+    kept = None
 
     for step_number in range(STEPS):
         queries, sources = [], []
-        waiting = None
+        gathered = [normed[0]]
+        for _ in range(tensor_count - 2):
+            gathered.append(ring(gathered[-1]))
         for i in range(CHUNKS):
-            own = normed[i]
-            if waiting is not None:
-                gathered_before, own = lax.optimization_barrier((waiting[-1], own))
-                waiting[-1] = gathered_before
-                waiting.append(ring(waiting[-1]))
-                query, pair = project(waiting, weights, gather_order, norm_gain)
-                queries.append(query)
-                sources.append(halo(pair))
-            waiting = [own]
-            for _ in range(tensor_count - 2):
-                waiting.append(ring(waiting[-1]))
-        waiting.append(ring(waiting[-1]))
-        query, pair = project(waiting, weights, gather_order, norm_gain)
-        queries.append(query)
-        sources.append(halo(pair))
-
-        def flags(names):
-            return jnp.stack([usable[name] for _, name in names])
-
+            if i > 0:
+                gathered[-1], sources[-1]["own"] = tie(gathered[-1], sources[-1]["own"])
+            following = None
+            if i + 1 < CHUNKS:
+                gathered[-1], own = tie(gathered[-1], normed[i + 1])
+                last, arrived = tie(ring(gathered[-1]), ring(own))
+                following = [own, arrived]
+                for _ in range(tensor_count - 3):
+                    following.append(ring(following[-1]))
+            else:
+                last = ring(gathered[-1])
+            if i > 1:
+                last, sources[-2]["second"] = tie(last, sources[-2]["second"])
+                halo_sibling(sources[-2])
+            if 0 < i < CHUNKS - 1:
+                last, sources[-1]["across"] = tie(last, sources[-1]["across"])
+                halo_second(sources[-1])
+            query, pair = project(gathered + [last], weights, gather_order, norm_gain)
+            queries.append(query)
+            sources.append(halo(pair))
+            gathered = following
         final = CHUNKS - 1
-        late_names = ("second", "other")
         early = [(i, name) for i in range(final - 1) for name in SOURCES]
-        early += [(final - 1, name) for name in SOURCES if name not in late_names]
-        middle = [(final - 1, name) for name in late_names]
-        middle += [(final, name) for name in SOURCES if name not in late_names]
-        late = [(final, name) for name in late_names]
-        running = None
-        for names in (early, middle, late):
-            running = attend(
+        early += [(final - 1, name) for name in ("own", "across", "third")] + [(final, "own")]
+        middle = [(final - 1, "second"), (final, "across"), (final, "third")]
+        middle += [(final - 1, name) for name in SIBLING]
+        late = [(final, "second")] + [(final, name) for name in SIBLING]
+
+        def absorb(names, running, last):
+            return attend(
                 queries,
-                [sources[i][name] for i, name in names],
-                flags(names),
+                [sources[i]["sibling" if name in SIBLING else name] for i, name in names],
+                [SIBLING.get(name, 0) for _, name in names],
+                jnp.stack([usable[name] for _, name in names]),
                 running,
-                names is late,
+                last,
                 head_dim,
             )
 
+        before, after = sources[-2], sources[-1]
+        queries[-1], before["across"] = tie(queries[-1], before["across"])
+        halo_second(before)
+        running = absorb(early, None, False)
+        running, before["second"], after["across"] = tie(running, before["second"], after["across"])
+        halo_second(after)
+        halo_sibling(before)
+        running = absorb(middle, running, False)
+        running, after["second"] = tie(running, after["second"])
+        halo_sibling(after)
+        running = absorb(late, running, True)
+
         if step_number > 0:
-            advanced, running = lax.optimization_barrier((advanced, running))
-            moved = [permute(done, "frame", lambda i: i + 1) for done in advanced]
-            latents = [jnp.where(slot == 0, chunk(fresh_noise, j), moved[j]) for j in range(CHUNKS)]
+            kept, running = tie(kept, running)
+            latents = [onward(block) for block in kept]
 
         totals = list(shares(running, output_weight, scatter_order[:1], CHUNKS))
         others = shares(running, output_weight, scatter_order[1:], 0)
+        turning = step_number < STEPS - 1
         for hop in range(tensor_count - 1):
+            last = hop == tensor_count - 2
             for j in range(CHUNKS):
-                total = ring(totals[j]).astype(jnp.float32) + chunk(others[hop], j).astype(jnp.float32)
-                totals[j] = total.astype(jnp.bfloat16) if hop < tensor_count - 2 else total
-        advanced = [
-            latents[j] + step_size * (latents[j] + gate * totals[j]) for j in range(CHUNKS)
-        ]
-        if step_number < STEPS - 1:
-            normed = []
+                totals[j] = ring(totals[j])
+                if not (last and turning):
+                    totals[j] = add_share(totals[j], others, hop, j, jnp.float32 if last else jnp.bfloat16)
+        if turning:
+            kept, normed = [], []
             for j in range(CHUNKS):
-                sums = summed(sums_of(advanced[j]))
-                ready = permute(
-                    normalize(advanced[j], sums, full_width, next_shift, next_scale), "frame", lambda i: i + 1
+                block, sums = turn(
+                    totals[j],
+                    others,
+                    tensor_count - 2,
+                    j,
+                    queue_state,
+                    fresh_noise,
+                    update_rows,
+                    leaves,
+                    full_width,
                 )
-                normed.append(jnp.where(slot == 0, chunk(fresh_normed, j), ready))
+                kept.append(block)
+                normed.append(onward(normalize_turned(block, sums, next_rows, full_width)))
+    advanced = [latents[j] + step_size * (latents[j] + gate * totals[j]) for j in range(CHUNKS)]
     return jnp.concatenate(advanced, axis=0)
 
 

time: 662 us -> 638 us (0.964)
  waiting for transfers between devices: 325 us -> 255 us
  Pallas kernels: 172 us -> 217 us
  starting transfers between devices: 120 us -> 97.9 us
  local copies, waits for them, and re-layouts: 12.2 us -> 28.8 us
    ppermute x91 -> x79, waiting for transfers between devices: 325 us -> 255 us  [permute(): return lax.ppermute(block, axis, pairs)]
    pallas_call x0 -> x21, Pallas kernels: none -> 44.9 us  [the longest x15 29.7 us: add_share(): pl.pallas_call(add_kernel, grid=(1,), in_specs=[pl.BlockSpec((rows, colum...]
    ppermute x91 -> x79, starting transfers between devices: 120 us -> 97.9 us  [permute(): return lax.ppermute(block, axis, pairs)]
    unnamed x118 -> x170, local copies, waits for them, and re-layouts: 9 us -> 25.2 us
    concatenate x1 -> x6, other arithmetic: 0.02 us -> 13.3 us  [halo_sibling(): jnp.concatenate([held['own'], held['across'], held['second']])]
  transfers between devices with their start and end apart: 91 -> 79, of which waited for: 43 -> 41; matrix products, arithmetic and copies ran while one was open for 1% -> 1% of each run, Pallas kernels for 22% -> 30%
where the time goes in v2:
time: 638 us; the launch traced here: 627 us
  waiting for transfers between devices  255 us (40%)
  Pallas kernels  217 us (34%)
  starting transfers between devices  97.9 us (15%)
  local copies, waits for them, and re-layouts  28.8 us (5%)
  other arithmetic  23.6 us (4%)
    ppermute x79, waiting for transfers between devices, permute(): return lax.ppermute(block, axis, pairs)  255 us
    ppermute x79, starting transfers between devices, permute(): return lax.ppermute(block, axis, pairs)  97.9 us
    pallas_call x6, Pallas kernels, attend(): pl.pallas_call(functools.partial(attend_kernel, chunks, pieces, first, la...  85 us
    pallas_call x6, Pallas kernels, project(): pl.pallas_call(functools.partial(qkv_kernel, parts, columns // head_dim,...  63.7 us
    pallas_call x15, Pallas kernels, add_share(): pl.pallas_call(add_kernel, grid=(1,), in_specs=[pl.BlockSpec((rows, colum...  29.7 us
    unnamed x170, local copies, waits for them, and re-layouts  25.2 us
    pallas_call x4, Pallas kernels, shares(): pl.pallas_call(kernel, grid_spec=pltpu.PrefetchScalarGridSpec(num_scalar_...  23 us
    concatenate x6, other arithmetic, halo_sibling(): jnp.concatenate([held['own'], held['across'], held['second']])  13.3 us
  transfers between devices with their start and end apart: 79, of which 41 were waited for; matrix products, arithmetic and copies ran while one was open for 1% of the time, Pallas kernels for 30%

profile of v2, /device:TPU:0, one launch (start us, length us, event | category | flops | bytes accessed | tf_op | source)
XLA Modules:
  0.0 626.7 jit_solution(13610852293479900325)
XLA Ops:
  2.2 3.1 collective-permute-start
  16.6 12.8 %collective-permute-done.3.refs_1_ = bf16[256,768]{1,0:T(8,128)(2,1)S(1)} collective-permute-done((bf16[256,768]{1,0:T(8,128)(2,1)S(1)}, bf16[256,768]{1,0:T(8,128)(2,1)S(1)}, u32[]{:S(2)}, u32[]{:S(2)}) %collective-permute-start.3) | collective-permute-done | bytes 393248 | tf_op jit(solution)/shard_map/ppermute | solution.py:24
  29.4 12.7 %collective-permute-done.4.refs_2_ = bf16[256,768]{1,0:T(8,128)(2,1)S(1)} collective-permute-done((bf16[256,768]{1,0:T(8,128)(2,1)S(1)}, bf16[256,768]{1,0:T(8,128)(2,1)S(1)}, u32[]{:S(2)}, u32[]{:S(2)}) %collective-permute-start.4) | collective-permute-done | bytes 393248 | tf_op jit(solution)/shard_map/ppermute | solution.py:24
  42.0 13.8 %collective-permute-done.5.refs_3_ = bf16[256,768]{1,0:T(8,128)(2,1)S(1)} collective-permute-done((bf16[256,768]{1,0:T(8,128)(2,1)S(1)}, bf16[256,768]{1,0:T(8,128)(2,1)S(1)}, u32[]{:S(2)}, u32[]{:S(2)}) %collective-permute-start.5) | collective-permute-done | bytes 393248 | tf_op jit(solution)/shard_map/ppermute | solution.py:24
  55.9 6.4 %collective-permute-done.6.refs_1_ = bf16[256,768]{1,0:T(8,128)(2,1)S(1)} collective-permute-done((bf16[256,768]{1,0:T(8,128)(2,1)S(1)}, bf16[256,768]{1,0:T(8,128)(2,1)S(1)}, u32[]{:S(2)}, u32[]{:S(2)}) %collective-permute-start.6) | collective-permute-done | bytes 393248 | tf_op jit(solution)/shard_map/ppermute | solution.py:24
  62.9 10.6 %qkv.6 = (bf16[256,768]{1,0:T(8,128)(2,1)}, bf16[256,1536]{1,0:T(8,128)(2,1)}) custom-call(s32[4]{0:T(128)} %and_select_fusion.order_ref, f32[2,128]{1,0:T(2,128)} %gain_ref.11, bf16[256,768]{1,0:T(8,128)(2,1)} %copy-done.28, bf16[256,768]{1,0:T(8,128)(2,1)} %copy-done.46, bf16[256,768]{1,0:T(8,128)(2,1)} %copy-done.49, bf16[256,768]{1,0:T(8,128)(2,1)} %copy-done.52, ...), custom_call_target="tpu_custom_call" | custom-call | flops 1000 | bytes 1000 | tf_op jit(solution)/shard_map/qkv/pallas_call | solution.py:69
  75.8 13.2 %collective-permute-done.8.refs_3_ = bf16[256,768]{1,0:T(8,128)(2,1)S(1)} collective-permute-done((bf16[256,768]{1,0:T(8,128)(2,1)S(1)}, bf16[256,768]{1,0:T(8,128)(2,1)S(1)}, u32[]{:S(2)}, u32[]{:S(2)}) %collective-permute-start.8) | collective-permute-done | bytes 393248 | tf_op jit(solution)/shard_map/ppermute | solution.py:24
  89.0 5.9 collective-permute-done.9.refs_1_
  94.9 3.5 collective-permute-start.13
  98.4 10.6 %qkv.7 = (bf16[256,768]{1,0:T(8,128)(2,1)}, bf16[256,1536]{1,0:T(8,128)(2,1)}) custom-call(s32[4]{0:T(128)} %and_select_fusion.order_ref, f32[2,128]{1,0:T(2,128)} %gain_ref.11, bf16[256,768]{1,0:T(8,128)(2,1)} %copy-done.27, bf16[256,768]{1,0:T(8,128)(2,1)} %copy-done.42, bf16[256,768]{1,0:T(8,128)(2,1)} %copy-done.45, bf16[256,768]{1,0:T(8,128)(2,1)} %copy-done.50, ...), custom_call_target="tpu_custom_call" | custom-call | flops 1000 | bytes 1000 | tf_op jit(solution)/shard_map/qkv/pallas_call | solution.py:69
  109.4 9.8 %collective-permute-done.12.refs_3_ = bf16[256,768]{1,0:T(8,128)(2,1)S(1)} collective-permute-done((bf16[256,768]{1,0:T(8,128)(2,1)S(1)}, bf16[256,768]{1,0:T(8,128)(2,1)S(1)}, u32[]{:S(2)}, u32[]{:S(2)}) %collective-permute-start.12) | collective-permute-done | bytes 393248 | tf_op jit(solution)/shard_map/ppermute | solution.py:24
  124.3 10.6 %qkv.8 = (bf16[256,768]{1,0:T(8,128)(2,1)}, bf16[256,1536]{1,0:T(8,128)(2,1)}) custom-call(s32[4]{0:T(128)} %and_select_fusion.order_ref, f32[2,128]{1,0:T(2,128)} %gain_ref.11, bf16[256,768]{1,0:T(8,128)(2,1)} %copy-done.26, bf16[256,768]{1,0:T(8,128)(2,1)} %copy-done.41, bf16[256,768]{1,0:T(8,128)(2,1)} %copy-done.44, bf16[256,768]{1,0:T(8,128)(2,1)} %copy-done.48, ...), custom_call_target="tpu_custom_call" | custom-call | flops 1000 | bytes 1000 | tf_op jit(solution)/shard_map/qkv/pallas_call | solution.py:69
  134.9 6.4 %collective-permute-done.14.refs_11_.refs_22_ = bf16[256,1536]{1,0:T(8,128)(2,1)} collective-permute-done((bf16[256,1536]{1,0:T(8,128)(2,1)}, bf16[256,1536]{1,0:T(8,128)(2,1)}, u32[]{:S(2)}, u32[]{:S(2)}) %collective-permute-start.14) | collective-permute-done | bytes 786464 | tf_op jit(solution)/shard_map/ppermute | solution.py:24
  146.5 19.1 %attend.6.refs_15_ = f32[6,768,256]{2,1,0:T(8,128)} custom-call(s32[11]{0:T(128)} %stack.126.usable_ref, bf16[256,768]{1,0:T(8,128)(2,1)} %get-tuple-element.82.refs_0_, bf16[256,768]{1,0:T(8,128)(2,1)} %get-tuple-element.90.refs_1_, bf16[256,768]{1,0:T(8,128)(2,1)} %get-tuple-element.97.refs_2_, bf16[256,1536]{1,0:T(8,128)(2,1)} %get-tuple-element.98.refs_3_.refs_14_, ...), custom_call_target="tpu_custom_call" | custom-call | flops 1000 | bytes 1000 | tf_op jit(solution)/shard_map/attend/pallas_call | solution.py:140
  165.6 3.2 pad_maximum_fusion.1
  170.3 5.1 collective-permute-start.22
  177.5 12.9 %attend.7.refs_11_ = f32[6,768,256]{2,1,0:T(8,128)} custom-call(s32[6]{0:T(128)} %stack.123.usable_ref, bf16[256,768]{1,0:T(8,128)(2,1)} %get-tuple-element.82.refs_0_, bf16[256,768]{1,0:T(8,128)(2,1)} %get-tuple-element.90.refs_1_, bf16[256,768]{1,0:T(8,128)(2,1)} %get-tuple-element.97.refs_2_, bf16[256,1536]{1,0:T(8,128)(2,1)} %collective-permute-done.18.refs_3_.refs_9_, ...), custom_call_target="tpu_custom_call" | custom-call | flops 1000 | bytes 1000 | tf_op jit(solution)/shard_map/attend/pallas_call | solution.py:140
  190.4 3.2 collective-permute-done.22.refs_3_.refs_7_
  193.5 3.2 pad_maximum_fusion.2
  196.8 9.3 %collective-permute-start.23 = (bf16[768,1536]{1,0:T(8,128)(2,1)}, bf16[768,1536]{1,0:T(8,128)(2,1)S(1)}, u32[]{:S(2)}, u32[]{:S(2)}) collective-permute-start(bf16[768,1536]{1,0:T(8,128)(2,1)} %pad_maximum_fusion.2), channel_id=1, source_target_pairs={{0,4},{4,0},{8,12},{12,8},{16,20},{20,16},{24,28},{28,24},{1,5},{5... | collective-permute-start | bytes 7077896 | tf_op jit(solution)/shard_map/ppermute | solution.py:24
  207.3 3.1 collective-permute-done.23.refs_4_.refs_5_.refs_6_.refs_8_.refs_9_.refs_10_
  211.9 10.5 %attend.8.attended_ref = bf16[768,768]{1,0:T(8,128)(2,1)} custom-call(s32[4]{0:T(128)} %pad_add_fusion.usable_ref, bf16[256,768]{1,0:T(8,128)(2,1)} %get-tuple-element.82.refs_0_, bf16[256,768]{1,0:T(8,128)(2,1)} %get-tuple-element.90.refs_1_, bf16[256,768]{1,0:T(8,128)(2,1)} %get-tuple-element.97.refs_2_, bf16[256,1536]{1,0:T(8,128)(2,1)} %copy-done.7, ...), custom_call_target="tpu_custom_call" | custom-call | flops 1000 | bytes 1000 | tf_op jit(solution)/shard_map/attend/pallas_call | solution.py:140
  222.3 4.3 shares.4
  227.3 7.3 %shares.5.share_ref = bf16[3,768,768]{2,1,0:T(8,128)(2,1)} custom-call(s32[3]{0:T(128)} %slice.54.order_ref, bf16[768,768]{1,0:T(8,128)(2,1)} %attend.8.attended_ref, bf16[768,3072]{1,0:T(8,128)(2,1)} %weight_ref.7), custom_call_target="tpu_custom_call" | custom-call | flops 1000 | bytes 1000 | tf_op jit(solution)/shard_map/shares/pallas_call | solution.py:187
  234.5 5.5 collective-permute-done.24.total_ref
  242.8 14.0 %collective-permute-done.25.total_ref = bf16[256,768]{1,0:T(8,128)(2,1)S(1)} collective-permute-done((bf16[256,768]{1,0:T(8,128)(2,1)}, bf16[256,768]{1,0:T(8,128)(2,1)S(1)}, u32[]{:S(2)}, u32[]{:S(2)}) %collective-permute-start.25) | collective-permute-done | bytes 393248 | tf_op jit(solution)/shard_map/ppermute | solution.py:24
  261.3 3.9 collective-permute-done.27.total_ref
  267.9 5.7 collective-permute-done.26.total_ref
  277.3 3.6 collective-permute-start.36
  291.0 3.6 collective-permute-done.37.refs_0_
  296.6 4.1 collective-permute-done.29.total_ref
  301.4 2.8 turn.4
  312.0 5.9 collective-permute-done.40.refs_1_
  320.8 11.1 %collective-permute-start.43 = (bf16[256,768]{1,0:T(8,128)(2,1)}, bf16[256,768]{1,0:T(8,128)(2,1)S(1)}, u32[]{:S(2)}, u32[]{:S(2)}) collective-permute-start(bf16[256,768]{1,0:T(8,128)(2,1)} %normalize.4), channel_id=1, source_target_pairs={{0,4},{4,8},{8,12},{12,16},{16,20},{20,24},{24,28},{28,0},{1,5},{5... | collective-permute-start | bytes 1179656 | tf_op jit(solution)/shard_map/ppermute | solution.py:24
  335.1 8.4 %collective-permute-done.39.refs_2_ = bf16[256,768]{1,0:T(8,128)(2,1)S(1)} collective-permute-done((bf16[256,768]{1,0:T(8,128)(2,1)S(1)}, bf16[256,768]{1,0:T(8,128)(2,1)S(1)}, u32[]{:S(2)}, u32[]{:S(2)}) %collective-permute-start.39) | collective-permute-done | bytes 393248 | tf_op jit(solution)/shard_map/ppermute | solution.py:24
  344.2 7.7 %collective-permute-done.32.total_ref = bf16[256,768]{1,0:T(8,128)(2,1)S(1)} collective-permute-done((bf16[256,768]{1,0:T(8,128)(2,1)}, bf16[256,768]{1,0:T(8,128)(2,1)S(1)}, u32[]{:S(2)}, u32[]{:S(2)}) %collective-permute-start.32) | collective-permute-done | bytes 393248 | tf_op jit(solution)/shard_map/ppermute | solution.py:24
  355.7 3.6 collective-permute-start.49
  360.4 8.6 %collective-permute-done.45.refs_1_ = bf16[256,768]{1,0:T(8,128)(2,1)S(1)} collective-permute-done((bf16[256,768]{1,0:T(8,128)(2,1)S(1)}, bf16[256,768]{1,0:T(8,128)(2,1)S(1)}, u32[]{:S(2)}, u32[]{:S(2)}) %collective-permute-start.45) | collective-permute-done | bytes 393248 | tf_op jit(solution)/shard_map/ppermute | solution.py:24
  374.6 10.6 %qkv.9 = (bf16[256,768]{1,0:T(8,128)(2,1)}, bf16[256,1536]{1,0:T(8,128)(2,1)}) custom-call(s32[4]{0:T(128)} %and_select_fusion.order_ref, f32[2,128]{1,0:T(2,128)} %gain_ref.11, bf16[256,768]{1,0:T(8,128)(2,1)} %copy-done.32, bf16[256,768]{1,0:T(8,128)(2,1)} %copy-done.33, bf16[256,768]{1,0:T(8,128)(2,1)} %copy-done.37, bf16[256,768]{1,0:T(8,128)(2,1)} %copy-done.39, ...), custom_call_target="tpu_custom_call" | custom-call | flops 1000 | bytes 1000 | tf_op jit(solution)/shard_map/qkv/pallas_call | solution.py:69
  385.2 2.9 collective-permute-start.53
  389.3 12.7 %collective-permute-done.51.refs_3_ = bf16[256,768]{1,0:T(8,128)(2,1)S(1)} collective-permute-done((bf16[256,768]{1,0:T(8,128)(2,1)S(1)}, bf16[256,768]{1,0:T(8,128)(2,1)S(1)}, u32[]{:S(2)}, u32[]{:S(2)}) %collective-permute-start.51) | collective-permute-done | bytes 393248 | tf_op jit(solution)/shard_map/ppermute | solution.py:24
  402.0 7.6 %collective-permute-done.52.refs_1_ = bf16[256,768]{1,0:T(8,128)(2,1)S(1)} collective-permute-done((bf16[256,768]{1,0:T(8,128)(2,1)S(1)}, bf16[256,768]{1,0:T(8,128)(2,1)S(1)}, u32[]{:S(2)}, u32[]{:S(2)}) %collective-permute-start.52) | collective-permute-done | bytes 393248 | tf_op jit(solution)/shard_map/ppermute | solution.py:24
  409.6 3.7 collective-permute-start.56
  413.3 10.6 %qkv.10 = (bf16[256,768]{1,0:T(8,128)(2,1)}, bf16[256,1536]{1,0:T(8,128)(2,1)}) custom-call(s32[4]{0:T(128)} %and_select_fusion.order_ref, f32[2,128]{1,0:T(2,128)} %gain_ref.11, bf16[256,768]{1,0:T(8,128)(2,1)} %copy-done.34, bf16[256,768]{1,0:T(8,128)(2,1)} %copy-done.35, bf16[256,768]{1,0:T(8,128)(2,1)} %copy-done.38, bf16[256,768]{1,0:T(8,128)(2,1)} %copy-done.51, ...), custom_call_target="tpu_custom_call" | custom-call | flops 1000 | bytes 1000 | tf_op jit(solution)/shard_map/qkv/pallas_call | solution.py:69
  424.1 11.8 %collective-permute-done.55.refs_3_ = bf16[256,768]{1,0:T(8,128)(2,1)S(1)} collective-permute-done((bf16[256,768]{1,0:T(8,128)(2,1)S(1)}, bf16[256,768]{1,0:T(8,128)(2,1)S(1)}, u32[]{:S(2)}, u32[]{:S(2)}) %collective-permute-start.55) | collective-permute-done | bytes 393248 | tf_op jit(solution)/shard_map/ppermute | solution.py:24
  439.1 10.7 %qkv.11 = (bf16[256,768]{1,0:T(8,128)(2,1)}, bf16[256,1536]{1,0:T(8,128)(2,1)}) custom-call(s32[4]{0:T(128)} %and_select_fusion.order_ref, f32[2,128]{1,0:T(2,128)} %gain_ref.11, bf16[256,768]{1,0:T(8,128)(2,1)} %copy-done.36, bf16[256,768]{1,0:T(8,128)(2,1)} %copy-done.40, bf16[256,768]{1,0:T(8,128)(2,1)} %copy-done.43, bf16[256,768]{1,0:T(8,128)(2,1)} %copy-done.47, ...), custom_call_target="tpu_custom_call" | custom-call | flops 1000 | bytes 1000 | tf_op jit(solution)/shard_map/qkv/pallas_call | solution.py:69
  449.8 7.7 %collective-permute-done.57.refs_11_.refs_22_ = bf16[256,1536]{1,0:T(8,128)(2,1)S(1)} collective-permute-done((bf16[256,1536]{1,0:T(8,128)(2,1)S(1)}, bf16[256,1536]{1,0:T(8,128)(2,1)S(1)}, u32[]{:S(2)}, u32[]{:S(2)}) %collective-permute-start.57) | collective-permute-done | bytes 786464 | tf_op jit(solution)/shard_map/ppermute | solution.py:24
  461.5 19.3 %attend.9.refs_15_ = f32[6,768,256]{2,1,0:T(8,128)} custom-call(s32[11]{0:T(128)} %stack.126.usable_ref, bf16[256,768]{1,0:T(8,128)(2,1)} %get-tuple-element.119.refs_0_, bf16[256,768]{1,0:T(8,128)(2,1)} %get-tuple-element.128.refs_1_, bf16[256,768]{1,0:T(8,128)(2,1)} %get-tuple-element.135.refs_2_, bf16[256,1536]{1,0:T(8,128)(2,1)} %get-tuple-element.136.refs_3_.refs_14_, ...), custom_call_target="tpu_custom_call" | custom-call | flops 1000 | bytes 1000 | tf_op jit(solution)/shard_map/attend/pallas_call | solution.py:140
  483.5 5.7 collective-permute-start.65
  491.6 12.9 %attend.10.refs_11_ = f32[6,768,256]{2,1,0:T(8,128)} custom-call(s32[6]{0:T(128)} %stack.123.usable_ref, bf16[256,768]{1,0:T(8,128)(2,1)} %get-tuple-element.119.refs_0_, bf16[256,768]{1,0:T(8,128)(2,1)} %get-tuple-element.128.refs_1_, bf16[256,768]{1,0:T(8,128)(2,1)} %get-tuple-element.135.refs_2_, bf16[256,1536]{1,0:T(8,128)(2,1)} %copy-done.20, ...), custom_call_target="tpu_custom_call" | custom-call | flops 1000 | bytes 1000 | tf_op jit(solution)/shard_map/attend/pallas_call | solution.py:140
  508.5 10.2 %collective-permute-start.66 = (bf16[768,1536]{1,0:T(8,128)(2,1)S(1)}, bf16[768,1536]{1,0:T(8,128)(2,1)S(1)}, u32[]{:S(2)}, u32[]{:S(2)}) collective-permute-start(bf16[768,1536]{1,0:T(8,128)(2,1)S(1)} %pad_maximum_fusion.5), channel_id=1, source_target_pairs={{0,4},{4,0},{8,12},{12,8},{16,20},{20,16},{24,28},{28,24},{1,5},{5... | collective-permute-start | bytes 7077896 | tf_op jit(solution)/shard_map/ppermute | solution.py:24
  518.8 4.2 collective-permute-done.66.refs_4_.refs_5_.refs_6_.refs_8_.refs_9_.refs_10_
  524.3 10.4 %attend.11.attended_ref = bf16[768,768]{1,0:T(8,128)(2,1)} custom-call(s32[4]{0:T(128)} %pad_add_fusion.usable_ref, bf16[256,768]{1,0:T(8,128)(2,1)} %get-tuple-element.119.refs_0_, bf16[256,768]{1,0:T(8,128)(2,1)} %get-tuple-element.128.refs_1_, bf16[256,768]{1,0:T(8,128)(2,1)} %get-tuple-element.135.refs_2_, bf16[256,1536]{1,0:T(8,128)(2,1)} %copy-done.8, ...), custom_call_target="tpu_custom_call" | custom-call | flops 1000 | bytes 1000 | tf_op jit(solution)/shard_map/attend/pallas_call | solution.py:140
  534.8 4.2 shares.6
  541.8 7.3 %shares.7.share_ref = bf16[3,768,768]{2,1,0:T(8,128)(2,1)} custom-call(s32[3]{0:T(128)} %slice.54.order_ref, bf16[768,768]{1,0:T(8,128)(2,1)} %attend.11.attended_ref, bf16[768,3072]{1,0:T(8,128)(2,1)} %weight_ref.7), custom_call_target="tpu_custom_call" | custom-call | flops 1000 | bytes 1000 | tf_op jit(solution)/shard_map/shares/pallas_call | solution.py:187
  549.1 3.9 collective-permute-done.76.total_ref
  555.6 5.7 collective-permute-done.72.total_ref
  564.1 5.7 collective-permute-done.68.total_ref
  572.5 5.7 collective-permute-done.77.total_ref
  580.9 5.7 collective-permute-done.73.total_ref
  589.3 5.7 collective-permute-done.69.total_ref
  597.7 5.7 collective-permute-done.78.total_ref
  606.3 5.6 collective-permute-done.74.total_ref
  614.7 5.0 collective-permute-done.70.total_ref
  (328 shorter events, 131.6 us)
Async XLA Ops:
  2.2 13.1 %collective-permute-start = (f32[2,768]{1,0:T(2,128)S(1)}, f32[2,768]{1,0:T(2,128)S(1)}, u32[]{:S(2)}, u32[]{:S(2)}) collective-permute-start(f32[2,768]{1,0:T(2,128)S(1)} %pad_maximum_fusion.7), channel_id=1, source_target_pairs={{0,1},{1,2},{2,3},{3,0},{4,5},{5,6},{6,7},{7,4},{8,9},{9,10},{10,1... | collective-permute-start | bytes 18440 | tf_op jit(solution)/shard_map/ppermute | solution.py:24
  15.9 13.5 %collective-permute-start.3 = (bf16[256,768]{1,0:T(8,128)(2,1)S(1)}, bf16[256,768]{1,0:T(8,128)(2,1)S(1)}, u32[]{:S(2)}, u32[]{:S(2)}) collective-permute-start(bf16[256,768]{1,0:T(8,128)(2,1)S(1)} %get-tuple-element.161.refs_0_), channel_id=1, source_target_pairs={{0,1},{1,2},{2,3},{3,0},{4,5},{5,6},{6,7},{7,4},{8,9},{9,10},{10,1... | collective-permute-start | bytes 1179656 | tf_op jit(solution)/shard_map/ppermute | solution.py:24
  29.4 12.7 %collective-permute-start.4 = (bf16[256,768]{1,0:T(8,128)(2,1)S(1)}, bf16[256,768]{1,0:T(8,128)(2,1)S(1)}, u32[]{:S(2)}, u32[]{:S(2)}) collective-permute-start(bf16[256,768]{1,0:T(8,128)(2,1)S(1)} %collective-permute-done.3.refs_1_), channel_id=1, source_target_pairs={{0,1},{1,2},{2,3},{3,0},{4,5},{5,6},{6,7},{7,4},{8,9},{9,10},{10,1... | collective-permute-start | bytes 1179656 | tf_op jit(solution)/shard_map/ppermute | solution.py:24
  42.0 13.8 %collective-permute-start.5 = (bf16[256,768]{1,0:T(8,128)(2,1)S(1)}, bf16[256,768]{1,0:T(8,128)(2,1)S(1)}, u32[]{:S(2)}, u32[]{:S(2)}) collective-permute-start(bf16[256,768]{1,0:T(8,128)(2,1)S(1)} %collective-permute-done.4.refs_2_), channel_id=1, source_target_pairs={{0,1},{1,2},{2,3},{3,0},{4,5},{5,6},{6,7},{7,4},{8,9},{9,10},{10,1... | collective-permute-start | bytes 1179656 | tf_op jit(solution)/shard_map/ppermute | solution.py:24
  42.0 20.2 %collective-permute-start.6 = (bf16[256,768]{1,0:T(8,128)(2,1)S(1)}, bf16[256,768]{1,0:T(8,128)(2,1)S(1)}, u32[]{:S(2)}, u32[]{:S(2)}) collective-permute-start(bf16[256,768]{1,0:T(8,128)(2,1)S(1)} %get-tuple-element.80.refs_0_), channel_id=1, source_target_pairs={{0,1},{1,2},{2,3},{3,0},{4,5},{5,6},{6,7},{7,4},{8,9},{9,10},{10,1... | collective-permute-start | bytes 1179656 | tf_op jit(solution)/shard_map/ppermute | solution.py:24
  62.3 12.9 %collective-permute-start.7 = (bf16[256,768]{1,0:T(8,128)(2,1)S(1)}, bf16[256,768]{1,0:T(8,128)(2,1)S(1)}, u32[]{:S(2)}, u32[]{:S(2)}) collective-permute-start(bf16[256,768]{1,0:T(8,128)(2,1)S(1)} %collective-permute-done.6.refs_1_), channel_id=1, source_target_pairs={{0,1},{1,2},{2,3},{3,0},{4,5},{5,6},{6,7},{7,4},{8,9},{9,10},{10,1... | collective-permute-start | bytes 1179656 | tf_op jit(solution)/shard_map/ppermute | solution.py:24
  73.6 21.3 %collective-permute-start.10 = (bf16[256,1536]{1,0:T(8,128)(2,1)}, bf16[256,1536]{1,0:T(8,128)(2,1)S(1)}, u32[]{:S(2)}, u32[]{:S(2)}) collective-permute-start(bf16[256,1536]{1,0:T(8,128)(2,1)} %get-tuple-element.98.refs_3_.refs_14_), channel_id=1, source_target_pairs={{0,8},{4,12},{8,0},{12,4},{16,24},{20,28},{24,16},{28,20},{1,9},{5... | collective-permute-start | bytes 2359304 | tf_op jit(solution)/shard_map/ppermute | solution.py:24
  75.1 13.9 %collective-permute-start.8 = (bf16[256,768]{1,0:T(8,128)(2,1)S(1)}, bf16[256,768]{1,0:T(8,128)(2,1)S(1)}, u32[]{:S(2)}, u32[]{:S(2)}) collective-permute-start(bf16[256,768]{1,0:T(8,128)(2,1)S(1)} %collective-permute-done.7.refs_2_), channel_id=1, source_target_pairs={{0,1},{1,2},{2,3},{3,0},{4,5},{5,6},{6,7},{7,4},{8,9},{9,10},{10,1... | collective-permute-start | bytes 1179656 | tf_op jit(solution)/shard_map/ppermute | solution.py:24
  75.2 19.7 %collective-permute-start.9 = (bf16[256,768]{1,0:T(8,128)(2,1)S(1)}, bf16[256,768]{1,0:T(8,128)(2,1)S(1)}, u32[]{:S(2)}, u32[]{:S(2)}) collective-permute-start(bf16[256,768]{1,0:T(8,128)(2,1)S(1)} %get-tuple-element.87.refs_0_), channel_id=1, source_target_pairs={{0,1},{1,2},{2,3},{3,0},{4,5},{5,6},{6,7},{7,4},{8,9},{9,10},{10,1... | collective-permute-start | bytes 1179656 | tf_op jit(solution)/shard_map/ppermute | solution.py:24
  94.9 14.1 %collective-permute-start.11 = (bf16[256,768]{1,0:T(8,128)(2,1)S(1)}, bf16[256,768]{1,0:T(8,128)(2,1)S(1)}, u32[]{:S(2)}, u32[]{:S(2)}) collective-permute-start(bf16[256,768]{1,0:T(8,128)(2,1)S(1)} %collective-permute-done.9.refs_1_), channel_id=1, source_target_pairs={{0,1},{1,2},{2,3},{3,0},{4,5},{5,6},{6,7},{7,4},{8,9},{9,10},{10,1... | collective-permute-start | bytes 1179656 | tf_op jit(solution)/shard_map/ppermute | solution.py:24
  94.9 24.3 %collective-permute-start.13 = (bf16[256,1536]{1,0:T(8,128)(2,1)S(1)}, bf16[256,1536]{1,0:T(8,128)(2,1)S(1)}, u32[]{:S(2)}, u32[]{:S(2)}) collective-permute-start(bf16[256,1536]{1,0:T(8,128)(2,1)S(1)} %collective-permute-done.10.refs_5_.refs_16_), channel_id=1, source_target_pairs={{0,16},{4,20},{24,8},{28,12},{1,17},{5,21},{25,9},{29,13},{2,18},{... | collective-permute-start | bytes 2359304 | tf_op jit(solution)/shard_map/ppermute | solution.py:24
  121.1 24.0 %collective-permute-start.15 = (bf16[768,1536]{1,0:T(8,128)(2,1)}, bf16[768,1536]{1,0:T(8,128)(2,1)S(1)}, u32[]{:S(2)}, u32[]{:S(2)}) collective-permute-start(bf16[768,1536]{1,0:T(8,128)(2,1)} %pad_maximum_fusion), channel_id=1, source_target_pairs={{0,4},{4,0},{8,12},{12,8},{16,20},{20,16},{24,28},{28,24},{1,5},{5... | collective-permute-start | bytes 7077896 | tf_op jit(solution)/shard_map/ppermute | solution.py:24
  121.1 20.3 %collective-permute-start.14 = (bf16[256,1536]{1,0:T(8,128)(2,1)}, bf16[256,1536]{1,0:T(8,128)(2,1)}, u32[]{:S(2)}, u32[]{:S(2)}) collective-permute-start(bf16[256,1536]{1,0:T(8,128)(2,1)} %get-tuple-element.100.refs_10_.refs_21_), channel_id=1, source_target_pairs={{0,8},{4,12},{8,0},{12,4},{16,24},{20,28},{24,16},{28,20},{1,9},{5... | collective-permute-start | bytes 2359304 | tf_op jit(solution)/shard_map/ppermute | solution.py:24
  121.1 23.9 %collective-permute-start.16 = (bf16[256,1536]{1,0:T(8,128)(2,1)S(1)}, bf16[256,1536]{1,0:T(8,128)(2,1)}, u32[]{:S(2)}, u32[]{:S(2)}) collective-permute-start(bf16[256,1536]{1,0:T(8,128)(2,1)S(1)} %copy-done.9), channel_id=1, source_target_pairs={{4,16},{12,24},{16,4},{24,12},{5,17},{13,25},{17,5},{25,13},{6,18}... | collective-permute-start | bytes 2359304 | tf_op jit(solution)/shard_map/ppermute | solution.py:24
  122.7 22.3 %collective-permute-start.17 = (bf16[256,1536]{1,0:T(8,128)(2,1)}, bf16[256,1536]{1,0:T(8,128)(2,1)}, u32[]{:S(2)}, u32[]{:S(2)}) collective-permute-start(bf16[256,1536]{1,0:T(8,128)(2,1)} %get-tuple-element.100.refs_10_.refs_21_), channel_id=1, source_target_pairs={{4,16},{12,24},{16,4},{24,12},{5,17},{13,25},{17,5},{25,13},{6,18}... | collective-permute-start | bytes 2359304 | tf_op jit(solution)/shard_map/ppermute | solution.py:24
  141.3 24.2 %collective-permute-start.18 = (bf16[256,1536]{1,0:T(8,128)(2,1)}, bf16[256,1536]{1,0:T(8,128)(2,1)}, u32[]{:S(2)}, u32[]{:S(2)}) collective-permute-start(bf16[256,1536]{1,0:T(8,128)(2,1)} %collective-permute-done.14.refs_11_.refs_22_), channel_id=1, source_target_pairs={{0,16},{4,20},{24,8},{28,12},{1,17},{5,21},{25,9},{29,13},{2,18},{... | collective-permute-start | bytes 2359304 | tf_op jit(solution)/shard_map/ppermute | solution.py:24
  143.8 21.8 %collective-permute-start.19 = (bf16[256,1536]{1,0:T(8,128)(2,1)}, bf16[256,1536]{1,0:T(8,128)(2,1)}, u32[]{:S(2)}, u32[]{:S(2)}) collective-permute-start(bf16[256,1536]{1,0:T(8,128)(2,1)} %get-tuple-element.102.refs_13_.refs_24_), channel_id=1, source_target_pairs={{0,8},{4,12},{8,0},{12,4},{16,24},{20,28},{24,16},{28,20},{1,9},{5... | collective-permute-start | bytes 2359304 | tf_op jit(solution)/shard_map/ppermute | solution.py:24
  170.3 23.2 %collective-permute-start.22 = (bf16[256,1536]{1,0:T(8,128)(2,1)}, bf16[256,1536]{1,0:T(8,128)(2,1)S(1)}, u32[]{:S(2)}, u32[]{:S(2)}) collective-permute-start(bf16[256,1536]{1,0:T(8,128)(2,1)} %collective-permute-done.19.refs_4_.refs_10_), channel_id=1, source_target_pairs={{0,16},{4,20},{24,8},{28,12},{1,17},{5,21},{25,9},{29,13},{2,18},{... | collective-permute-start | bytes 2359304 | tf_op jit(solution)/shard_map/ppermute | solution.py:24
  196.8 13.7 %collective-permute-start.23 = (bf16[768,1536]{1,0:T(8,128)(2,1)}, bf16[768,1536]{1,0:T(8,128)(2,1)S(1)}, u32[]{:S(2)}, u32[]{:S(2)}) collective-permute-start(bf16[768,1536]{1,0:T(8,128)(2,1)} %pad_maximum_fusion.2), channel_id=1, source_target_pairs={{0,4},{4,0},{8,12},{12,8},{16,20},{20,16},{24,28},{28,24},{1,5},{5... | collective-permute-start | bytes 7077896 | tf_op jit(solution)/shard_map/ppermute | solution.py:24
  226.6 13.4 %collective-permute-start.24 = (bf16[256,768]{1,0:T(8,128)(2,1)}, bf16[256,768]{1,0:T(8,128)(2,1)S(1)}, u32[]{:S(2)}, u32[]{:S(2)}) collective-permute-start(bf16[256,768]{1,0:T(8,128)(2,1)} %get-tuple-element.108), channel_id=1, source_target_pairs={{0,1},{1,2},{2,3},{3,0},{4,5},{5,6},{6,7},{7,4},{8,9},{9,10},{10,1... | collective-permute-start | bytes 1179656 | tf_op jit(solution)/shard_map/ppermute | solution.py:24
  242.7 14.1 %collective-permute-start.25 = (bf16[256,768]{1,0:T(8,128)(2,1)}, bf16[256,768]{1,0:T(8,128)(2,1)S(1)}, u32[]{:S(2)}, u32[]{:S(2)}) collective-permute-start(bf16[256,768]{1,0:T(8,128)(2,1)} %add_share.15), channel_id=1, source_target_pairs={{0,1},{1,2},{2,3},{3,0},{4,5},{5,6},{6,7},{7,4},{8,9},{9,10},{10,1... | collective-permute-start | bytes 1179656 | tf_op jit(solution)/shard_map/ppermute | solution.py:24
  242.7 22.5 %collective-permute-start.27 = (bf16[256,768]{1,0:T(8,128)(2,1)S(1)}, bf16[256,768]{1,0:T(8,128)(2,1)S(1)}, u32[]{:S(2)}, u32[]{:S(2)}) collective-permute-start(bf16[256,768]{1,0:T(8,128)(2,1)S(1)} %copy-done.83), channel_id=1, source_target_pairs={{0,1},{1,2},{2,3},{3,0},{4,5},{5,6},{6,7},{7,4},{8,9},{9,10},{10,1... | collective-permute-start | bytes 1179656 | tf_op jit(solution)/shard_map/ppermute | solution.py:24
  259.5 14.1 %collective-permute-start.26 = (bf16[256,768]{1,0:T(8,128)(2,1)}, bf16[256,768]{1,0:T(8,128)(2,1)S(1)}, u32[]{:S(2)}, u32[]{:S(2)}) collective-permute-start(bf16[256,768]{1,0:T(8,128)(2,1)} %add_share.16), channel_id=1, source_target_pairs={{0,1},{1,2},{2,3},{3,0},{4,5},{5,6},{6,7},{7,4},{8,9},{9,10},{10,1... | collective-permute-start | bytes 1179656 | tf_op jit(solution)/shard_map/ppermute | solution.py:24
  267.9 18.4 %collective-permute-start.28 = (bf16[256,768]{1,0:T(8,128)(2,1)}, bf16[256,768]{1,0:T(8,128)(2,1)S(1)}, u32[]{:S(2)}, u32[]{:S(2)}) collective-permute-start(bf16[256,768]{1,0:T(8,128)(2,1)} %add_share.17), channel_id=1, source_target_pairs={{0,1},{1,2},{2,3},{3,0},{4,5},{5,6},{6,7},{7,4},{8,9},{9,10},{10,1... | collective-permute-start | bytes 1179656 | tf_op jit(solution)/shard_map/ppermute | solution.py:24
  291.0 18.1 %collective-permute-start.30 = (bf16[256,768]{1,0:T(8,128)(2,1)S(1)}, bf16[256,768]{1,0:T(8,128)(2,1)S(1)}, u32[]{:S(2)}, u32[]{:S(2)}) collective-permute-start(bf16[256,768]{1,0:T(8,128)(2,1)S(1)} %copy-done.82), channel_id=1, source_target_pairs={{0,1},{1,2},{2,3},{3,0},{4,5},{5,6},{6,7},{7,4},{8,9},{9,10},{10,1... | collective-permute-start | bytes 1179656 | tf_op jit(solution)/shard_map/ppermute | solution.py:24
  294.6 37.4 %collective-permute-start.38 = (bf16[256,768]{1,0:T(8,128)(2,1)S(1)}, bf16[256,768]{1,0:T(8,128)(2,1)S(1)}, u32[]{:S(2)}, u32[]{:S(2)}) collective-permute-start(bf16[256,768]{1,0:T(8,128)(2,1)S(1)} %collective-permute-done.37.refs_0_), channel_id=1, source_target_pairs={{0,1},{1,2},{2,3},{3,0},{4,5},{5,6},{6,7},{7,4},{8,9},{9,10},{10,1... | collective-permute-start | bytes 1179656 | tf_op jit(solution)/shard_map/ppermute | solution.py:24
  304.2 13.7 %collective-permute-start.40 = (f32[8,256]{1,0:T(8,128)}, f32[8,256]{1,0:T(8,128)S(1)}, u32[]{:S(2)}, u32[]{:S(2)}) collective-permute-start(f32[8,256]{1,0:T(8,128)} %get-tuple-element.115.refs_0_), channel_id=1, source_target_pairs={{0,1},{1,2},{2,3},{3,0},{4,5},{5,6},{6,7},{7,4},{8,9},{9,10},{10,1... | collective-permute-start | bytes 24584 | tf_op jit(solution)/shard_map/ppermute | solution.py:24
  304.4 13.5 %collective-permute-start.41 = (f32[8,256]{1,0:T(8,128)}, f32[8,256]{1,0:T(8,128)S(1)}, u32[]{:S(2)}, u32[]{:S(2)}) collective-permute-start(f32[8,256]{1,0:T(8,128)} %get-tuple-element.115.refs_0_), channel_id=1, source_target_pairs={{0,2},{1,3},{2,0},{3,1},{4,6},{5,7},{6,4},{7,5},{8,10},{9,11},{10,... | collective-permute-start | bytes 24584 | tf_op jit(solution)/shard_map/ppermute | solution.py:24
  311.8 20.5 %collective-permute-start.31 = (bf16[256,768]{1,0:T(8,128)(2,1)}, bf16[256,768]{1,0:T(8,128)(2,1)S(1)}, u32[]{:S(2)}, u32[]{:S(2)}) collective-permute-start(bf16[256,768]{1,0:T(8,128)(2,1)} %add_share.19), channel_id=1, source_target_pairs={{0,1},{1,2},{2,3},{3,0},{4,5},{5,6},{6,7},{7,4},{8,9},{9,10},{10,1... | collective-permute-start | bytes 1179656 | tf_op jit(solution)/shard_map/ppermute | solution.py:24
  320.8 14.2 %collective-permute-start.43 = (bf16[256,768]{1,0:T(8,128)(2,1)}, bf16[256,768]{1,0:T(8,128)(2,1)S(1)}, u32[]{:S(2)}, u32[]{:S(2)}) collective-permute-start(bf16[256,768]{1,0:T(8,128)(2,1)} %normalize.4), channel_id=1, source_target_pairs={{0,4},{4,8},{8,12},{12,16},{16,20},{20,24},{24,28},{28,0},{1,5},{5... | collective-permute-start | bytes 1179656 | tf_op jit(solution)/shard_map/ppermute | solution.py:24
  335.0 16.9 %collective-permute-start.32 = (bf16[256,768]{1,0:T(8,128)(2,1)}, bf16[256,768]{1,0:T(8,128)(2,1)S(1)}, u32[]{:S(2)}, u32[]{:S(2)}) collective-permute-start(bf16[256,768]{1,0:T(8,128)(2,1)} %add_share.20), channel_id=1, source_target_pairs={{0,1},{1,2},{2,3},{3,0},{4,5},{5,6},{6,7},{7,4},{8,9},{9,10},{10,1... | collective-permute-start | bytes 1179656 | tf_op jit(solution)/shard_map/ppermute | solution.py:24
  343.5 16.9 %collective-permute-start.44 = (bf16[256,768]{1,0:T(8,128)(2,1)S(1)}, bf16[256,768]{1,0:T(8,128)(2,1)S(1)}, u32[]{:S(2)}, u32[]{:S(2)}) collective-permute-start(bf16[256,768]{1,0:T(8,128)(2,1)S(1)} %collective-permute-done.39.refs_2_), channel_id=1, source_target_pairs={{0,1},{1,2},{2,3},{3,0},{4,5},{5,6},{6,7},{7,4},{8,9},{9,10},{10,1... | collective-permute-start | bytes 1179656 | tf_op jit(solution)/shard_map/ppermute | solution.py:24
  344.2 24.8 %collective-permute-start.45 = (bf16[256,768]{1,0:T(8,128)(2,1)S(1)}, bf16[256,768]{1,0:T(8,128)(2,1)S(1)}, u32[]{:S(2)}, u32[]{:S(2)}) collective-permute-start(bf16[256,768]{1,0:T(8,128)(2,1)S(1)} %collective-permute-done.43.refs_0_), channel_id=1, source_target_pairs={{0,1},{1,2},{2,3},{3,0},{4,5},{5,6},{6,7},{7,4},{8,9},{9,10},{10,1... | collective-permute-start | bytes 1179656 | tf_op jit(solution)/shard_map/ppermute | solution.py:24
  355.5 13.7 %collective-permute-start.47 = (f32[8,256]{1,0:T(8,128)}, f32[8,256]{1,0:T(8,128)S(1)}, u32[]{:S(2)}, u32[]{:S(2)}) collective-permute-start(f32[8,256]{1,0:T(8,128)} %get-tuple-element.123.refs_0_), channel_id=1, source_target_pairs={{0,1},{1,2},{2,3},{3,0},{4,5},{5,6},{6,7},{7,4},{8,9},{9,10},{10,1... | collective-permute-start | bytes 24584 | tf_op jit(solution)/shard_map/ppermute | solution.py:24
  355.5 13.7 %collective-permute-start.48 = (f32[8,256]{1,0:T(8,128)}, f32[8,256]{1,0:T(8,128)S(1)}, u32[]{:S(2)}, u32[]{:S(2)}) collective-permute-start(f32[8,256]{1,0:T(8,128)} %get-tuple-element.123.refs_0_), channel_id=1, source_target_pairs={{0,2},{1,3},{2,0},{3,1},{4,6},{5,7},{6,4},{7,5},{8,10},{9,11},{10,... | collective-permute-start | bytes 24584 | tf_op jit(solution)/shard_map/ppermute | solution.py:24
  355.7 13.5 %collective-permute-start.49 = (f32[8,256]{1,0:T(8,128)}, f32[8,256]{1,0:T(8,128)S(1)}, u32[]{:S(2)}, u32[]{:S(2)}) collective-permute-start(f32[8,256]{1,0:T(8,128)} %get-tuple-element.123.refs_0_), channel_id=1, source_target_pairs={{0,3},{1,0},{2,1},{3,2},{4,7},{5,4},{6,5},{7,6},{8,11},{9,8},{10,9... | collective-permute-start | bytes 24584 | tf_op jit(solution)/shard_map/ppermute | solution.py:24
  369.0 19.2 %collective-permute-start.46 = (bf16[256,768]{1,0:T(8,128)(2,1)S(1)}, bf16[256,768]{1,0:T(8,128)(2,1)S(1)}, u32[]{:S(2)}, u32[]{:S(2)}) collective-permute-start(bf16[256,768]{1,0:T(8,128)(2,1)S(1)} %collective-permute-done.45.refs_1_), channel_id=1, source_target_pairs={{0,1},{1,2},{2,3},{3,0},{4,5},{5,6},{6,7},{7,4},{8,9},{9,10},{10,1... | collective-permute-start | bytes 1179656 | tf_op jit(solution)/shard_map/ppermute | solution.py:24
  372.1 16.0 %collective-permute-start.50 = (bf16[256,768]{1,0:T(8,128)(2,1)}, bf16[256,768]{1,0:T(8,128)(2,1)S(1)}, u32[]{:S(2)}, u32[]{:S(2)}) collective-permute-start(bf16[256,768]{1,0:T(8,128)(2,1)} %normalize.5), channel_id=1, source_target_pairs={{0,4},{4,8},{8,12},{12,16},{16,20},{20,24},{24,28},{28,0},{1,5},{5... | collective-permute-start | bytes 1179656 | tf_op jit(solution)/shard_map/ppermute | solution.py:24
  385.2 24.4 %collective-permute-start.53 = (bf16[256,1536]{1,0:T(8,128)(2,1)}, bf16[256,1536]{1,0:T(8,128)(2,1)S(1)}, u32[]{:S(2)}, u32[]{:S(2)}) collective-permute-start(bf16[256,1536]{1,0:T(8,128)(2,1)} %get-tuple-element.136.refs_3_.refs_14_), channel_id=1, source_target_pairs={{0,8},{4,12},{8,0},{12,4},{16,24},{20,28},{24,16},{28,20},{1,9},{5... | collective-permute-start | bytes 2359304 | tf_op jit(solution)/shard_map/ppermute | solution.py:24
  388.2 13.8 %collective-permute-start.51 = (bf16[256,768]{1,0:T(8,128)(2,1)S(1)}, bf16[256,768]{1,0:T(8,128)(2,1)S(1)}, u32[]{:S(2)}, u32[]{:S(2)}) collective-permute-start(bf16[256,768]{1,0:T(8,128)(2,1)S(1)} %collective-permute-done.46.refs_2_), channel_id=1, source_target_pairs={{0,1},{1,2},{2,3},{3,0},{4,5},{5,6},{6,7},{7,4},{8,9},{9,10},{10,1... | collective-permute-start | bytes 1179656 | tf_op jit(solution)/shard_map/ppermute | solution.py:24
  388.9 20.7 %collective-permute-start.52 = (bf16[256,768]{1,0:T(8,128)(2,1)S(1)}, bf16[256,768]{1,0:T(8,128)(2,1)S(1)}, u32[]{:S(2)}, u32[]{:S(2)}) collective-permute-start(bf16[256,768]{1,0:T(8,128)(2,1)S(1)} %collective-permute-done.50.refs_0_), channel_id=1, source_target_pairs={{0,1},{1,2},{2,3},{3,0},{4,5},{5,6},{6,7},{7,4},{8,9},{9,10},{10,1... | collective-permute-start | bytes 1179656 | tf_op jit(solution)/shard_map/ppermute | solution.py:24
  409.6 14.4 %collective-permute-start.54 = (bf16[256,768]{1,0:T(8,128)(2,1)S(1)}, bf16[256,768]{1,0:T(8,128)(2,1)S(1)}, u32[]{:S(2)}, u32[]{:S(2)}) collective-permute-start(bf16[256,768]{1,0:T(8,128)(2,1)S(1)} %collective-permute-done.52.refs_1_), channel_id=1, source_target_pairs={{0,1},{1,2},{2,3},{3,0},{4,5},{5,6},{6,7},{7,4},{8,9},{9,10},{10,1... | collective-permute-start | bytes 1179656 | tf_op jit(solution)/shard_map/ppermute | solution.py:24
  409.6 26.2 %collective-permute-start.56 = (bf16[256,1536]{1,0:T(8,128)(2,1)S(1)}, bf16[256,1536]{1,0:T(8,128)(2,1)S(1)}, u32[]{:S(2)}, u32[]{:S(2)}) collective-permute-start(bf16[256,1536]{1,0:T(8,128)(2,1)S(1)} %collective-permute-done.53.refs_5_.refs_16_), channel_id=1, source_target_pairs={{0,16},{4,20},{24,8},{28,12},{1,17},{5,21},{25,9},{29,13},{2,18},{... | collective-permute-start | bytes 2359304 | tf_op jit(solution)/shard_map/ppermute | solution.py:24
  424.0 11.9 %collective-permute-start.55 = (bf16[256,768]{1,0:T(8,128)(2,1)S(1)}, bf16[256,768]{1,0:T(8,128)(2,1)S(1)}, u32[]{:S(2)}, u32[]{:S(2)}) collective-permute-start(bf16[256,768]{1,0:T(8,128)(2,1)S(1)} %collective-permute-done.54.refs_2_), channel_id=1, source_target_pairs={{0,1},{1,2},{2,3},{3,0},{4,5},{5,6},{6,7},{7,4},{8,9},{9,10},{10,1... | collective-permute-start | bytes 1179656 | tf_op jit(solution)/shard_map/ppermute | solution.py:24
  437.6 22.0 %collective-permute-start.58 = (bf16[768,1536]{1,0:T(8,128)(2,1)}, bf16[768,1536]{1,0:T(8,128)(2,1)S(1)}, u32[]{:S(2)}, u32[]{:S(2)}) collective-permute-start(bf16[768,1536]{1,0:T(8,128)(2,1)} %pad_maximum_fusion.3), channel_id=1, source_target_pairs={{0,4},{4,0},{8,12},{12,8},{16,20},{20,16},{24,28},{28,24},{1,5},{5... | collective-permute-start | bytes 7077896 | tf_op jit(solution)/shard_map/ppermute | solution.py:24
  437.6 20.0 %collective-permute-start.57 = (bf16[256,1536]{1,0:T(8,128)(2,1)S(1)}, bf16[256,1536]{1,0:T(8,128)(2,1)S(1)}, u32[]{:S(2)}, u32[]{:S(2)}) collective-permute-start(bf16[256,1536]{1,0:T(8,128)(2,1)S(1)} %copy-done.14), channel_id=1, source_target_pairs={{0,8},{4,12},{8,0},{12,4},{16,24},{20,28},{24,16},{28,20},{1,9},{5... | collective-permute-start | bytes 2359304 | tf_op jit(solution)/shard_map/ppermute | solution.py:24
  437.7 21.9 %collective-permute-start.59 = (bf16[256,1536]{1,0:T(8,128)(2,1)S(1)}, bf16[256,1536]{1,0:T(8,128)(2,1)S(1)}, u32[]{:S(2)}, u32[]{:S(2)}) collective-permute-start(bf16[256,1536]{1,0:T(8,128)(2,1)S(1)} %copy-done.12), channel_id=1, source_target_pairs={{4,16},{12,24},{16,4},{24,12},{5,17},{13,25},{17,5},{25,13},{6,18}... | collective-permute-start | bytes 2359304 | tf_op jit(solution)/shard_map/ppermute | solution.py:24
  438.4 21.2 %collective-permute-start.60 = (bf16[256,1536]{1,0:T(8,128)(2,1)S(1)}, bf16[256,1536]{1,0:T(8,128)(2,1)S(1)}, u32[]{:S(2)}, u32[]{:S(2)}) collective-permute-start(bf16[256,1536]{1,0:T(8,128)(2,1)S(1)} %copy-done.14), channel_id=1, source_target_pairs={{4,16},{12,24},{16,4},{24,12},{5,17},{13,25},{17,5},{25,13},{6,18}... | collective-permute-start | bytes 2359304 | tf_op jit(solution)/shard_map/ppermute | solution.py:24
  457.6 23.2 %collective-permute-start.61 = (bf16[256,1536]{1,0:T(8,128)(2,1)S(1)}, bf16[256,1536]{1,0:T(8,128)(2,1)S(1)}, u32[]{:S(2)}, u32[]{:S(2)}) collective-permute-start(bf16[256,1536]{1,0:T(8,128)(2,1)S(1)} %collective-permute-done.57.refs_11_.refs_22_), channel_id=1, source_target_pairs={{0,16},{4,20},{24,8},{28,12},{1,17},{5,21},{25,9},{29,13},{2,18},{... | collective-permute-start | bytes 2359304 | tf_op jit(solution)/shard_map/ppermute | solution.py:24
  459.5 21.3 %collective-permute-start.62 = (bf16[256,1536]{1,0:T(8,128)(2,1)}, bf16[256,1536]{1,0:T(8,128)(2,1)S(1)}, u32[]{:S(2)}, u32[]{:S(2)}) collective-permute-start(bf16[256,1536]{1,0:T(8,128)(2,1)} %get-tuple-element.140.refs_13_.refs_24_), channel_id=1, source_target_pairs={{0,8},{4,12},{8,0},{12,4},{16,24},{20,28},{24,16},{28,20},{1,9},{5... | collective-permute-start | bytes 2359304 | tf_op jit(solution)/shard_map/ppermute | solution.py:24
  483.5 23.4 %collective-permute-start.65 = (bf16[256,1536]{1,0:T(8,128)(2,1)S(1)}, bf16[256,1536]{1,0:T(8,128)(2,1)S(1)}, u32[]{:S(2)}, u32[]{:S(2)}) collective-permute-start(bf16[256,1536]{1,0:T(8,128)(2,1)S(1)} %collective-permute-done.62.refs_4_.refs_10_), channel_id=1, source_target_pairs={{0,16},{4,20},{24,8},{28,12},{1,17},{5,21},{25,9},{29,13},{2,18},{... | collective-permute-start | bytes 2359304 | tf_op jit(solution)/shard_map/ppermute | solution.py:24
  508.5 14.4 %collective-permute-start.66 = (bf16[768,1536]{1,0:T(8,128)(2,1)S(1)}, bf16[768,1536]{1,0:T(8,128)(2,1)S(1)}, u32[]{:S(2)}, u32[]{:S(2)}) collective-permute-start(bf16[768,1536]{1,0:T(8,128)(2,1)S(1)} %pad_maximum_fusion.5), channel_id=1, source_target_pairs={{0,4},{4,0},{8,12},{12,8},{16,20},{20,16},{24,28},{28,24},{1,5},{5... | collective-permute-start | bytes 7077896 | tf_op jit(solution)/shard_map/ppermute | solution.py:24
  539.0 14.0 %collective-permute-start.76 = (bf16[256,768]{1,0:T(8,128)(2,1)}, bf16[256,768]{1,0:T(8,128)(2,1)S(1)}, u32[]{:S(2)}, u32[]{:S(2)}) collective-permute-start(bf16[256,768]{1,0:T(8,128)(2,1)} %get-tuple-element.152), channel_id=1, source_target_pairs={{0,1},{1,2},{2,3},{3,0},{4,5},{5,6},{6,7},{7,4},{8,9},{9,10},{10,1... | collective-permute-start | bytes 1179656 | tf_op jit(solution)/shard_map/ppermute | solution.py:24
  539.0 22.4 %collective-permute-start.72 = (bf16[256,768]{1,0:T(8,128)(2,1)}, bf16[256,768]{1,0:T(8,128)(2,1)S(1)}, u32[]{:S(2)}, u32[]{:S(2)}) collective-permute-start(bf16[256,768]{1,0:T(8,128)(2,1)} %get-tuple-element.150), channel_id=1, source_target_pairs={{0,1},{1,2},{2,3},{3,0},{4,5},{5,6},{6,7},{7,4},{8,9},{9,10},{10,1... | collective-permute-start | bytes 1179656 | tf_op jit(solution)/shard_map/ppermute | solution.py:24
  539.1 30.7 %collective-permute-start.68 = (bf16[256,768]{1,0:T(8,128)(2,1)}, bf16[256,768]{1,0:T(8,128)(2,1)S(1)}, u32[]{:S(2)}, u32[]{:S(2)}) collective-permute-start(bf16[256,768]{1,0:T(8,128)(2,1)} %get-tuple-element.148), channel_id=1, source_target_pairs={{0,1},{1,2},{2,3},{3,0},{4,5},{5,6},{6,7},{7,4},{8,9},{9,10},{10,1... | collective-permute-start | bytes 1179656 | tf_op jit(solution)/shard_map/ppermute | solution.py:24
  555.6 22.6 %collective-permute-start.77 = (bf16[256,768]{1,0:T(8,128)(2,1)}, bf16[256,768]{1,0:T(8,128)(2,1)S(1)}, u32[]{:S(2)}, u32[]{:S(2)}) collective-permute-start(bf16[256,768]{1,0:T(8,128)(2,1)} %add_share.27), channel_id=1, source_target_pairs={{0,1},{1,2},{2,3},{3,0},{4,5},{5,6},{6,7},{7,4},{8,9},{9,10},{10,1... | collective-permute-start | bytes 1179656 | tf_op jit(solution)/shard_map/ppermute | solution.py:24
  564.0 22.6 %collective-permute-start.73 = (bf16[256,768]{1,0:T(8,128)(2,1)}, bf16[256,768]{1,0:T(8,128)(2,1)S(1)}, u32[]{:S(2)}, u32[]{:S(2)}) collective-permute-start(bf16[256,768]{1,0:T(8,128)(2,1)} %add_share.24), channel_id=1, source_target_pairs={{0,1},{1,2},{2,3},{3,0},{4,5},{5,6},{6,7},{7,4},{8,9},{9,10},{10,1... | collective-permute-start | bytes 1179656 | tf_op jit(solution)/shard_map/ppermute | solution.py:24
  564.1 58.5 %collective-permute-start.67 = (f32[256,768]{1,0:T(8,128)S(1)}, f32[256,768]{1,0:T(8,128)S(1)}, u32[]{:S(2)}, u32[]{:S(2)}) collective-permute-start(f32[256,768]{1,0:T(8,128)S(1)} %copy-done.29), channel_id=1, source_target_pairs={{0,4},{4,8},{8,12},{12,16},{16,20},{20,24},{24,28},{28,0},{1,5},{5... | collective-permute-start | bytes 2359304 | tf_op jit(solution)/shard_map/ppermute | solution.py:24
  572.5 22.6 %collective-permute-start.69 = (bf16[256,768]{1,0:T(8,128)(2,1)}, bf16[256,768]{1,0:T(8,128)(2,1)S(1)}, u32[]{:S(2)}, u32[]{:S(2)}) collective-permute-start(bf16[256,768]{1,0:T(8,128)(2,1)} %add_share.21), channel_id=1, source_target_pairs={{0,1},{1,2},{2,3},{3,0},{4,5},{5,6},{6,7},{7,4},{8,9},{9,10},{10,1... | collective-permute-start | bytes 1179656 | tf_op jit(solution)/shard_map/ppermute | solution.py:24
  580.9 22.6 %collective-permute-start.78 = (bf16[256,768]{1,0:T(8,128)(2,1)}, bf16[256,768]{1,0:T(8,128)(2,1)S(1)}, u32[]{:S(2)}, u32[]{:S(2)}) collective-permute-start(bf16[256,768]{1,0:T(8,128)(2,1)} %add_share.28), channel_id=1, source_target_pairs={{0,1},{1,2},{2,3},{3,0},{4,5},{5,6},{6,7},{7,4},{8,9},{9,10},{10,1... | collective-permute-start | bytes 1179656 | tf_op jit(solution)/shard_map/ppermute | solution.py:24
  580.9 41.7 %collective-permute-start.71 = (f32[256,768]{1,0:T(8,128)S(1)}, f32[256,768]{1,0:T(8,128)S(1)}, u32[]{:S(2)}, u32[]{:S(2)}) collective-permute-start(f32[256,768]{1,0:T(8,128)S(1)} %copy-done.30), channel_id=1, source_target_pairs={{0,4},{4,8},{8,12},{12,16},{16,20},{20,24},{24,28},{28,0},{1,5},{5... | collective-permute-start | bytes 2359304 | tf_op jit(solution)/shard_map/ppermute | solution.py:24
  586.6 36.0 %collective-permute-start.75 = (f32[256,768]{1,0:T(8,128)S(1)}, f32[256,768]{1,0:T(8,128)S(1)}, u32[]{:S(2)}, u32[]{:S(2)}) collective-permute-start(f32[256,768]{1,0:T(8,128)S(1)} %copy-done.31), channel_id=1, source_target_pairs={{0,4},{4,8},{8,12},{12,16},{16,20},{20,24},{24,28},{28,0},{1,5},{5... | collective-permute-start | bytes 2359304 | tf_op jit(solution)/shard_map/ppermute | solution.py:24
  595.0 16.9 %collective-permute-start.74 = (bf16[256,768]{1,0:T(8,128)(2,1)}, bf16[256,768]{1,0:T(8,128)(2,1)S(1)}, u32[]{:S(2)}, u32[]{:S(2)}) collective-permute-start(bf16[256,768]{1,0:T(8,128)(2,1)} %add_share.25), channel_id=1, source_target_pairs={{0,1},{1,2},{2,3},{3,0},{4,5},{5,6},{6,7},{7,4},{8,9},{9,10},{10,1... | collective-permute-start | bytes 1179656 | tf_op jit(solution)/shard_map/ppermute | solution.py:24
  603.5 16.3 %collective-permute-start.70 = (bf16[256,768]{1,0:T(8,128)(2,1)}, bf16[256,768]{1,0:T(8,128)(2,1)S(1)}, u32[]{:S(2)}, u32[]{:S(2)}) collective-permute-start(bf16[256,768]{1,0:T(8,128)(2,1)} %add_share.22), channel_id=1, source_target_pairs={{0,1},{1,2},{2,3},{3,0},{4,5},{5,6},{6,7},{7,4},{8,9},{9,10},{10,1... | collective-permute-start | bytes 1179656 | tf_op jit(solution)/shard_map/ppermute | solution.py:24
  (100 other events, 984.1 us)

commit v3 on v2

--- a/solution.py
+++ b/solution.py
@@ -89,7 +89,8 @@
     )(order, norm_gain, *inputs, *([weight] * parts))
 
 
-def attend_kernel(chunks, pieces, first, last, tile, usable_ref, *refs):
+def attend_kernel(chunks, marks, first, last, tile, usable_ref, *refs):
+    pieces = len(marks)
     queries, refs = refs[:chunks], refs[chunks:]
     keys, values = refs[:pieces], refs[pieces : 2 * pieces]
     rest = refs[2 * pieces :]
@@ -101,7 +102,7 @@
     wide = []
     for piece in range(pieces):
         value = values[piece][...]
-        usable = usable_ref[piece].astype(jnp.float32).astype(value.dtype)
+        usable = usable_ref[marks[piece]].astype(jnp.float32).astype(value.dtype)
         wide.append(jnp.concatenate([value, jnp.ones_like(value)], axis=1) * usable)
     for chunk in range(chunks):
         for start in range(0, height, tile):
@@ -121,12 +122,11 @@
                 out_ref[at, :] = total
 
 
-def attend(queries, blocks, parts, usable, running, last, head_dim):
+def attend(queries, blocks, parts, marks, usable, running, last, head_dim):
     height, columns = queries[0].shape
     chunks = len(queries)
     rows = height * chunks
     heads = columns // head_dim
-    pieces = len(blocks)
     first = running is None
     tile = TILE if height % TILE == 0 else height
 
@@ -138,7 +138,7 @@
 
     running_spec = pl.BlockSpec((None, rows, 2 * head_dim), lambda h, usable: (h, 0, 0))
     return pl.pallas_call(
-        functools.partial(attend_kernel, chunks, pieces, first, last, tile),
+        functools.partial(attend_kernel, chunks, marks, first, last, tile),
         grid_spec=pltpu.PrefetchScalarGridSpec(
             num_scalar_prefetch=1,
             grid=(heads,),
@@ -360,9 +360,8 @@
         second=jnp.where(place < 2, slot - 2, slot + 2),
         other=slot + jnp.where(place == 0, -1, jnp.where(place == 1, -3, jnp.where(place == 2, 3, 1))),
     )
-    return {
-        name: ((jnp.abs(g - slot) <= reach) & (g >= 0) & (g < frames)).astype(jnp.int32) for name, g in held.items()
-    }
+    held = jnp.stack([jnp.asarray(held[name], jnp.int32) for name in SOURCES])
+    return ((jnp.abs(held - slot) <= reach) & (held >= 0) & (held < frames)).astype(jnp.int32)
 
 
 def on_device(
@@ -453,7 +452,8 @@
                 queries,
                 [sources[i]["sibling" if name in SIBLING else name] for i, name in names],
                 [SIBLING.get(name, 0) for _, name in names],
-                jnp.stack([usable[name] for _, name in names]),
+                [SOURCES.index(name) for _, name in names],
+                usable,
                 running,
                 last,
                 head_dim,
@@ -463,7 +463,9 @@
         queries[-1], before["across"] = tie(queries[-1], before["across"])
         halo_second(before)
         running = absorb(early, None, False)
-        running, before["second"], after["across"] = tie(running, before["second"], after["across"])
+        running, before["second"], after["across"], after["third"] = tie(
+            running, before["second"], after["across"], after["third"]
+        )
         halo_second(after)
         halo_sibling(before)
         running = absorb(middle, running, False)

time: 638 us -> 615 us (0.964)
  starting transfers between devices: 97.9 us -> 77.2 us
    ppermute x79, starting transfers between devices: 97.9 us -> 77.2 us  [permute(): return lax.ppermute(block, axis, pairs)]
    unnamed x170 -> x174, local copies, waits for them, and re-layouts: 25.2 us -> 25.1 us
  transfers between devices with their start and end apart: 79 -> 79, of which waited for: 41 -> 45; matrix products, arithmetic and copies ran while one was open for 1% -> 1% of each run, Pallas kernels for 30% -> 31%
where the time goes in v3:
time: 615 us; the launch traced here: 604 us
  waiting for transfers between devices  257 us (42%)
  Pallas kernels  217 us (35%)
  starting transfers between devices  77.2 us (13%)
  local copies, waits for them, and re-layouts  27.5 us (4%)
  other arithmetic  21.8 us (4%)
    ppermute x79, waiting for transfers between devices, permute(): return lax.ppermute(block, axis, pairs)  257 us
    pallas_call x6, Pallas kernels, attend(): pl.pallas_call(functools.partial(attend_kernel, chunks, marks, first, las...  85 us
    ppermute x79, starting transfers between devices, permute(): return lax.ppermute(block, axis, pairs)  77.2 us
    pallas_call x6, Pallas kernels, project(): pl.pallas_call(functools.partial(qkv_kernel, parts, columns // head_dim,...  63.7 us
    pallas_call x15, Pallas kernels, add_share(): pl.pallas_call(add_kernel, grid=(1,), in_specs=[pl.BlockSpec((rows, colum...  29.8 us
    unnamed x174, local copies, waits for them, and re-layouts  25.1 us
    pallas_call x4, Pallas kernels, shares(): pl.pallas_call(kernel, grid_spec=pltpu.PrefetchScalarGridSpec(num_scalar_...  23 us
  transfers between devices with their start and end apart: 79, of which 45 were waited for; matrix products, arithmetic and copies ran while one was open for 1% of the time, Pallas kernels for 31%

profile of v3, /device:TPU:0, one launch (start us, length us, event | category | flops | bytes accessed | tf_op | source)
XLA Modules:
  0.0 604.5 jit_solution(4948842031511937565)
XLA Ops:
  2.2 3.1 collective-permute-start
  16.3 12.6 %collective-permute-done.3.refs_1_ = bf16[256,768]{1,0:T(8,128)(2,1)S(1)} collective-permute-done((bf16[256,768]{1,0:T(8,128)(2,1)S(1)}, bf16[256,768]{1,0:T(8,128)(2,1)S(1)}, u32[]{:S(2)}, u32[]{:S(2)}) %collective-permute-start.3) | collective-permute-done | bytes 393248 | tf_op jit(solution)/shard_map/ppermute | solution.py:24
  28.9 12.5 %collective-permute-done.4.refs_2_ = bf16[256,768]{1,0:T(8,128)(2,1)S(1)} collective-permute-done((bf16[256,768]{1,0:T(8,128)(2,1)S(1)}, bf16[256,768]{1,0:T(8,128)(2,1)S(1)}, u32[]{:S(2)}, u32[]{:S(2)}) %collective-permute-start.4) | collective-permute-done | bytes 393248 | tf_op jit(solution)/shard_map/ppermute | solution.py:24
  41.3 13.8 %collective-permute-done.5.refs_3_ = bf16[256,768]{1,0:T(8,128)(2,1)S(1)} collective-permute-done((bf16[256,768]{1,0:T(8,128)(2,1)S(1)}, bf16[256,768]{1,0:T(8,128)(2,1)S(1)}, u32[]{:S(2)}, u32[]{:S(2)}) %collective-permute-start.5) | collective-permute-done | bytes 393248 | tf_op jit(solution)/shard_map/ppermute | solution.py:24
  55.2 6.1 %collective-permute-done.6.refs_1_ = bf16[256,768]{1,0:T(8,128)(2,1)S(1)} collective-permute-done((bf16[256,768]{1,0:T(8,128)(2,1)S(1)}, bf16[256,768]{1,0:T(8,128)(2,1)S(1)}, u32[]{:S(2)}, u32[]{:S(2)}) %collective-permute-start.6) | collective-permute-done | bytes 393248 | tf_op jit(solution)/shard_map/ppermute | solution.py:24
  61.9 10.6 %qkv.6 = (bf16[256,768]{1,0:T(8,128)(2,1)}, bf16[256,1536]{1,0:T(8,128)(2,1)}) custom-call(s32[4]{0:T(128)} %and_select_fusion.order_ref, f32[2,128]{1,0:T(2,128)} %gain_ref.11, bf16[256,768]{1,0:T(8,128)(2,1)} %copy-done.30, bf16[256,768]{1,0:T(8,128)(2,1)} %copy-done.48, bf16[256,768]{1,0:T(8,128)(2,1)} %copy-done.51, bf16[256,768]{1,0:T(8,128)(2,1)} %copy-done.54, ...), custom_call_target="tpu_custom_call" | custom-call | flops 1000 | bytes 1000 | tf_op jit(solution)/shard_map/qkv/pallas_call | solution.py:69
  75.2 13.2 %collective-permute-done.8.refs_3_ = bf16[256,768]{1,0:T(8,128)(2,1)S(1)} collective-permute-done((bf16[256,768]{1,0:T(8,128)(2,1)S(1)}, bf16[256,768]{1,0:T(8,128)(2,1)S(1)}, u32[]{:S(2)}, u32[]{:S(2)}) %collective-permute-start.8) | collective-permute-done | bytes 393248 | tf_op jit(solution)/shard_map/ppermute | solution.py:24
  88.4 5.7 collective-permute-done.9.refs_1_
  94.1 3.5 collective-permute-start.13
  97.6 10.6 %qkv.7 = (bf16[256,768]{1,0:T(8,128)(2,1)}, bf16[256,1536]{1,0:T(8,128)(2,1)}) custom-call(s32[4]{0:T(128)} %and_select_fusion.order_ref, f32[2,128]{1,0:T(2,128)} %gain_ref.11, bf16[256,768]{1,0:T(8,128)(2,1)} %copy-done.29, bf16[256,768]{1,0:T(8,128)(2,1)} %copy-done.44, bf16[256,768]{1,0:T(8,128)(2,1)} %copy-done.47, bf16[256,768]{1,0:T(8,128)(2,1)} %copy-done.52, ...), custom_call_target="tpu_custom_call" | custom-call | flops 1000 | bytes 1000 | tf_op jit(solution)/shard_map/qkv/pallas_call | solution.py:69
  108.9 9.3 %collective-permute-done.12.refs_3_ = bf16[256,768]{1,0:T(8,128)(2,1)S(1)} collective-permute-done((bf16[256,768]{1,0:T(8,128)(2,1)S(1)}, bf16[256,768]{1,0:T(8,128)(2,1)S(1)}, u32[]{:S(2)}, u32[]{:S(2)}) %collective-permute-start.12) | collective-permute-done | bytes 393248 | tf_op jit(solution)/shard_map/ppermute | solution.py:24
  122.4 10.6 %qkv.8 = (bf16[256,768]{1,0:T(8,128)(2,1)}, bf16[256,1536]{1,0:T(8,128)(2,1)}) custom-call(s32[4]{0:T(128)} %and_select_fusion.order_ref, f32[2,128]{1,0:T(2,128)} %gain_ref.11, bf16[256,768]{1,0:T(8,128)(2,1)} %copy-done.28, bf16[256,768]{1,0:T(8,128)(2,1)} %copy-done.43, bf16[256,768]{1,0:T(8,128)(2,1)} %copy-done.46, bf16[256,768]{1,0:T(8,128)(2,1)} %copy-done.50, ...), custom_call_target="tpu_custom_call" | custom-call | flops 1000 | bytes 1000 | tf_op jit(solution)/shard_map/qkv/pallas_call | solution.py:69
  133.0 7.3 %collective-permute-done.14.refs_11_.refs_22_ = bf16[256,1536]{1,0:T(8,128)(2,1)} collective-permute-done((bf16[256,1536]{1,0:T(8,128)(2,1)}, bf16[256,1536]{1,0:T(8,128)(2,1)}, u32[]{:S(2)}, u32[]{:S(2)}) %collective-permute-start.14) | collective-permute-done | bytes 786464 | tf_op jit(solution)/shard_map/ppermute | solution.py:24
  147.1 19.1 %attend.6.refs_15_ = f32[6,768,256]{2,1,0:T(8,128)} custom-call(s32[7]{0:T(128)} %and_convert_fusion.usable_ref, bf16[256,768]{1,0:T(8,128)(2,1)} %get-tuple-element.84.refs_0_, bf16[256,768]{1,0:T(8,128)(2,1)} %get-tuple-element.92.refs_1_, bf16[256,768]{1,0:T(8,128)(2,1)} %get-tuple-element.99.refs_2_, ...), custom_call_target="tpu_custom_call" | custom-call | flops 1000 | bytes 1000 | tf_op jit(solution)/shard_map/attend/pallas_call | solution.py:140
  168.3 4.1 collective-permute-start.21
  177.9 12.9 %attend.7.refs_11_ = f32[6,768,256]{2,1,0:T(8,128)} custom-call(s32[7]{0:T(128)} %and_convert_fusion.usable_ref, bf16[256,768]{1,0:T(8,128)(2,1)} %get-tuple-element.84.refs_0_, bf16[256,768]{1,0:T(8,128)(2,1)} %get-tuple-element.92.refs_1_, bf16[256,768]{1,0:T(8,128)(2,1)} %get-tuple-element.99.refs_2_, ...), custom_call_target="tpu_custom_call" | custom-call | flops 1000 | bytes 1000 | tf_op jit(solution)/shard_map/attend/pallas_call | solution.py:140
  191.9 3.0 pad_maximum_fusion.2
  195.4 4.2 collective-permute-done.23.refs_4_.refs_5_.refs_6_.refs_8_.refs_9_.refs_10_
  201.0 10.4 %attend.8.attended_ref = bf16[768,768]{1,0:T(8,128)(2,1)} custom-call(s32[7]{0:T(128)} %and_convert_fusion.usable_ref, bf16[256,768]{1,0:T(8,128)(2,1)} %get-tuple-element.84.refs_0_, bf16[256,768]{1,0:T(8,128)(2,1)} %get-tuple-element.92.refs_1_, bf16[256,768]{1,0:T(8,128)(2,1)} %get-tuple-element.99.refs_2_, bf16[256,1536]{1,0:T(8,128)(2,1)} %copy-done.7, ...), custom_call_target="tpu_custom_call" | custom-call | flops 1000 | bytes 1000 | tf_op jit(solution)/shard_map/attend/pallas_call | solution.py:140
  211.5 4.3 shares.4
  216.4 7.3 %shares.5.share_ref = bf16[3,768,768]{2,1,0:T(8,128)(2,1)} custom-call(s32[3]{0:T(128)} %slice.54.order_ref, bf16[768,768]{1,0:T(8,128)(2,1)} %attend.8.attended_ref, bf16[768,3072]{1,0:T(8,128)(2,1)} %weight_ref.7), custom_call_target="tpu_custom_call" | custom-call | flops 1000 | bytes 1000 | tf_op jit(solution)/shard_map/shares/pallas_call | solution.py:187
  223.6 5.3 collective-permute-done.24.total_ref
  231.7 14.0 %collective-permute-done.25.total_ref = bf16[256,768]{1,0:T(8,128)(2,1)S(1)} collective-permute-done((bf16[256,768]{1,0:T(8,128)(2,1)}, bf16[256,768]{1,0:T(8,128)(2,1)S(1)}, u32[]{:S(2)}, u32[]{:S(2)}) %collective-permute-start.25) | collective-permute-done | bytes 393248 | tf_op jit(solution)/shard_map/ppermute | solution.py:24
  250.1 4.0 collective-permute-done.27.total_ref
  256.9 5.7 collective-permute-done.26.total_ref
  263.3 2.8 turn.3
  266.3 3.6 collective-permute-start.36
  280.0 3.5 collective-permute-done.37.refs_0_
  285.5 5.1 collective-permute-done.29.total_ref
  291.4 2.8 turn.4
  302.0 5.9 collective-permute-done.40.refs_1_
  310.9 9.8 %collective-permute-start.43 = (bf16[256,768]{1,0:T(8,128)(2,1)}, bf16[256,768]{1,0:T(8,128)(2,1)S(1)}, u32[]{:S(2)}, u32[]{:S(2)}) collective-permute-start(bf16[256,768]{1,0:T(8,128)(2,1)} %normalize.4), channel_id=1, source_target_pairs={{0,4},{4,8},{8,12},{12,16},{16,20},{20,24},{24,28},{28,0},{1,5},{5... | collective-permute-start | bytes 1179656 | tf_op jit(solution)/shard_map/ppermute | solution.py:24
  324.3 2.9 collective-permute-done.43.refs_0_
  327.2 7.3 %collective-permute-done.39.refs_2_ = bf16[256,768]{1,0:T(8,128)(2,1)S(1)} collective-permute-done((bf16[256,768]{1,0:T(8,128)(2,1)S(1)}, bf16[256,768]{1,0:T(8,128)(2,1)S(1)}, u32[]{:S(2)}, u32[]{:S(2)}) %collective-permute-start.39) | collective-permute-done | bytes 393248 | tf_op jit(solution)/shard_map/ppermute | solution.py:24
  334.5 8.4 %collective-permute-done.32.total_ref = bf16[256,768]{1,0:T(8,128)(2,1)S(1)} collective-permute-done((bf16[256,768]{1,0:T(8,128)(2,1)}, bf16[256,768]{1,0:T(8,128)(2,1)S(1)}, u32[]{:S(2)}, u32[]{:S(2)}) %collective-permute-start.32) | collective-permute-done | bytes 393248 | tf_op jit(solution)/shard_map/ppermute | solution.py:24
  343.6 2.7 turn.5
  346.6 3.6 collective-permute-start.49
  351.5 7.7 %collective-permute-done.45.refs_1_ = bf16[256,768]{1,0:T(8,128)(2,1)S(1)} collective-permute-done((bf16[256,768]{1,0:T(8,128)(2,1)S(1)}, bf16[256,768]{1,0:T(8,128)(2,1)S(1)}, u32[]{:S(2)}, u32[]{:S(2)}) %collective-permute-start.45) | collective-permute-done | bytes 393248 | tf_op jit(solution)/shard_map/ppermute | solution.py:24
  362.4 10.6 %qkv.9 = (bf16[256,768]{1,0:T(8,128)(2,1)}, bf16[256,1536]{1,0:T(8,128)(2,1)}) custom-call(s32[4]{0:T(128)} %and_select_fusion.order_ref, f32[2,128]{1,0:T(2,128)} %gain_ref.11, bf16[256,768]{1,0:T(8,128)(2,1)} %copy-done.34, bf16[256,768]{1,0:T(8,128)(2,1)} %copy-done.35, bf16[256,768]{1,0:T(8,128)(2,1)} %copy-done.39, bf16[256,768]{1,0:T(8,128)(2,1)} %copy-done.41, ...), custom_call_target="tpu_custom_call" | custom-call | flops 1000 | bytes 1000 | tf_op jit(solution)/shard_map/qkv/pallas_call | solution.py:69
  373.0 2.9 collective-permute-start.53
  377.6 9.6 %collective-permute-done.51.refs_3_ = bf16[256,768]{1,0:T(8,128)(2,1)S(1)} collective-permute-done((bf16[256,768]{1,0:T(8,128)(2,1)S(1)}, bf16[256,768]{1,0:T(8,128)(2,1)S(1)}, u32[]{:S(2)}, u32[]{:S(2)}) %collective-permute-start.51) | collective-permute-done | bytes 393248 | tf_op jit(solution)/shard_map/ppermute | solution.py:24
  387.2 8.4 %collective-permute-done.52.refs_1_ = bf16[256,768]{1,0:T(8,128)(2,1)S(1)} collective-permute-done((bf16[256,768]{1,0:T(8,128)(2,1)S(1)}, bf16[256,768]{1,0:T(8,128)(2,1)S(1)}, u32[]{:S(2)}, u32[]{:S(2)}) %collective-permute-start.52) | collective-permute-done | bytes 393248 | tf_op jit(solution)/shard_map/ppermute | solution.py:24
  395.6 4.3 collective-permute-start.56
  400.0 10.6 %qkv.10 = (bf16[256,768]{1,0:T(8,128)(2,1)}, bf16[256,1536]{1,0:T(8,128)(2,1)}) custom-call(s32[4]{0:T(128)} %and_select_fusion.order_ref, f32[2,128]{1,0:T(2,128)} %gain_ref.11, bf16[256,768]{1,0:T(8,128)(2,1)} %copy-done.36, bf16[256,768]{1,0:T(8,128)(2,1)} %copy-done.37, bf16[256,768]{1,0:T(8,128)(2,1)} %copy-done.40, bf16[256,768]{1,0:T(8,128)(2,1)} %copy-done.53, ...), custom_call_target="tpu_custom_call" | custom-call | flops 1000 | bytes 1000 | tf_op jit(solution)/shard_map/qkv/pallas_call | solution.py:69
  410.7 12.4 %collective-permute-done.55.refs_3_ = bf16[256,768]{1,0:T(8,128)(2,1)S(1)} collective-permute-done((bf16[256,768]{1,0:T(8,128)(2,1)S(1)}, bf16[256,768]{1,0:T(8,128)(2,1)S(1)}, u32[]{:S(2)}, u32[]{:S(2)}) %collective-permute-start.55) | collective-permute-done | bytes 393248 | tf_op jit(solution)/shard_map/ppermute | solution.py:24
  426.5 10.7 %qkv.11 = (bf16[256,768]{1,0:T(8,128)(2,1)}, bf16[256,1536]{1,0:T(8,128)(2,1)}) custom-call(s32[4]{0:T(128)} %and_select_fusion.order_ref, f32[2,128]{1,0:T(2,128)} %gain_ref.11, bf16[256,768]{1,0:T(8,128)(2,1)} %copy-done.38, bf16[256,768]{1,0:T(8,128)(2,1)} %copy-done.42, bf16[256,768]{1,0:T(8,128)(2,1)} %copy-done.45, bf16[256,768]{1,0:T(8,128)(2,1)} %copy-done.49, ...), custom_call_target="tpu_custom_call" | custom-call | flops 1000 | bytes 1000 | tf_op jit(solution)/shard_map/qkv/pallas_call | solution.py:69
  437.1 7.8 %collective-permute-done.57.refs_11_.refs_22_ = bf16[256,1536]{1,0:T(8,128)(2,1)S(1)} collective-permute-done((bf16[256,1536]{1,0:T(8,128)(2,1)S(1)}, bf16[256,1536]{1,0:T(8,128)(2,1)S(1)}, u32[]{:S(2)}, u32[]{:S(2)}) %collective-permute-start.57) | collective-permute-done | bytes 786464 | tf_op jit(solution)/shard_map/ppermute | solution.py:24
  449.8 19.3 %attend.9.refs_15_ = f32[6,768,256]{2,1,0:T(8,128)} custom-call(s32[7]{0:T(128)} %and_convert_fusion.usable_ref, bf16[256,768]{1,0:T(8,128)(2,1)} %get-tuple-element.122.refs_0_, bf16[256,768]{1,0:T(8,128)(2,1)} %get-tuple-element.131.refs_1_, bf16[256,768]{1,0:T(8,128)(2,1)} %get-tuple-element.138.refs_2_, ...), custom_call_target="tpu_custom_call" | custom-call | flops 1000 | bytes 1000 | tf_op jit(solution)/shard_map/attend/pallas_call | solution.py:140
  470.9 3.2 collective-permute-start.64
  474.1 3.4 collective-permute-start.65
  479.7 12.9 %attend.10.refs_11_ = f32[6,768,256]{2,1,0:T(8,128)} custom-call(s32[7]{0:T(128)} %and_convert_fusion.usable_ref, bf16[256,768]{1,0:T(8,128)(2,1)} %get-tuple-element.122.refs_0_, bf16[256,768]{1,0:T(8,128)(2,1)} %get-tuple-element.131.refs_1_, bf16[256,768]{1,0:T(8,128)(2,1)} %get-tuple-element.138.refs_2_, bf16[256,1536]{1,0:T(8,128)(2,1)} %copy-done.21, ...), custom_call_target="tpu_custom_call" | custom-call | flops 1000 | bytes 1000 | tf_op jit(solution)/shard_map/attend/pallas_call | solution.py:140
  496.5 4.5 collective-permute-done.66.refs_4_.refs_5_.refs_6_.refs_8_.refs_9_.refs_10_
  502.4 10.4 %attend.11.attended_ref = bf16[768,768]{1,0:T(8,128)(2,1)} custom-call(s32[7]{0:T(128)} %and_convert_fusion.usable_ref, bf16[256,768]{1,0:T(8,128)(2,1)} %get-tuple-element.122.refs_0_, bf16[256,768]{1,0:T(8,128)(2,1)} %get-tuple-element.131.refs_1_, bf16[256,768]{1,0:T(8,128)(2,1)} %get-tuple-element.138.refs_2_, bf16[256,1536]{1,0:T(8,128)(2,1)} %copy-done.8, ...), custom_call_target="tpu_custom_call" | custom-call | flops 1000 | bytes 1000 | tf_op jit(solution)/shard_map/attend/pallas_call | solution.py:140
  512.8 4.2 shares.6
  520.1 7.3 %shares.7.share_ref = bf16[3,768,768]{2,1,0:T(8,128)(2,1)} custom-call(s32[3]{0:T(128)} %slice.54.order_ref, bf16[768,768]{1,0:T(8,128)(2,1)} %attend.11.attended_ref, bf16[768,3072]{1,0:T(8,128)(2,1)} %weight_ref.7), custom_call_target="tpu_custom_call" | custom-call | flops 1000 | bytes 1000 | tf_op jit(solution)/shard_map/shares/pallas_call | solution.py:187
  527.4 3.6 collective-permute-done.76.total_ref
  533.7 5.7 collective-permute-done.72.total_ref
  542.2 5.7 collective-permute-done.68.total_ref
  550.6 5.7 collective-permute-done.77.total_ref
  559.0 5.7 collective-permute-done.73.total_ref
  567.4 5.7 collective-permute-done.69.total_ref
  575.8 5.7 collective-permute-done.78.total_ref
  584.4 5.6 collective-permute-done.74.total_ref
  592.8 4.8 collective-permute-done.70.total_ref
  (331 shorter events, 130.2 us)
Async XLA Ops:
  2.2 12.7 %collective-permute-start = (f32[2,768]{1,0:T(2,128)S(1)}, f32[2,768]{1,0:T(2,128)S(1)}, u32[]{:S(2)}, u32[]{:S(2)}) collective-permute-start(f32[2,768]{1,0:T(2,128)S(1)} %pad_maximum_fusion.7), channel_id=1, source_target_pairs={{0,1},{1,2},{2,3},{3,0},{4,5},{5,6},{6,7},{7,4},{8,9},{9,10},{10,1... | collective-permute-start | bytes 18440 | tf_op jit(solution)/shard_map/ppermute | solution.py:24
  15.5 13.3 %collective-permute-start.3 = (bf16[256,768]{1,0:T(8,128)(2,1)S(1)}, bf16[256,768]{1,0:T(8,128)(2,1)S(1)}, u32[]{:S(2)}, u32[]{:S(2)}) collective-permute-start(bf16[256,768]{1,0:T(8,128)(2,1)S(1)} %get-tuple-element.165.refs_0_), channel_id=1, source_target_pairs={{0,1},{1,2},{2,3},{3,0},{4,5},{5,6},{6,7},{7,4},{8,9},{9,10},{10,1... | collective-permute-start | bytes 1179656 | tf_op jit(solution)/shard_map/ppermute | solution.py:24
  41.3 13.8 %collective-permute-start.5 = (bf16[256,768]{1,0:T(8,128)(2,1)S(1)}, bf16[256,768]{1,0:T(8,128)(2,1)S(1)}, u32[]{:S(2)}, u32[]{:S(2)}) collective-permute-start(bf16[256,768]{1,0:T(8,128)(2,1)S(1)} %collective-permute-done.4.refs_2_), channel_id=1, source_target_pairs={{0,1},{1,2},{2,3},{3,0},{4,5},{5,6},{6,7},{7,4},{8,9},{9,10},{10,1... | collective-permute-start | bytes 1179656 | tf_op jit(solution)/shard_map/ppermute | solution.py:24
  41.3 20.0 %collective-permute-start.6 = (bf16[256,768]{1,0:T(8,128)(2,1)S(1)}, bf16[256,768]{1,0:T(8,128)(2,1)S(1)}, u32[]{:S(2)}, u32[]{:S(2)}) collective-permute-start(bf16[256,768]{1,0:T(8,128)(2,1)S(1)} %get-tuple-element.82.refs_0_), channel_id=1, source_target_pairs={{0,1},{1,2},{2,3},{3,0},{4,5},{5,6},{6,7},{7,4},{8,9},{9,10},{10,1... | collective-permute-start | bytes 1179656 | tf_op jit(solution)/shard_map/ppermute | solution.py:24
  61.3 13.2 %collective-permute-start.7 = (bf16[256,768]{1,0:T(8,128)(2,1)S(1)}, bf16[256,768]{1,0:T(8,128)(2,1)S(1)}, u32[]{:S(2)}, u32[]{:S(2)}) collective-permute-start(bf16[256,768]{1,0:T(8,128)(2,1)S(1)} %collective-permute-done.6.refs_1_), channel_id=1, source_target_pairs={{0,1},{1,2},{2,3},{3,0},{4,5},{5,6},{6,7},{7,4},{8,9},{9,10},{10,1... | collective-permute-start | bytes 1179656 | tf_op jit(solution)/shard_map/ppermute | solution.py:24
  72.5 21.5 %collective-permute-start.10 = (bf16[256,1536]{1,0:T(8,128)(2,1)}, bf16[256,1536]{1,0:T(8,128)(2,1)S(1)}, u32[]{:S(2)}, u32[]{:S(2)}) collective-permute-start(bf16[256,1536]{1,0:T(8,128)(2,1)} %get-tuple-element.100.refs_3_.refs_14_), channel_id=1, source_target_pairs={{0,8},{4,12},{8,0},{12,4},{16,24},{20,28},{24,16},{28,20},{1,9},{5... | collective-permute-start | bytes 2359304 | tf_op jit(solution)/shard_map/ppermute | solution.py:24
  74.5 13.8 %collective-permute-start.8 = (bf16[256,768]{1,0:T(8,128)(2,1)S(1)}, bf16[256,768]{1,0:T(8,128)(2,1)S(1)}, u32[]{:S(2)}, u32[]{:S(2)}) collective-permute-start(bf16[256,768]{1,0:T(8,128)(2,1)S(1)} %collective-permute-done.7.refs_2_), channel_id=1, source_target_pairs={{0,1},{1,2},{2,3},{3,0},{4,5},{5,6},{6,7},{7,4},{8,9},{9,10},{10,1... | collective-permute-start | bytes 1179656 | tf_op jit(solution)/shard_map/ppermute | solution.py:24
  74.5 19.5 %collective-permute-start.9 = (bf16[256,768]{1,0:T(8,128)(2,1)S(1)}, bf16[256,768]{1,0:T(8,128)(2,1)S(1)}, u32[]{:S(2)}, u32[]{:S(2)}) collective-permute-start(bf16[256,768]{1,0:T(8,128)(2,1)S(1)} %get-tuple-element.89.refs_0_), channel_id=1, source_target_pairs={{0,1},{1,2},{2,3},{3,0},{4,5},{5,6},{6,7},{7,4},{8,9},{9,10},{10,1... | collective-permute-start | bytes 1179656 | tf_op jit(solution)/shard_map/ppermute | solution.py:24
  94.1 14.2 %collective-permute-start.11 = (bf16[256,768]{1,0:T(8,128)(2,1)S(1)}, bf16[256,768]{1,0:T(8,128)(2,1)S(1)}, u32[]{:S(2)}, u32[]{:S(2)}) collective-permute-start(bf16[256,768]{1,0:T(8,128)(2,1)S(1)} %collective-permute-done.9.refs_1_), channel_id=1, source_target_pairs={{0,1},{1,2},{2,3},{3,0},{4,5},{5,6},{6,7},{7,4},{8,9},{9,10},{10,1... | collective-permute-start | bytes 1179656 | tf_op jit(solution)/shard_map/ppermute | solution.py:24
  94.1 24.1 %collective-permute-start.13 = (bf16[256,1536]{1,0:T(8,128)(2,1)S(1)}, bf16[256,1536]{1,0:T(8,128)(2,1)S(1)}, u32[]{:S(2)}, u32[]{:S(2)}) collective-permute-start(bf16[256,1536]{1,0:T(8,128)(2,1)S(1)} %collective-permute-done.10.refs_5_.refs_16_), channel_id=1, source_target_pairs={{0,16},{4,20},{24,8},{28,12},{1,17},{5,21},{25,9},{29,13},{2,18},{... | collective-permute-start | bytes 2359304 | tf_op jit(solution)/shard_map/ppermute | solution.py:24
  120.0 25.7 %collective-permute-start.15 = (bf16[768,1536]{1,0:T(8,128)(2,1)}, bf16[768,1536]{1,0:T(8,128)(2,1)S(1)}, u32[]{:S(2)}, u32[]{:S(2)}) collective-permute-start(bf16[768,1536]{1,0:T(8,128)(2,1)} %pad_maximum_fusion), channel_id=1, source_target_pairs={{0,4},{4,0},{8,12},{12,8},{16,20},{20,16},{24,28},{28,24},{1,5},{5... | collective-permute-start | bytes 7077896 | tf_op jit(solution)/shard_map/ppermute | solution.py:24
  120.0 20.3 %collective-permute-start.14 = (bf16[256,1536]{1,0:T(8,128)(2,1)}, bf16[256,1536]{1,0:T(8,128)(2,1)}, u32[]{:S(2)}, u32[]{:S(2)}) collective-permute-start(bf16[256,1536]{1,0:T(8,128)(2,1)} %get-tuple-element.102.refs_10_.refs_21_), channel_id=1, source_target_pairs={{0,8},{4,12},{8,0},{12,4},{16,24},{20,28},{24,16},{28,20},{1,9},{5... | collective-permute-start | bytes 2359304 | tf_op jit(solution)/shard_map/ppermute | solution.py:24
  120.1 22.6 %collective-permute-start.16 = (bf16[256,1536]{1,0:T(8,128)(2,1)S(1)}, bf16[256,1536]{1,0:T(8,128)(2,1)S(1)}, u32[]{:S(2)}, u32[]{:S(2)}) collective-permute-start(bf16[256,1536]{1,0:T(8,128)(2,1)S(1)} %copy-done.9), channel_id=1, source_target_pairs={{4,16},{12,24},{16,4},{24,12},{5,17},{13,25},{17,5},{25,13},{6,18}... | collective-permute-start | bytes 2359304 | tf_op jit(solution)/shard_map/ppermute | solution.py:24
  120.8 24.8 %collective-permute-start.17 = (bf16[256,1536]{1,0:T(8,128)(2,1)}, bf16[256,1536]{1,0:T(8,128)(2,1)}, u32[]{:S(2)}, u32[]{:S(2)}) collective-permute-start(bf16[256,1536]{1,0:T(8,128)(2,1)} %get-tuple-element.102.refs_10_.refs_21_), channel_id=1, source_target_pairs={{4,16},{12,24},{16,4},{24,12},{5,17},{13,25},{17,5},{25,13},{6,18}... | collective-permute-start | bytes 2359304 | tf_op jit(solution)/shard_map/ppermute | solution.py:24
  140.3 25.9 %collective-permute-start.18 = (bf16[256,1536]{1,0:T(8,128)(2,1)}, bf16[256,1536]{1,0:T(8,128)(2,1)}, u32[]{:S(2)}, u32[]{:S(2)}) collective-permute-start(bf16[256,1536]{1,0:T(8,128)(2,1)} %collective-permute-done.14.refs_11_.refs_22_), channel_id=1, source_target_pairs={{0,16},{4,20},{24,8},{28,12},{1,17},{5,21},{25,9},{29,13},{2,18},{... | collective-permute-start | bytes 2359304 | tf_op jit(solution)/shard_map/ppermute | solution.py:24
  142.7 23.5 %collective-permute-start.19 = (bf16[256,1536]{1,0:T(8,128)(2,1)}, bf16[256,1536]{1,0:T(8,128)(2,1)}, u32[]{:S(2)}, u32[]{:S(2)}) collective-permute-start(bf16[256,1536]{1,0:T(8,128)(2,1)} %get-tuple-element.104.refs_13_.refs_24_), channel_id=1, source_target_pairs={{0,8},{4,12},{8,0},{12,4},{16,24},{20,28},{24,16},{28,20},{1,9},{5... | collective-permute-start | bytes 2359304 | tf_op jit(solution)/shard_map/ppermute | solution.py:24
  143.6 22.6 %collective-permute-start.20 = (bf16[256,1536]{1,0:T(8,128)(2,1)}, bf16[256,1536]{1,0:T(8,128)(2,1)S(1)}, u32[]{:S(2)}, u32[]{:S(2)}) collective-permute-start(bf16[256,1536]{1,0:T(8,128)(2,1)} %get-tuple-element.104.refs_13_.refs_24_), channel_id=1, source_target_pairs={{4,16},{12,24},{16,4},{24,12},{5,17},{13,25},{17,5},{25,13},{6,18}... | collective-permute-start | bytes 2359304 | tf_op jit(solution)/shard_map/ppermute | solution.py:24
  172.3 19.6 %collective-permute-start.22 = (bf16[256,1536]{1,0:T(8,128)(2,1)}, bf16[256,1536]{1,0:T(8,128)(2,1)S(1)}, u32[]{:S(2)}, u32[]{:S(2)}) collective-permute-start(bf16[256,1536]{1,0:T(8,128)(2,1)} %collective-permute-done.19.refs_4_.refs_10_), channel_id=1, source_target_pairs={{0,16},{4,20},{24,8},{28,12},{1,17},{5,21},{25,9},{29,13},{2,18},{... | collective-permute-start | bytes 2359304 | tf_op jit(solution)/shard_map/ppermute | solution.py:24
  215.8 13.2 %collective-permute-start.24 = (bf16[256,768]{1,0:T(8,128)(2,1)}, bf16[256,768]{1,0:T(8,128)(2,1)S(1)}, u32[]{:S(2)}, u32[]{:S(2)}) collective-permute-start(bf16[256,768]{1,0:T(8,128)(2,1)} %get-tuple-element.111), channel_id=1, source_target_pairs={{0,1},{1,2},{2,3},{3,0},{4,5},{5,6},{6,7},{7,4},{8,9},{9,10},{10,1... | collective-permute-start | bytes 1179656 | tf_op jit(solution)/shard_map/ppermute | solution.py:24
  231.6 14.1 %collective-permute-start.25 = (bf16[256,768]{1,0:T(8,128)(2,1)}, bf16[256,768]{1,0:T(8,128)(2,1)S(1)}, u32[]{:S(2)}, u32[]{:S(2)}) collective-permute-start(bf16[256,768]{1,0:T(8,128)(2,1)} %add_share.15), channel_id=1, source_target_pairs={{0,1},{1,2},{2,3},{3,0},{4,5},{5,6},{6,7},{7,4},{8,9},{9,10},{10,1... | collective-permute-start | bytes 1179656 | tf_op jit(solution)/shard_map/ppermute | solution.py:24
  231.7 22.5 %collective-permute-start.27 = (bf16[256,768]{1,0:T(8,128)(2,1)S(1)}, bf16[256,768]{1,0:T(8,128)(2,1)S(1)}, u32[]{:S(2)}, u32[]{:S(2)}) collective-permute-start(bf16[256,768]{1,0:T(8,128)(2,1)S(1)} %copy-done.85), channel_id=1, source_target_pairs={{0,1},{1,2},{2,3},{3,0},{4,5},{5,6},{6,7},{7,4},{8,9},{9,10},{10,1... | collective-permute-start | bytes 1179656 | tf_op jit(solution)/shard_map/ppermute | solution.py:24
  248.4 14.1 %collective-permute-start.26 = (bf16[256,768]{1,0:T(8,128)(2,1)}, bf16[256,768]{1,0:T(8,128)(2,1)S(1)}, u32[]{:S(2)}, u32[]{:S(2)}) collective-permute-start(bf16[256,768]{1,0:T(8,128)(2,1)} %add_share.16), channel_id=1, source_target_pairs={{0,1},{1,2},{2,3},{3,0},{4,5},{5,6},{6,7},{7,4},{8,9},{9,10},{10,1... | collective-permute-start | bytes 1179656 | tf_op jit(solution)/shard_map/ppermute | solution.py:24
  256.8 18.4 %collective-permute-start.28 = (bf16[256,768]{1,0:T(8,128)(2,1)}, bf16[256,768]{1,0:T(8,128)(2,1)S(1)}, u32[]{:S(2)}, u32[]{:S(2)}) collective-permute-start(bf16[256,768]{1,0:T(8,128)(2,1)} %add_share.17), channel_id=1, source_target_pairs={{0,1},{1,2},{2,3},{3,0},{4,5},{5,6},{6,7},{7,4},{8,9},{9,10},{10,1... | collective-permute-start | bytes 1179656 | tf_op jit(solution)/shard_map/ppermute | solution.py:24
  278.0 12.7 %collective-permute-start.29 = (bf16[256,768]{1,0:T(8,128)(2,1)}, bf16[256,768]{1,0:T(8,128)(2,1)S(1)}, u32[]{:S(2)}, u32[]{:S(2)}) collective-permute-start(bf16[256,768]{1,0:T(8,128)(2,1)} %add_share.18), channel_id=1, source_target_pairs={{0,1},{1,2},{2,3},{3,0},{4,5},{5,6},{6,7},{7,4},{8,9},{9,10},{10,1... | collective-permute-start | bytes 1179656 | tf_op jit(solution)/shard_map/ppermute | solution.py:24
  280.0 19.1 %collective-permute-start.30 = (bf16[256,768]{1,0:T(8,128)(2,1)S(1)}, bf16[256,768]{1,0:T(8,128)(2,1)S(1)}, u32[]{:S(2)}, u32[]{:S(2)}) collective-permute-start(bf16[256,768]{1,0:T(8,128)(2,1)S(1)} %copy-done.84), channel_id=1, source_target_pairs={{0,1},{1,2},{2,3},{3,0},{4,5},{5,6},{6,7},{7,4},{8,9},{9,10},{10,1... | collective-permute-start | bytes 1179656 | tf_op jit(solution)/shard_map/ppermute | solution.py:24
  283.5 37.1 %collective-permute-start.38 = (bf16[256,768]{1,0:T(8,128)(2,1)S(1)}, bf16[256,768]{1,0:T(8,128)(2,1)S(1)}, u32[]{:S(2)}, u32[]{:S(2)}) collective-permute-start(bf16[256,768]{1,0:T(8,128)(2,1)S(1)} %collective-permute-done.37.refs_0_), channel_id=1, source_target_pairs={{0,1},{1,2},{2,3},{3,0},{4,5},{5,6},{6,7},{7,4},{8,9},{9,10},{10,1... | collective-permute-start | bytes 1179656 | tf_op jit(solution)/shard_map/ppermute | solution.py:24
  294.2 13.7 %collective-permute-start.40 = (f32[8,256]{1,0:T(8,128)}, f32[8,256]{1,0:T(8,128)S(1)}, u32[]{:S(2)}, u32[]{:S(2)}) collective-permute-start(f32[8,256]{1,0:T(8,128)} %get-tuple-element.118.refs_0_), channel_id=1, source_target_pairs={{0,1},{1,2},{2,3},{3,0},{4,5},{5,6},{6,7},{7,4},{8,9},{9,10},{10,1... | collective-permute-start | bytes 24584 | tf_op jit(solution)/shard_map/ppermute | solution.py:24
  294.4 13.5 %collective-permute-start.41 = (f32[8,256]{1,0:T(8,128)}, f32[8,256]{1,0:T(8,128)S(1)}, u32[]{:S(2)}, u32[]{:S(2)}) collective-permute-start(f32[8,256]{1,0:T(8,128)} %get-tuple-element.118.refs_0_), channel_id=1, source_target_pairs={{0,2},{1,3},{2,0},{3,1},{4,6},{5,7},{6,4},{7,5},{8,10},{9,11},{10,... | collective-permute-start | bytes 24584 | tf_op jit(solution)/shard_map/ppermute | solution.py:24
  301.8 19.7 %collective-permute-start.31 = (bf16[256,768]{1,0:T(8,128)(2,1)}, bf16[256,768]{1,0:T(8,128)(2,1)S(1)}, u32[]{:S(2)}, u32[]{:S(2)}) collective-permute-start(bf16[256,768]{1,0:T(8,128)(2,1)} %add_share.19), channel_id=1, source_target_pairs={{0,1},{1,2},{2,3},{3,0},{4,5},{5,6},{6,7},{7,4},{8,9},{9,10},{10,1... | collective-permute-start | bytes 1179656 | tf_op jit(solution)/shard_map/ppermute | solution.py:24
  310.9 16.3 %collective-permute-start.43 = (bf16[256,768]{1,0:T(8,128)(2,1)}, bf16[256,768]{1,0:T(8,128)(2,1)S(1)}, u32[]{:S(2)}, u32[]{:S(2)}) collective-permute-start(bf16[256,768]{1,0:T(8,128)(2,1)} %normalize.4), channel_id=1, source_target_pairs={{0,4},{4,8},{8,12},{12,16},{16,20},{20,24},{24,28},{28,0},{1,5},{5... | collective-permute-start | bytes 1179656 | tf_op jit(solution)/shard_map/ppermute | solution.py:24
  320.7 13.8 %collective-permute-start.39 = (bf16[256,768]{1,0:T(8,128)(2,1)S(1)}, bf16[256,768]{1,0:T(8,128)(2,1)S(1)}, u32[]{:S(2)}, u32[]{:S(2)}) collective-permute-start(bf16[256,768]{1,0:T(8,128)(2,1)S(1)} %collective-permute-done.38.refs_1_), channel_id=1, source_target_pairs={{0,1},{1,2},{2,3},{3,0},{4,5},{5,6},{6,7},{7,4},{8,9},{9,10},{10,1... | collective-permute-start | bytes 1179656 | tf_op jit(solution)/shard_map/ppermute | solution.py:24
  324.3 18.6 %collective-permute-start.32 = (bf16[256,768]{1,0:T(8,128)(2,1)}, bf16[256,768]{1,0:T(8,128)(2,1)S(1)}, u32[]{:S(2)}, u32[]{:S(2)}) collective-permute-start(bf16[256,768]{1,0:T(8,128)(2,1)} %add_share.20), channel_id=1, source_target_pairs={{0,1},{1,2},{2,3},{3,0},{4,5},{5,6},{6,7},{7,4},{8,9},{9,10},{10,1... | collective-permute-start | bytes 1179656 | tf_op jit(solution)/shard_map/ppermute | solution.py:24
  334.4 17.0 %collective-permute-start.44 = (bf16[256,768]{1,0:T(8,128)(2,1)S(1)}, bf16[256,768]{1,0:T(8,128)(2,1)S(1)}, u32[]{:S(2)}, u32[]{:S(2)}) collective-permute-start(bf16[256,768]{1,0:T(8,128)(2,1)S(1)} %collective-permute-done.39.refs_2_), channel_id=1, source_target_pairs={{0,1},{1,2},{2,3},{3,0},{4,5},{5,6},{6,7},{7,4},{8,9},{9,10},{10,1... | collective-permute-start | bytes 1179656 | tf_op jit(solution)/shard_map/ppermute | solution.py:24
  334.4 24.8 %collective-permute-start.45 = (bf16[256,768]{1,0:T(8,128)(2,1)S(1)}, bf16[256,768]{1,0:T(8,128)(2,1)S(1)}, u32[]{:S(2)}, u32[]{:S(2)}) collective-permute-start(bf16[256,768]{1,0:T(8,128)(2,1)S(1)} %collective-permute-done.43.refs_0_), channel_id=1, source_target_pairs={{0,1},{1,2},{2,3},{3,0},{4,5},{5,6},{6,7},{7,4},{8,9},{9,10},{10,1... | collective-permute-start | bytes 1179656 | tf_op jit(solution)/shard_map/ppermute | solution.py:24
  346.4 12.9 %collective-permute-start.47 = (f32[8,256]{1,0:T(8,128)}, f32[8,256]{1,0:T(8,128)S(1)}, u32[]{:S(2)}, u32[]{:S(2)}) collective-permute-start(f32[8,256]{1,0:T(8,128)} %get-tuple-element.126.refs_0_), channel_id=1, source_target_pairs={{0,1},{1,2},{2,3},{3,0},{4,5},{5,6},{6,7},{7,4},{8,9},{9,10},{10,1... | collective-permute-start | bytes 24584 | tf_op jit(solution)/shard_map/ppermute | solution.py:24
  346.4 13.1 %collective-permute-start.48 = (f32[8,256]{1,0:T(8,128)}, f32[8,256]{1,0:T(8,128)S(1)}, u32[]{:S(2)}, u32[]{:S(2)}) collective-permute-start(f32[8,256]{1,0:T(8,128)} %get-tuple-element.126.refs_0_), channel_id=1, source_target_pairs={{0,2},{1,3},{2,0},{3,1},{4,6},{5,7},{6,4},{7,5},{8,10},{9,11},{10,... | collective-permute-start | bytes 24584 | tf_op jit(solution)/shard_map/ppermute | solution.py:24
  346.6 12.9 %collective-permute-start.49 = (f32[8,256]{1,0:T(8,128)}, f32[8,256]{1,0:T(8,128)S(1)}, u32[]{:S(2)}, u32[]{:S(2)}) collective-permute-start(f32[8,256]{1,0:T(8,128)} %get-tuple-element.126.refs_0_), channel_id=1, source_target_pairs={{0,3},{1,0},{2,1},{3,2},{4,7},{5,4},{6,5},{7,6},{8,11},{9,8},{10,9... | collective-permute-start | bytes 24584 | tf_op jit(solution)/shard_map/ppermute | solution.py:24
  359.2 16.7 %collective-permute-start.46 = (bf16[256,768]{1,0:T(8,128)(2,1)S(1)}, bf16[256,768]{1,0:T(8,128)(2,1)S(1)}, u32[]{:S(2)}, u32[]{:S(2)}) collective-permute-start(bf16[256,768]{1,0:T(8,128)(2,1)S(1)} %collective-permute-done.45.refs_1_), channel_id=1, source_target_pairs={{0,1},{1,2},{2,3},{3,0},{4,5},{5,6},{6,7},{7,4},{8,9},{9,10},{10,1... | collective-permute-start | bytes 1179656 | tf_op jit(solution)/shard_map/ppermute | solution.py:24
  362.4 13.5 %collective-permute-start.50 = (bf16[256,768]{1,0:T(8,128)(2,1)}, bf16[256,768]{1,0:T(8,128)(2,1)S(1)}, u32[]{:S(2)}, u32[]{:S(2)}) collective-permute-start(bf16[256,768]{1,0:T(8,128)(2,1)} %normalize.5), channel_id=1, source_target_pairs={{0,4},{4,8},{8,12},{12,16},{16,20},{20,24},{24,28},{28,0},{1,5},{5... | collective-permute-start | bytes 1179656 | tf_op jit(solution)/shard_map/ppermute | solution.py:24
  373.0 22.6 %collective-permute-start.53 = (bf16[256,1536]{1,0:T(8,128)(2,1)}, bf16[256,1536]{1,0:T(8,128)(2,1)S(1)}, u32[]{:S(2)}, u32[]{:S(2)}) collective-permute-start(bf16[256,1536]{1,0:T(8,128)(2,1)} %get-tuple-element.139.refs_3_.refs_14_), channel_id=1, source_target_pairs={{0,8},{4,12},{8,0},{12,4},{16,24},{20,28},{24,16},{28,20},{1,9},{5... | collective-permute-start | bytes 2359304 | tf_op jit(solution)/shard_map/ppermute | solution.py:24
  377.1 18.5 %collective-permute-start.52 = (bf16[256,768]{1,0:T(8,128)(2,1)S(1)}, bf16[256,768]{1,0:T(8,128)(2,1)S(1)}, u32[]{:S(2)}, u32[]{:S(2)}) collective-permute-start(bf16[256,768]{1,0:T(8,128)(2,1)S(1)} %collective-permute-done.50.refs_0_), channel_id=1, source_target_pairs={{0,1},{1,2},{2,3},{3,0},{4,5},{5,6},{6,7},{7,4},{8,9},{9,10},{10,1... | collective-permute-start | bytes 1179656 | tf_op jit(solution)/shard_map/ppermute | solution.py:24
  395.6 15.0 %collective-permute-start.54 = (bf16[256,768]{1,0:T(8,128)(2,1)S(1)}, bf16[256,768]{1,0:T(8,128)(2,1)S(1)}, u32[]{:S(2)}, u32[]{:S(2)}) collective-permute-start(bf16[256,768]{1,0:T(8,128)(2,1)S(1)} %collective-permute-done.52.refs_1_), channel_id=1, source_target_pairs={{0,1},{1,2},{2,3},{3,0},{4,5},{5,6},{6,7},{7,4},{8,9},{9,10},{10,1... | collective-permute-start | bytes 1179656 | tf_op jit(solution)/shard_map/ppermute | solution.py:24
  395.6 27.6 %collective-permute-start.56 = (bf16[256,1536]{1,0:T(8,128)(2,1)S(1)}, bf16[256,1536]{1,0:T(8,128)(2,1)S(1)}, u32[]{:S(2)}, u32[]{:S(2)}) collective-permute-start(bf16[256,1536]{1,0:T(8,128)(2,1)S(1)} %collective-permute-done.53.refs_5_.refs_16_), channel_id=1, source_target_pairs={{0,16},{4,20},{24,8},{28,12},{1,17},{5,21},{25,9},{29,13},{2,18},{... | collective-permute-start | bytes 2359304 | tf_op jit(solution)/shard_map/ppermute | solution.py:24
  410.7 12.5 %collective-permute-start.55 = (bf16[256,768]{1,0:T(8,128)(2,1)S(1)}, bf16[256,768]{1,0:T(8,128)(2,1)S(1)}, u32[]{:S(2)}, u32[]{:S(2)}) collective-permute-start(bf16[256,768]{1,0:T(8,128)(2,1)S(1)} %collective-permute-done.54.refs_2_), channel_id=1, source_target_pairs={{0,1},{1,2},{2,3},{3,0},{4,5},{5,6},{6,7},{7,4},{8,9},{9,10},{10,1... | collective-permute-start | bytes 1179656 | tf_op jit(solution)/shard_map/ppermute | solution.py:24
  424.9 23.2 %collective-permute-start.58 = (bf16[768,1536]{1,0:T(8,128)(2,1)}, bf16[768,1536]{1,0:T(8,128)(2,1)S(1)}, u32[]{:S(2)}, u32[]{:S(2)}) collective-permute-start(bf16[768,1536]{1,0:T(8,128)(2,1)} %pad_maximum_fusion.3), channel_id=1, source_target_pairs={{0,4},{4,0},{8,12},{12,8},{16,20},{20,16},{24,28},{28,24},{1,5},{5... | collective-permute-start | bytes 7077896 | tf_op jit(solution)/shard_map/ppermute | solution.py:24
  424.9 20.0 %collective-permute-start.57 = (bf16[256,1536]{1,0:T(8,128)(2,1)S(1)}, bf16[256,1536]{1,0:T(8,128)(2,1)S(1)}, u32[]{:S(2)}, u32[]{:S(2)}) collective-permute-start(bf16[256,1536]{1,0:T(8,128)(2,1)S(1)} %copy-done.15), channel_id=1, source_target_pairs={{0,8},{4,12},{8,0},{12,4},{16,24},{20,28},{24,16},{28,20},{1,9},{5... | collective-permute-start | bytes 2359304 | tf_op jit(solution)/shard_map/ppermute | solution.py:24
  425.0 21.5 %collective-permute-start.59 = (bf16[256,1536]{1,0:T(8,128)(2,1)S(1)}, bf16[256,1536]{1,0:T(8,128)(2,1)S(1)}, u32[]{:S(2)}, u32[]{:S(2)}) collective-permute-start(bf16[256,1536]{1,0:T(8,128)(2,1)S(1)} %copy-done.13), channel_id=1, source_target_pairs={{4,16},{12,24},{16,4},{24,12},{5,17},{13,25},{17,5},{25,13},{6,18}... | collective-permute-start | bytes 2359304 | tf_op jit(solution)/shard_map/ppermute | solution.py:24
  425.7 22.4 %collective-permute-start.60 = (bf16[256,1536]{1,0:T(8,128)(2,1)S(1)}, bf16[256,1536]{1,0:T(8,128)(2,1)S(1)}, u32[]{:S(2)}, u32[]{:S(2)}) collective-permute-start(bf16[256,1536]{1,0:T(8,128)(2,1)S(1)} %copy-done.15), channel_id=1, source_target_pairs={{4,16},{12,24},{16,4},{24,12},{5,17},{13,25},{17,5},{25,13},{6,18}... | collective-permute-start | bytes 2359304 | tf_op jit(solution)/shard_map/ppermute | solution.py:24
  444.9 24.1 %collective-permute-start.61 = (bf16[256,1536]{1,0:T(8,128)(2,1)S(1)}, bf16[256,1536]{1,0:T(8,128)(2,1)S(1)}, u32[]{:S(2)}, u32[]{:S(2)}) collective-permute-start(bf16[256,1536]{1,0:T(8,128)(2,1)S(1)} %collective-permute-done.57.refs_11_.refs_22_), channel_id=1, source_target_pairs={{0,16},{4,20},{24,8},{28,12},{1,17},{5,21},{25,9},{29,13},{2,18},{... | collective-permute-start | bytes 2359304 | tf_op jit(solution)/shard_map/ppermute | solution.py:24
  446.2 22.8 %collective-permute-start.62 = (bf16[256,1536]{1,0:T(8,128)(2,1)}, bf16[256,1536]{1,0:T(8,128)(2,1)S(1)}, u32[]{:S(2)}, u32[]{:S(2)}) collective-permute-start(bf16[256,1536]{1,0:T(8,128)(2,1)} %get-tuple-element.143.refs_13_.refs_24_), channel_id=1, source_target_pairs={{0,8},{4,12},{8,0},{12,4},{16,24},{20,28},{24,16},{28,20},{1,9},{5... | collective-permute-start | bytes 2359304 | tf_op jit(solution)/shard_map/ppermute | solution.py:24
  446.5 22.5 %collective-permute-start.63 = (bf16[256,1536]{1,0:T(8,128)(2,1)}, bf16[256,1536]{1,0:T(8,128)(2,1)}, u32[]{:S(2)}, u32[]{:S(2)}) collective-permute-start(bf16[256,1536]{1,0:T(8,128)(2,1)} %get-tuple-element.143.refs_13_.refs_24_), channel_id=1, source_target_pairs={{4,16},{12,24},{16,4},{24,12},{5,17},{13,25},{17,5},{25,13},{6,18}... | collective-permute-start | bytes 2359304 | tf_op jit(solution)/shard_map/ppermute | solution.py:24
  474.1 20.6 %collective-permute-start.65 = (bf16[256,1536]{1,0:T(8,128)(2,1)S(1)}, bf16[256,1536]{1,0:T(8,128)(2,1)S(1)}, u32[]{:S(2)}, u32[]{:S(2)}) collective-permute-start(bf16[256,1536]{1,0:T(8,128)(2,1)S(1)} %collective-permute-done.62.refs_4_.refs_10_), channel_id=1, source_target_pairs={{0,16},{4,20},{24,8},{28,12},{1,17},{5,21},{25,9},{29,13},{2,18},{... | collective-permute-start | bytes 2359304 | tf_op jit(solution)/shard_map/ppermute | solution.py:24
  517.0 14.0 %collective-permute-start.76 = (bf16[256,768]{1,0:T(8,128)(2,1)}, bf16[256,768]{1,0:T(8,128)(2,1)S(1)}, u32[]{:S(2)}, u32[]{:S(2)}) collective-permute-start(bf16[256,768]{1,0:T(8,128)(2,1)} %get-tuple-element.156), channel_id=1, source_target_pairs={{0,1},{1,2},{2,3},{3,0},{4,5},{5,6},{6,7},{7,4},{8,9},{9,10},{10,1... | collective-permute-start | bytes 1179656 | tf_op jit(solution)/shard_map/ppermute | solution.py:24
  517.0 22.4 %collective-permute-start.72 = (bf16[256,768]{1,0:T(8,128)(2,1)}, bf16[256,768]{1,0:T(8,128)(2,1)S(1)}, u32[]{:S(2)}, u32[]{:S(2)}) collective-permute-start(bf16[256,768]{1,0:T(8,128)(2,1)} %get-tuple-element.154), channel_id=1, source_target_pairs={{0,1},{1,2},{2,3},{3,0},{4,5},{5,6},{6,7},{7,4},{8,9},{9,10},{10,1... | collective-permute-start | bytes 1179656 | tf_op jit(solution)/shard_map/ppermute | solution.py:24
  519.0 28.8 %collective-permute-start.68 = (bf16[256,768]{1,0:T(8,128)(2,1)}, bf16[256,768]{1,0:T(8,128)(2,1)S(1)}, u32[]{:S(2)}, u32[]{:S(2)}) collective-permute-start(bf16[256,768]{1,0:T(8,128)(2,1)} %get-tuple-element.152), channel_id=1, source_target_pairs={{0,1},{1,2},{2,3},{3,0},{4,5},{5,6},{6,7},{7,4},{8,9},{9,10},{10,1... | collective-permute-start | bytes 1179656 | tf_op jit(solution)/shard_map/ppermute | solution.py:24
  533.7 22.5 %collective-permute-start.77 = (bf16[256,768]{1,0:T(8,128)(2,1)}, bf16[256,768]{1,0:T(8,128)(2,1)S(1)}, u32[]{:S(2)}, u32[]{:S(2)}) collective-permute-start(bf16[256,768]{1,0:T(8,128)(2,1)} %add_share.27), channel_id=1, source_target_pairs={{0,1},{1,2},{2,3},{3,0},{4,5},{5,6},{6,7},{7,4},{8,9},{9,10},{10,1... | collective-permute-start | bytes 1179656 | tf_op jit(solution)/shard_map/ppermute | solution.py:24
  542.1 22.5 %collective-permute-start.73 = (bf16[256,768]{1,0:T(8,128)(2,1)}, bf16[256,768]{1,0:T(8,128)(2,1)S(1)}, u32[]{:S(2)}, u32[]{:S(2)}) collective-permute-start(bf16[256,768]{1,0:T(8,128)(2,1)} %add_share.24), channel_id=1, source_target_pairs={{0,1},{1,2},{2,3},{3,0},{4,5},{5,6},{6,7},{7,4},{8,9},{9,10},{10,1... | collective-permute-start | bytes 1179656 | tf_op jit(solution)/shard_map/ppermute | solution.py:24
  542.1 58.3 %collective-permute-start.67 = (f32[256,768]{1,0:T(8,128)S(1)}, f32[256,768]{1,0:T(8,128)S(1)}, u32[]{:S(2)}, u32[]{:S(2)}) collective-permute-start(f32[256,768]{1,0:T(8,128)S(1)} %copy-done.31), channel_id=1, source_target_pairs={{0,4},{4,8},{8,12},{12,16},{16,20},{20,24},{24,28},{28,0},{1,5},{5... | collective-permute-start | bytes 2359304 | tf_op jit(solution)/shard_map/ppermute | solution.py:24
  550.6 22.6 %collective-permute-start.69 = (bf16[256,768]{1,0:T(8,128)(2,1)}, bf16[256,768]{1,0:T(8,128)(2,1)S(1)}, u32[]{:S(2)}, u32[]{:S(2)}) collective-permute-start(bf16[256,768]{1,0:T(8,128)(2,1)} %add_share.21), channel_id=1, source_target_pairs={{0,1},{1,2},{2,3},{3,0},{4,5},{5,6},{6,7},{7,4},{8,9},{9,10},{10,1... | collective-permute-start | bytes 1179656 | tf_op jit(solution)/shard_map/ppermute | solution.py:24
  559.0 22.6 %collective-permute-start.78 = (bf16[256,768]{1,0:T(8,128)(2,1)}, bf16[256,768]{1,0:T(8,128)(2,1)S(1)}, u32[]{:S(2)}, u32[]{:S(2)}) collective-permute-start(bf16[256,768]{1,0:T(8,128)(2,1)} %add_share.28), channel_id=1, source_target_pairs={{0,1},{1,2},{2,3},{3,0},{4,5},{5,6},{6,7},{7,4},{8,9},{9,10},{10,1... | collective-permute-start | bytes 1179656 | tf_op jit(solution)/shard_map/ppermute | solution.py:24
  559.0 41.4 %collective-permute-start.71 = (f32[256,768]{1,0:T(8,128)S(1)}, f32[256,768]{1,0:T(8,128)S(1)}, u32[]{:S(2)}, u32[]{:S(2)}) collective-permute-start(f32[256,768]{1,0:T(8,128)S(1)} %copy-done.32), channel_id=1, source_target_pairs={{0,4},{4,8},{8,12},{12,16},{16,20},{20,24},{24,28},{28,0},{1,5},{5... | collective-permute-start | bytes 2359304 | tf_op jit(solution)/shard_map/ppermute | solution.py:24
  564.7 35.7 %collective-permute-start.75 = (f32[256,768]{1,0:T(8,128)S(1)}, f32[256,768]{1,0:T(8,128)S(1)}, u32[]{:S(2)}, u32[]{:S(2)}) collective-permute-start(f32[256,768]{1,0:T(8,128)S(1)} %copy-done.33), channel_id=1, source_target_pairs={{0,4},{4,8},{8,12},{12,16},{16,20},{20,24},{24,28},{28,0},{1,5},{5... | collective-permute-start | bytes 2359304 | tf_op jit(solution)/shard_map/ppermute | solution.py:24
  573.1 16.9 %collective-permute-start.74 = (bf16[256,768]{1,0:T(8,128)(2,1)}, bf16[256,768]{1,0:T(8,128)(2,1)S(1)}, u32[]{:S(2)}, u32[]{:S(2)}) collective-permute-start(bf16[256,768]{1,0:T(8,128)(2,1)} %add_share.25), channel_id=1, source_target_pairs={{0,1},{1,2},{2,3},{3,0},{4,5},{5,6},{6,7},{7,4},{8,9},{9,10},{10,1... | collective-permute-start | bytes 1179656 | tf_op jit(solution)/shard_map/ppermute | solution.py:24
  581.5 16.0 %collective-permute-start.70 = (bf16[256,768]{1,0:T(8,128)(2,1)}, bf16[256,768]{1,0:T(8,128)(2,1)S(1)}, u32[]{:S(2)}, u32[]{:S(2)}) collective-permute-start(bf16[256,768]{1,0:T(8,128)(2,1)} %add_share.22), channel_id=1, source_target_pairs={{0,1},{1,2},{2,3},{3,0},{4,5},{5,6},{6,7},{7,4},{8,9},{9,10},{10,1... | collective-permute-start | bytes 1179656 | tf_op jit(solution)/shard_map/ppermute | solution.py:24
  (102 other events, 1014.7 us)

commit v4 on v3

--- a/solution.py
+++ b/solution.py
@@ -484,8 +484,8 @@
             last = hop == tensor_count - 2
             for j in range(CHUNKS):
                 totals[j] = ring(totals[j])
-                if not (last and turning):
-                    totals[j] = add_share(totals[j], others, hop, j, jnp.float32 if last else jnp.bfloat16)
+                if not last:
+                    totals[j] = add_share(totals[j], others, hop, j, jnp.bfloat16)
         if turning:
             kept, normed = [], []
             for j in range(CHUNKS):
@@ -502,7 +502,10 @@
                 )
                 kept.append(block)
                 normed.append(onward(normalize_turned(block, sums, next_rows, full_width)))
-    advanced = [latents[j] + step_size * (latents[j] + gate * totals[j]) for j in range(CHUNKS)]
+    advanced = []
+    for j in range(CHUNKS):
+        total = totals[j].astype(jnp.float32) + chunk(others[tensor_count - 2], j).astype(jnp.float32)
+        advanced.append(latents[j] + step_size * (latents[j] + gate * total))
     return jnp.concatenate(advanced, axis=0)
 
 

time: 615 us -> 613 us (level)
    pallas_call x15 -> x12, Pallas kernels: 29.8 us -> 23.6 us  [add_share(): pl.pallas_call(add_kernel, grid=(1,), in_specs=[pl.BlockSpec((rows, colum...]
    unnamed x174 -> x164, local copies, waits for them, and re-layouts: 25.1 us -> 22.9 us
  transfers between devices with their start and end apart: 79 -> 79, of which waited for: 45 -> 45; matrix products, arithmetic and copies ran while one was open for 1% -> 1% of each run, Pallas kernels for 31% -> 30%
where the time goes in v4:
time: 613 us; the launch traced here: 603 us
  waiting for transfers between devices  261 us (43%)
  Pallas kernels  211 us (34%)
  starting transfers between devices  79.4 us (13%)
  local copies, waits for them, and re-layouts  25.3 us (4%)
  other arithmetic  22.3 us (4%)
    ppermute x79, waiting for transfers between devices, permute(): return lax.ppermute(block, axis, pairs)  261 us
    pallas_call x6, Pallas kernels, attend(): pl.pallas_call(functools.partial(attend_kernel, chunks, marks, first, las...  85 us
    ppermute x79, starting transfers between devices, permute(): return lax.ppermute(block, axis, pairs)  79.4 us
    pallas_call x6, Pallas kernels, project(): pl.pallas_call(functools.partial(qkv_kernel, parts, columns // head_dim,...  63.6 us
    pallas_call x12, Pallas kernels, add_share(): pl.pallas_call(add_kernel, grid=(1,), in_specs=[pl.BlockSpec((rows, colum...  23.6 us
    pallas_call x4, Pallas kernels, shares(): pl.pallas_call(kernel, grid_spec=pltpu.PrefetchScalarGridSpec(num_scalar_...  23.1 us
    unnamed x164, local copies, waits for them, and re-layouts  22.9 us
  transfers between devices with their start and end apart: 79, of which 45 were waited for; matrix products, arithmetic and copies ran while one was open for 1% of the time, Pallas kernels for 30%

profile of v4, /device:TPU:0, one launch (start us, length us, event | category | flops | bytes accessed | tf_op | source)
XLA Modules:
  0.0 603.0 jit_solution(7642647348544403853)
XLA Ops:
  2.2 3.1 collective-permute-start
  16.6 12.7 %collective-permute-done.3.refs_1_ = bf16[256,768]{1,0:T(8,128)(2,1)S(1)} collective-permute-done((bf16[256,768]{1,0:T(8,128)(2,1)S(1)}, bf16[256,768]{1,0:T(8,128)(2,1)S(1)}, u32[]{:S(2)}, u32[]{:S(2)}) %collective-permute-start.3) | collective-permute-done | bytes 393248 | tf_op jit(solution)/shard_map/ppermute | solution.py:24
  29.4 12.6 %collective-permute-done.4.refs_2_ = bf16[256,768]{1,0:T(8,128)(2,1)S(1)} collective-permute-done((bf16[256,768]{1,0:T(8,128)(2,1)S(1)}, bf16[256,768]{1,0:T(8,128)(2,1)S(1)}, u32[]{:S(2)}, u32[]{:S(2)}) %collective-permute-start.4) | collective-permute-done | bytes 393248 | tf_op jit(solution)/shard_map/ppermute | solution.py:24
  42.0 13.8 %collective-permute-done.5.refs_3_ = bf16[256,768]{1,0:T(8,128)(2,1)S(1)} collective-permute-done((bf16[256,768]{1,0:T(8,128)(2,1)S(1)}, bf16[256,768]{1,0:T(8,128)(2,1)S(1)}, u32[]{:S(2)}, u32[]{:S(2)}) %collective-permute-start.5) | collective-permute-done | bytes 393248 | tf_op jit(solution)/shard_map/ppermute | solution.py:24
  55.9 6.3 %collective-permute-done.6.refs_1_ = bf16[256,768]{1,0:T(8,128)(2,1)S(1)} collective-permute-done((bf16[256,768]{1,0:T(8,128)(2,1)S(1)}, bf16[256,768]{1,0:T(8,128)(2,1)S(1)}, u32[]{:S(2)}, u32[]{:S(2)}) %collective-permute-start.6) | collective-permute-done | bytes 393248 | tf_op jit(solution)/shard_map/ppermute | solution.py:24
  62.8 10.6 %qkv.6 = (bf16[256,768]{1,0:T(8,128)(2,1)}, bf16[256,1536]{1,0:T(8,128)(2,1)}) custom-call(s32[4]{0:T(128)} %and_select_fusion.order_ref, f32[2,128]{1,0:T(2,128)} %gain_ref.11, bf16[256,768]{1,0:T(8,128)(2,1)} %copy-done.28, bf16[256,768]{1,0:T(8,128)(2,1)} %copy-done.46, bf16[256,768]{1,0:T(8,128)(2,1)} %copy-done.49, bf16[256,768]{1,0:T(8,128)(2,1)} %copy-done.52, ...), custom_call_target="tpu_custom_call" | custom-call | flops 1000 | bytes 1000 | tf_op jit(solution)/shard_map/qkv/pallas_call | solution.py:69
  75.7 13.2 %collective-permute-done.8.refs_3_ = bf16[256,768]{1,0:T(8,128)(2,1)S(1)} collective-permute-done((bf16[256,768]{1,0:T(8,128)(2,1)S(1)}, bf16[256,768]{1,0:T(8,128)(2,1)S(1)}, u32[]{:S(2)}, u32[]{:S(2)}) %collective-permute-start.8) | collective-permute-done | bytes 393248 | tf_op jit(solution)/shard_map/ppermute | solution.py:24
  88.9 5.9 collective-permute-done.9.refs_1_
  94.8 3.5 collective-permute-start.13
  98.3 10.6 %qkv.7 = (bf16[256,768]{1,0:T(8,128)(2,1)}, bf16[256,1536]{1,0:T(8,128)(2,1)}) custom-call(s32[4]{0:T(128)} %and_select_fusion.order_ref, f32[2,128]{1,0:T(2,128)} %gain_ref.11, bf16[256,768]{1,0:T(8,128)(2,1)} %copy-done.27, bf16[256,768]{1,0:T(8,128)(2,1)} %copy-done.42, bf16[256,768]{1,0:T(8,128)(2,1)} %copy-done.45, bf16[256,768]{1,0:T(8,128)(2,1)} %copy-done.50, ...), custom_call_target="tpu_custom_call" | custom-call | flops 1000 | bytes 1000 | tf_op jit(solution)/shard_map/qkv/pallas_call | solution.py:69
  109.3 9.8 %collective-permute-done.12.refs_3_ = bf16[256,768]{1,0:T(8,128)(2,1)S(1)} collective-permute-done((bf16[256,768]{1,0:T(8,128)(2,1)S(1)}, bf16[256,768]{1,0:T(8,128)(2,1)S(1)}, u32[]{:S(2)}, u32[]{:S(2)}) %collective-permute-start.12) | collective-permute-done | bytes 393248 | tf_op jit(solution)/shard_map/ppermute | solution.py:24
  123.4 10.6 %qkv.8 = (bf16[256,768]{1,0:T(8,128)(2,1)}, bf16[256,1536]{1,0:T(8,128)(2,1)}) custom-call(s32[4]{0:T(128)} %and_select_fusion.order_ref, f32[2,128]{1,0:T(2,128)} %gain_ref.11, bf16[256,768]{1,0:T(8,128)(2,1)} %copy-done.26, bf16[256,768]{1,0:T(8,128)(2,1)} %copy-done.41, bf16[256,768]{1,0:T(8,128)(2,1)} %copy-done.44, bf16[256,768]{1,0:T(8,128)(2,1)} %copy-done.48, ...), custom_call_target="tpu_custom_call" | custom-call | flops 1000 | bytes 1000 | tf_op jit(solution)/shard_map/qkv/pallas_call | solution.py:69
  134.0 7.3 %collective-permute-done.14.refs_11_.refs_22_ = bf16[256,1536]{1,0:T(8,128)(2,1)} collective-permute-done((bf16[256,1536]{1,0:T(8,128)(2,1)}, bf16[256,1536]{1,0:T(8,128)(2,1)}, u32[]{:S(2)}, u32[]{:S(2)}) %collective-permute-start.14) | collective-permute-done | bytes 786464 | tf_op jit(solution)/shard_map/ppermute | solution.py:24
  148.1 19.1 %attend.6.refs_15_ = f32[6,768,256]{2,1,0:T(8,128)} custom-call(s32[7]{0:T(128)} %and_convert_fusion.usable_ref, bf16[256,768]{1,0:T(8,128)(2,1)} %get-tuple-element.84.refs_0_, bf16[256,768]{1,0:T(8,128)(2,1)} %get-tuple-element.92.refs_1_, bf16[256,768]{1,0:T(8,128)(2,1)} %get-tuple-element.99.refs_2_, ...), custom_call_target="tpu_custom_call" | custom-call | flops 1000 | bytes 1000 | tf_op jit(solution)/shard_map/attend/pallas_call | solution.py:140
  169.3 4.1 collective-permute-start.21
  178.9 12.9 %attend.7.refs_11_ = f32[6,768,256]{2,1,0:T(8,128)} custom-call(s32[7]{0:T(128)} %and_convert_fusion.usable_ref, bf16[256,768]{1,0:T(8,128)(2,1)} %get-tuple-element.84.refs_0_, bf16[256,768]{1,0:T(8,128)(2,1)} %get-tuple-element.92.refs_1_, bf16[256,768]{1,0:T(8,128)(2,1)} %get-tuple-element.99.refs_2_, ...), custom_call_target="tpu_custom_call" | custom-call | flops 1000 | bytes 1000 | tf_op jit(solution)/shard_map/attend/pallas_call | solution.py:140
  192.9 3.0 pad_maximum_fusion.2
  196.5 4.1 collective-permute-done.23.refs_4_.refs_5_.refs_6_.refs_8_.refs_9_.refs_10_
  202.1 10.4 %attend.8.attended_ref = bf16[768,768]{1,0:T(8,128)(2,1)} custom-call(s32[7]{0:T(128)} %and_convert_fusion.usable_ref, bf16[256,768]{1,0:T(8,128)(2,1)} %get-tuple-element.84.refs_0_, bf16[256,768]{1,0:T(8,128)(2,1)} %get-tuple-element.92.refs_1_, bf16[256,768]{1,0:T(8,128)(2,1)} %get-tuple-element.99.refs_2_, bf16[256,1536]{1,0:T(8,128)(2,1)} %copy-done.7, ...), custom_call_target="tpu_custom_call" | custom-call | flops 1000 | bytes 1000 | tf_op jit(solution)/shard_map/attend/pallas_call | solution.py:140
  212.5 4.4 shares.4
  217.5 7.2 %shares.5.share_ref = bf16[3,768,768]{2,1,0:T(8,128)(2,1)} custom-call(s32[3]{0:T(128)} %slice.72.order_ref, bf16[768,768]{1,0:T(8,128)(2,1)} %attend.8.attended_ref, bf16[768,3072]{1,0:T(8,128)(2,1)} %weight_ref.7), custom_call_target="tpu_custom_call" | custom-call | flops 1000 | bytes 1000 | tf_op jit(solution)/shard_map/shares/pallas_call | solution.py:187
  224.7 5.3 collective-permute-done.24.total_ref
  232.8 14.0 %collective-permute-done.25.total_ref = bf16[256,768]{1,0:T(8,128)(2,1)S(1)} collective-permute-done((bf16[256,768]{1,0:T(8,128)(2,1)}, bf16[256,768]{1,0:T(8,128)(2,1)S(1)}, u32[]{:S(2)}, u32[]{:S(2)}) %collective-permute-start.25) | collective-permute-done | bytes 393248 | tf_op jit(solution)/shard_map/ppermute | solution.py:24
  251.3 4.0 collective-permute-done.27.total_ref
  258.0 5.7 collective-permute-done.26.total_ref
  267.4 3.6 collective-permute-start.36
  281.1 3.5 collective-permute-done.37.refs_0_
  286.6 5.1 collective-permute-done.29.total_ref
  292.5 2.8 turn.4
  303.1 5.9 collective-permute-done.40.refs_1_
  312.0 9.8 %collective-permute-start.43 = (bf16[256,768]{1,0:T(8,128)(2,1)}, bf16[256,768]{1,0:T(8,128)(2,1)S(1)}, u32[]{:S(2)}, u32[]{:S(2)}) collective-permute-start(bf16[256,768]{1,0:T(8,128)(2,1)} %normalize.4), channel_id=1, source_target_pairs={{0,4},{4,8},{8,12},{12,16},{16,20},{20,24},{24,28},{28,0},{1,5},{5... | collective-permute-start | bytes 1179656 | tf_op jit(solution)/shard_map/ppermute | solution.py:24
  325.4 2.9 collective-permute-done.43.refs_0_
  328.3 7.3 %collective-permute-done.39.refs_2_ = bf16[256,768]{1,0:T(8,128)(2,1)S(1)} collective-permute-done((bf16[256,768]{1,0:T(8,128)(2,1)S(1)}, bf16[256,768]{1,0:T(8,128)(2,1)S(1)}, u32[]{:S(2)}, u32[]{:S(2)}) %collective-permute-start.39) | collective-permute-done | bytes 393248 | tf_op jit(solution)/shard_map/ppermute | solution.py:24
  335.6 8.4 %collective-permute-done.32.total_ref = bf16[256,768]{1,0:T(8,128)(2,1)S(1)} collective-permute-done((bf16[256,768]{1,0:T(8,128)(2,1)}, bf16[256,768]{1,0:T(8,128)(2,1)S(1)}, u32[]{:S(2)}, u32[]{:S(2)}) %collective-permute-start.32) | collective-permute-done | bytes 393248 | tf_op jit(solution)/shard_map/ppermute | solution.py:24
  344.7 2.7 turn.5
  347.7 3.6 collective-permute-start.49
  352.6 7.7 %collective-permute-done.45.refs_1_ = bf16[256,768]{1,0:T(8,128)(2,1)S(1)} collective-permute-done((bf16[256,768]{1,0:T(8,128)(2,1)S(1)}, bf16[256,768]{1,0:T(8,128)(2,1)S(1)}, u32[]{:S(2)}, u32[]{:S(2)}) %collective-permute-start.45) | collective-permute-done | bytes 393248 | tf_op jit(solution)/shard_map/ppermute | solution.py:24
  363.5 10.6 %qkv.9 = (bf16[256,768]{1,0:T(8,128)(2,1)}, bf16[256,1536]{1,0:T(8,128)(2,1)}) custom-call(s32[4]{0:T(128)} %and_select_fusion.order_ref, f32[2,128]{1,0:T(2,128)} %gain_ref.11, bf16[256,768]{1,0:T(8,128)(2,1)} %copy-done.32, bf16[256,768]{1,0:T(8,128)(2,1)} %copy-done.33, bf16[256,768]{1,0:T(8,128)(2,1)} %copy-done.37, bf16[256,768]{1,0:T(8,128)(2,1)} %copy-done.39, ...), custom_call_target="tpu_custom_call" | custom-call | flops 1000 | bytes 1000 | tf_op jit(solution)/shard_map/qkv/pallas_call | solution.py:69
  374.1 2.9 collective-permute-start.53
  378.7 9.6 %collective-permute-done.51.refs_3_ = bf16[256,768]{1,0:T(8,128)(2,1)S(1)} collective-permute-done((bf16[256,768]{1,0:T(8,128)(2,1)S(1)}, bf16[256,768]{1,0:T(8,128)(2,1)S(1)}, u32[]{:S(2)}, u32[]{:S(2)}) %collective-permute-start.51) | collective-permute-done | bytes 393248 | tf_op jit(solution)/shard_map/ppermute | solution.py:24
  388.3 8.4 %collective-permute-done.52.refs_1_ = bf16[256,768]{1,0:T(8,128)(2,1)S(1)} collective-permute-done((bf16[256,768]{1,0:T(8,128)(2,1)S(1)}, bf16[256,768]{1,0:T(8,128)(2,1)S(1)}, u32[]{:S(2)}, u32[]{:S(2)}) %collective-permute-start.52) | collective-permute-done | bytes 393248 | tf_op jit(solution)/shard_map/ppermute | solution.py:24
  396.7 4.3 collective-permute-start.56
  401.1 10.6 %qkv.10 = (bf16[256,768]{1,0:T(8,128)(2,1)}, bf16[256,1536]{1,0:T(8,128)(2,1)}) custom-call(s32[4]{0:T(128)} %and_select_fusion.order_ref, f32[2,128]{1,0:T(2,128)} %gain_ref.11, bf16[256,768]{1,0:T(8,128)(2,1)} %copy-done.34, bf16[256,768]{1,0:T(8,128)(2,1)} %copy-done.35, bf16[256,768]{1,0:T(8,128)(2,1)} %copy-done.38, bf16[256,768]{1,0:T(8,128)(2,1)} %copy-done.51, ...), custom_call_target="tpu_custom_call" | custom-call | flops 1000 | bytes 1000 | tf_op jit(solution)/shard_map/qkv/pallas_call | solution.py:69
  411.8 12.4 %collective-permute-done.55.refs_3_ = bf16[256,768]{1,0:T(8,128)(2,1)S(1)} collective-permute-done((bf16[256,768]{1,0:T(8,128)(2,1)S(1)}, bf16[256,768]{1,0:T(8,128)(2,1)S(1)}, u32[]{:S(2)}, u32[]{:S(2)}) %collective-permute-start.55) | collective-permute-done | bytes 393248 | tf_op jit(solution)/shard_map/ppermute | solution.py:24
  427.5 10.6 %qkv.11 = (bf16[256,768]{1,0:T(8,128)(2,1)}, bf16[256,1536]{1,0:T(8,128)(2,1)}) custom-call(s32[4]{0:T(128)} %and_select_fusion.order_ref, f32[2,128]{1,0:T(2,128)} %gain_ref.11, bf16[256,768]{1,0:T(8,128)(2,1)} %copy-done.36, bf16[256,768]{1,0:T(8,128)(2,1)} %copy-done.40, bf16[256,768]{1,0:T(8,128)(2,1)} %copy-done.43, bf16[256,768]{1,0:T(8,128)(2,1)} %copy-done.47, ...), custom_call_target="tpu_custom_call" | custom-call | flops 1000 | bytes 1000 | tf_op jit(solution)/shard_map/qkv/pallas_call | solution.py:69
  438.2 7.8 %collective-permute-done.57.refs_11_.refs_22_ = bf16[256,1536]{1,0:T(8,128)(2,1)S(1)} collective-permute-done((bf16[256,1536]{1,0:T(8,128)(2,1)S(1)}, bf16[256,1536]{1,0:T(8,128)(2,1)S(1)}, u32[]{:S(2)}, u32[]{:S(2)}) %collective-permute-start.57) | collective-permute-done | bytes 786464 | tf_op jit(solution)/shard_map/ppermute | solution.py:24
  450.8 19.3 %attend.9.refs_15_ = f32[6,768,256]{2,1,0:T(8,128)} custom-call(s32[7]{0:T(128)} %and_convert_fusion.usable_ref, bf16[256,768]{1,0:T(8,128)(2,1)} %get-tuple-element.122.refs_0_, bf16[256,768]{1,0:T(8,128)(2,1)} %get-tuple-element.131.refs_1_, bf16[256,768]{1,0:T(8,128)(2,1)} %get-tuple-element.138.refs_2_, ...), custom_call_target="tpu_custom_call" | custom-call | flops 1000 | bytes 1000 | tf_op jit(solution)/shard_map/attend/pallas_call | solution.py:140
  472.0 3.2 collective-permute-start.64
  475.2 3.4 collective-permute-start.65
  480.8 12.9 %attend.10.refs_11_ = f32[6,768,256]{2,1,0:T(8,128)} custom-call(s32[7]{0:T(128)} %and_convert_fusion.usable_ref, bf16[256,768]{1,0:T(8,128)(2,1)} %get-tuple-element.122.refs_0_, bf16[256,768]{1,0:T(8,128)(2,1)} %get-tuple-element.131.refs_1_, bf16[256,768]{1,0:T(8,128)(2,1)} %get-tuple-element.138.refs_2_, bf16[256,1536]{1,0:T(8,128)(2,1)} %copy-done.21, ...), custom_call_target="tpu_custom_call" | custom-call | flops 1000 | bytes 1000 | tf_op jit(solution)/shard_map/attend/pallas_call | solution.py:140
  497.5 4.5 collective-permute-done.66.refs_4_.refs_5_.refs_6_.refs_8_.refs_9_.refs_10_
  503.4 10.4 %attend.11.attended_ref = bf16[768,768]{1,0:T(8,128)(2,1)} custom-call(s32[7]{0:T(128)} %and_convert_fusion.usable_ref, bf16[256,768]{1,0:T(8,128)(2,1)} %get-tuple-element.122.refs_0_, bf16[256,768]{1,0:T(8,128)(2,1)} %get-tuple-element.131.refs_1_, bf16[256,768]{1,0:T(8,128)(2,1)} %get-tuple-element.138.refs_2_, bf16[256,1536]{1,0:T(8,128)(2,1)} %copy-done.8, ...), custom_call_target="tpu_custom_call" | custom-call | flops 1000 | bytes 1000 | tf_op jit(solution)/shard_map/attend/pallas_call | solution.py:140
  513.9 4.3 shares.6
  521.2 7.2 %shares.7.share_ref = bf16[3,768,768]{2,1,0:T(8,128)(2,1)} custom-call(s32[3]{0:T(128)} %slice.72.order_ref, bf16[768,768]{1,0:T(8,128)(2,1)} %attend.11.attended_ref, bf16[768,3072]{1,0:T(8,128)(2,1)} %weight_ref.7), custom_call_target="tpu_custom_call" | custom-call | flops 1000 | bytes 1000 | tf_op jit(solution)/shard_map/shares/pallas_call | solution.py:187
  528.5 3.6 collective-permute-done.72.total_ref
  534.8 2.9 collective-permute-start.71
  537.7 2.8 collective-permute-done.76.total_ref
  543.3 5.7 collective-permute-done.68.total_ref
  551.7 5.7 collective-permute-done.73.total_ref
  560.1 5.7 collective-permute-done.77.total_ref
  568.5 5.7 collective-permute-done.69.total_ref
  577.0 5.7 collective-permute-done.74
  582.6 8.4 %collective-permute-done.78 = bf16[256,768]{1,0:T(8,128)(2,1)S(1)} collective-permute-done((bf16[256,768]{1,0:T(8,128)(2,1)}, bf16[256,768]{1,0:T(8,128)(2,1)S(1)}, u32[]{:S(2)}, u32[]{:S(2)}) %collective-permute-start.78) | collective-permute-done | bytes 393248 | tf_op jit(solution)/shard_map/ppermute | solution.py:24
  591.1 7.6 %collective-permute-done.70 = bf16[256,768]{1,0:T(8,128)(2,1)S(1)} collective-permute-done((bf16[256,768]{1,0:T(8,128)(2,1)}, bf16[256,768]{1,0:T(8,128)(2,1)S(1)}, u32[]{:S(2)}, u32[]{:S(2)}) %collective-permute-start.70) | collective-permute-done | bytes 393248 | tf_op jit(solution)/shard_map/ppermute | solution.py:24
  (318 shorter events, 124.3 us)
Async XLA Ops:
  2.2 13.1 %collective-permute-start = (f32[2,768]{1,0:T(2,128)S(1)}, f32[2,768]{1,0:T(2,128)S(1)}, u32[]{:S(2)}, u32[]{:S(2)}) collective-permute-start(f32[2,768]{1,0:T(2,128)S(1)} %pad_maximum_fusion.7), channel_id=1, source_target_pairs={{0,1},{1,2},{2,3},{3,0},{4,5},{5,6},{6,7},{7,4},{8,9},{9,10},{10,1... | collective-permute-start | bytes 18440 | tf_op jit(solution)/shard_map/ppermute | solution.py:24
  15.9 13.5 %collective-permute-start.3 = (bf16[256,768]{1,0:T(8,128)(2,1)S(1)}, bf16[256,768]{1,0:T(8,128)(2,1)S(1)}, u32[]{:S(2)}, u32[]{:S(2)}) collective-permute-start(bf16[256,768]{1,0:T(8,128)(2,1)S(1)} %get-tuple-element.168.refs_0_), channel_id=1, source_target_pairs={{0,1},{1,2},{2,3},{3,0},{4,5},{5,6},{6,7},{7,4},{8,9},{9,10},{10,1... | collective-permute-start | bytes 1179656 | tf_op jit(solution)/shard_map/ppermute | solution.py:24
  29.4 12.6 %collective-permute-start.4 = (bf16[256,768]{1,0:T(8,128)(2,1)S(1)}, bf16[256,768]{1,0:T(8,128)(2,1)S(1)}, u32[]{:S(2)}, u32[]{:S(2)}) collective-permute-start(bf16[256,768]{1,0:T(8,128)(2,1)S(1)} %collective-permute-done.3.refs_1_), channel_id=1, source_target_pairs={{0,1},{1,2},{2,3},{3,0},{4,5},{5,6},{6,7},{7,4},{8,9},{9,10},{10,1... | collective-permute-start | bytes 1179656 | tf_op jit(solution)/shard_map/ppermute | solution.py:24
  42.0 13.8 %collective-permute-start.5 = (bf16[256,768]{1,0:T(8,128)(2,1)S(1)}, bf16[256,768]{1,0:T(8,128)(2,1)S(1)}, u32[]{:S(2)}, u32[]{:S(2)}) collective-permute-start(bf16[256,768]{1,0:T(8,128)(2,1)S(1)} %collective-permute-done.4.refs_2_), channel_id=1, source_target_pairs={{0,1},{1,2},{2,3},{3,0},{4,5},{5,6},{6,7},{7,4},{8,9},{9,10},{10,1... | collective-permute-start | bytes 1179656 | tf_op jit(solution)/shard_map/ppermute | solution.py:24
  42.0 20.2 %collective-permute-start.6 = (bf16[256,768]{1,0:T(8,128)(2,1)S(1)}, bf16[256,768]{1,0:T(8,128)(2,1)S(1)}, u32[]{:S(2)}, u32[]{:S(2)}) collective-permute-start(bf16[256,768]{1,0:T(8,128)(2,1)S(1)} %get-tuple-element.82.refs_0_), channel_id=1, source_target_pairs={{0,1},{1,2},{2,3},{3,0},{4,5},{5,6},{6,7},{7,4},{8,9},{9,10},{10,1... | collective-permute-start | bytes 1179656 | tf_op jit(solution)/shard_map/ppermute | solution.py:24
  62.2 12.8 %collective-permute-start.7 = (bf16[256,768]{1,0:T(8,128)(2,1)S(1)}, bf16[256,768]{1,0:T(8,128)(2,1)S(1)}, u32[]{:S(2)}, u32[]{:S(2)}) collective-permute-start(bf16[256,768]{1,0:T(8,128)(2,1)S(1)} %collective-permute-done.6.refs_1_), channel_id=1, source_target_pairs={{0,1},{1,2},{2,3},{3,0},{4,5},{5,6},{6,7},{7,4},{8,9},{9,10},{10,1... | collective-permute-start | bytes 1179656 | tf_op jit(solution)/shard_map/ppermute | solution.py:24
  73.4 21.4 %collective-permute-start.10 = (bf16[256,1536]{1,0:T(8,128)(2,1)}, bf16[256,1536]{1,0:T(8,128)(2,1)S(1)}, u32[]{:S(2)}, u32[]{:S(2)}) collective-permute-start(bf16[256,1536]{1,0:T(8,128)(2,1)} %get-tuple-element.100.refs_3_.refs_14_), channel_id=1, source_target_pairs={{0,8},{4,12},{8,0},{12,4},{16,24},{20,28},{24,16},{28,20},{1,9},{5... | collective-permute-start | bytes 2359304 | tf_op jit(solution)/shard_map/ppermute | solution.py:24
  75.0 13.8 %collective-permute-start.8 = (bf16[256,768]{1,0:T(8,128)(2,1)S(1)}, bf16[256,768]{1,0:T(8,128)(2,1)S(1)}, u32[]{:S(2)}, u32[]{:S(2)}) collective-permute-start(bf16[256,768]{1,0:T(8,128)(2,1)S(1)} %collective-permute-done.7.refs_2_), channel_id=1, source_target_pairs={{0,1},{1,2},{2,3},{3,0},{4,5},{5,6},{6,7},{7,4},{8,9},{9,10},{10,1... | collective-permute-start | bytes 1179656 | tf_op jit(solution)/shard_map/ppermute | solution.py:24
  75.1 19.7 %collective-permute-start.9 = (bf16[256,768]{1,0:T(8,128)(2,1)S(1)}, bf16[256,768]{1,0:T(8,128)(2,1)S(1)}, u32[]{:S(2)}, u32[]{:S(2)}) collective-permute-start(bf16[256,768]{1,0:T(8,128)(2,1)S(1)} %get-tuple-element.89.refs_0_), channel_id=1, source_target_pairs={{0,1},{1,2},{2,3},{3,0},{4,5},{5,6},{6,7},{7,4},{8,9},{9,10},{10,1... | collective-permute-start | bytes 1179656 | tf_op jit(solution)/shard_map/ppermute | solution.py:24
  94.8 14.1 %collective-permute-start.11 = (bf16[256,768]{1,0:T(8,128)(2,1)S(1)}, bf16[256,768]{1,0:T(8,128)(2,1)S(1)}, u32[]{:S(2)}, u32[]{:S(2)}) collective-permute-start(bf16[256,768]{1,0:T(8,128)(2,1)S(1)} %collective-permute-done.9.refs_1_), channel_id=1, source_target_pairs={{0,1},{1,2},{2,3},{3,0},{4,5},{5,6},{6,7},{7,4},{8,9},{9,10},{10,1... | collective-permute-start | bytes 1179656 | tf_op jit(solution)/shard_map/ppermute | solution.py:24
  94.8 24.3 %collective-permute-start.13 = (bf16[256,1536]{1,0:T(8,128)(2,1)S(1)}, bf16[256,1536]{1,0:T(8,128)(2,1)S(1)}, u32[]{:S(2)}, u32[]{:S(2)}) collective-permute-start(bf16[256,1536]{1,0:T(8,128)(2,1)S(1)} %collective-permute-done.10.refs_5_.refs_16_), channel_id=1, source_target_pairs={{0,16},{4,20},{24,8},{28,12},{1,17},{5,21},{25,9},{29,13},{2,18},{... | collective-permute-start | bytes 2359304 | tf_op jit(solution)/shard_map/ppermute | solution.py:24
  121.0 25.7 %collective-permute-start.15 = (bf16[768,1536]{1,0:T(8,128)(2,1)}, bf16[768,1536]{1,0:T(8,128)(2,1)S(1)}, u32[]{:S(2)}, u32[]{:S(2)}) collective-permute-start(bf16[768,1536]{1,0:T(8,128)(2,1)} %pad_maximum_fusion), channel_id=1, source_target_pairs={{0,4},{4,0},{8,12},{12,8},{16,20},{20,16},{24,28},{28,24},{1,5},{5... | collective-permute-start | bytes 7077896 | tf_op jit(solution)/shard_map/ppermute | solution.py:24
  121.0 20.3 %collective-permute-start.14 = (bf16[256,1536]{1,0:T(8,128)(2,1)}, bf16[256,1536]{1,0:T(8,128)(2,1)}, u32[]{:S(2)}, u32[]{:S(2)}) collective-permute-start(bf16[256,1536]{1,0:T(8,128)(2,1)} %get-tuple-element.102.refs_10_.refs_21_), channel_id=1, source_target_pairs={{0,8},{4,12},{8,0},{12,4},{16,24},{20,28},{24,16},{28,20},{1,9},{5... | collective-permute-start | bytes 2359304 | tf_op jit(solution)/shard_map/ppermute | solution.py:24
  121.1 22.6 %collective-permute-start.16 = (bf16[256,1536]{1,0:T(8,128)(2,1)S(1)}, bf16[256,1536]{1,0:T(8,128)(2,1)S(1)}, u32[]{:S(2)}, u32[]{:S(2)}) collective-permute-start(bf16[256,1536]{1,0:T(8,128)(2,1)S(1)} %copy-done.9), channel_id=1, source_target_pairs={{4,16},{12,24},{16,4},{24,12},{5,17},{13,25},{17,5},{25,13},{6,18}... | collective-permute-start | bytes 2359304 | tf_op jit(solution)/shard_map/ppermute | solution.py:24
  121.8 24.9 %collective-permute-start.17 = (bf16[256,1536]{1,0:T(8,128)(2,1)}, bf16[256,1536]{1,0:T(8,128)(2,1)}, u32[]{:S(2)}, u32[]{:S(2)}) collective-permute-start(bf16[256,1536]{1,0:T(8,128)(2,1)} %get-tuple-element.102.refs_10_.refs_21_), channel_id=1, source_target_pairs={{4,16},{12,24},{16,4},{24,12},{5,17},{13,25},{17,5},{25,13},{6,18}... | collective-permute-start | bytes 2359304 | tf_op jit(solution)/shard_map/ppermute | solution.py:24
  141.3 25.9 %collective-permute-start.18 = (bf16[256,1536]{1,0:T(8,128)(2,1)}, bf16[256,1536]{1,0:T(8,128)(2,1)}, u32[]{:S(2)}, u32[]{:S(2)}) collective-permute-start(bf16[256,1536]{1,0:T(8,128)(2,1)} %collective-permute-done.14.refs_11_.refs_22_), channel_id=1, source_target_pairs={{0,16},{4,20},{24,8},{28,12},{1,17},{5,21},{25,9},{29,13},{2,18},{... | collective-permute-start | bytes 2359304 | tf_op jit(solution)/shard_map/ppermute | solution.py:24
  143.7 23.5 %collective-permute-start.19 = (bf16[256,1536]{1,0:T(8,128)(2,1)}, bf16[256,1536]{1,0:T(8,128)(2,1)}, u32[]{:S(2)}, u32[]{:S(2)}) collective-permute-start(bf16[256,1536]{1,0:T(8,128)(2,1)} %get-tuple-element.104.refs_13_.refs_24_), channel_id=1, source_target_pairs={{0,8},{4,12},{8,0},{12,4},{16,24},{20,28},{24,16},{28,20},{1,9},{5... | collective-permute-start | bytes 2359304 | tf_op jit(solution)/shard_map/ppermute | solution.py:24
  144.6 22.6 %collective-permute-start.20 = (bf16[256,1536]{1,0:T(8,128)(2,1)}, bf16[256,1536]{1,0:T(8,128)(2,1)S(1)}, u32[]{:S(2)}, u32[]{:S(2)}) collective-permute-start(bf16[256,1536]{1,0:T(8,128)(2,1)} %get-tuple-element.104.refs_13_.refs_24_), channel_id=1, source_target_pairs={{4,16},{12,24},{16,4},{24,12},{5,17},{13,25},{17,5},{25,13},{6,18}... | collective-permute-start | bytes 2359304 | tf_op jit(solution)/shard_map/ppermute | solution.py:24
  173.4 19.6 %collective-permute-start.22 = (bf16[256,1536]{1,0:T(8,128)(2,1)}, bf16[256,1536]{1,0:T(8,128)(2,1)S(1)}, u32[]{:S(2)}, u32[]{:S(2)}) collective-permute-start(bf16[256,1536]{1,0:T(8,128)(2,1)} %collective-permute-done.19.refs_4_.refs_10_), channel_id=1, source_target_pairs={{0,16},{4,20},{24,8},{28,12},{1,17},{5,21},{25,9},{29,13},{2,18},{... | collective-permute-start | bytes 2359304 | tf_op jit(solution)/shard_map/ppermute | solution.py:24
  216.9 13.2 %collective-permute-start.24 = (bf16[256,768]{1,0:T(8,128)(2,1)}, bf16[256,768]{1,0:T(8,128)(2,1)S(1)}, u32[]{:S(2)}, u32[]{:S(2)}) collective-permute-start(bf16[256,768]{1,0:T(8,128)(2,1)} %get-tuple-element.111), channel_id=1, source_target_pairs={{0,1},{1,2},{2,3},{3,0},{4,5},{5,6},{6,7},{7,4},{8,9},{9,10},{10,1... | collective-permute-start | bytes 1179656 | tf_op jit(solution)/shard_map/ppermute | solution.py:24
  232.8 14.1 %collective-permute-start.25 = (bf16[256,768]{1,0:T(8,128)(2,1)}, bf16[256,768]{1,0:T(8,128)(2,1)S(1)}, u32[]{:S(2)}, u32[]{:S(2)}) collective-permute-start(bf16[256,768]{1,0:T(8,128)(2,1)} %add_share.12), channel_id=1, source_target_pairs={{0,1},{1,2},{2,3},{3,0},{4,5},{5,6},{6,7},{7,4},{8,9},{9,10},{10,1... | collective-permute-start | bytes 1179656 | tf_op jit(solution)/shard_map/ppermute | solution.py:24
  232.8 22.5 %collective-permute-start.27 = (bf16[256,768]{1,0:T(8,128)(2,1)S(1)}, bf16[256,768]{1,0:T(8,128)(2,1)S(1)}, u32[]{:S(2)}, u32[]{:S(2)}) collective-permute-start(bf16[256,768]{1,0:T(8,128)(2,1)S(1)} %copy-done.80), channel_id=1, source_target_pairs={{0,1},{1,2},{2,3},{3,0},{4,5},{5,6},{6,7},{7,4},{8,9},{9,10},{10,1... | collective-permute-start | bytes 1179656 | tf_op jit(solution)/shard_map/ppermute | solution.py:24
  249.5 14.1 %collective-permute-start.26 = (bf16[256,768]{1,0:T(8,128)(2,1)}, bf16[256,768]{1,0:T(8,128)(2,1)S(1)}, u32[]{:S(2)}, u32[]{:S(2)}) collective-permute-start(bf16[256,768]{1,0:T(8,128)(2,1)} %add_share.13), channel_id=1, source_target_pairs={{0,1},{1,2},{2,3},{3,0},{4,5},{5,6},{6,7},{7,4},{8,9},{9,10},{10,1... | collective-permute-start | bytes 1179656 | tf_op jit(solution)/shard_map/ppermute | solution.py:24
  257.9 18.4 %collective-permute-start.28 = (bf16[256,768]{1,0:T(8,128)(2,1)}, bf16[256,768]{1,0:T(8,128)(2,1)S(1)}, u32[]{:S(2)}, u32[]{:S(2)}) collective-permute-start(bf16[256,768]{1,0:T(8,128)(2,1)} %add_share.14), channel_id=1, source_target_pairs={{0,1},{1,2},{2,3},{3,0},{4,5},{5,6},{6,7},{7,4},{8,9},{9,10},{10,1... | collective-permute-start | bytes 1179656 | tf_op jit(solution)/shard_map/ppermute | solution.py:24
  279.1 12.7 %collective-permute-start.29 = (bf16[256,768]{1,0:T(8,128)(2,1)}, bf16[256,768]{1,0:T(8,128)(2,1)S(1)}, u32[]{:S(2)}, u32[]{:S(2)}) collective-permute-start(bf16[256,768]{1,0:T(8,128)(2,1)} %add_share.15), channel_id=1, source_target_pairs={{0,1},{1,2},{2,3},{3,0},{4,5},{5,6},{6,7},{7,4},{8,9},{9,10},{10,1... | collective-permute-start | bytes 1179656 | tf_op jit(solution)/shard_map/ppermute | solution.py:24
  281.1 19.1 %collective-permute-start.30 = (bf16[256,768]{1,0:T(8,128)(2,1)S(1)}, bf16[256,768]{1,0:T(8,128)(2,1)S(1)}, u32[]{:S(2)}, u32[]{:S(2)}) collective-permute-start(bf16[256,768]{1,0:T(8,128)(2,1)S(1)} %copy-done.79), channel_id=1, source_target_pairs={{0,1},{1,2},{2,3},{3,0},{4,5},{5,6},{6,7},{7,4},{8,9},{9,10},{10,1... | collective-permute-start | bytes 1179656 | tf_op jit(solution)/shard_map/ppermute | solution.py:24
  284.6 37.1 %collective-permute-start.38 = (bf16[256,768]{1,0:T(8,128)(2,1)S(1)}, bf16[256,768]{1,0:T(8,128)(2,1)S(1)}, u32[]{:S(2)}, u32[]{:S(2)}) collective-permute-start(bf16[256,768]{1,0:T(8,128)(2,1)S(1)} %collective-permute-done.37.refs_0_), channel_id=1, source_target_pairs={{0,1},{1,2},{2,3},{3,0},{4,5},{5,6},{6,7},{7,4},{8,9},{9,10},{10,1... | collective-permute-start | bytes 1179656 | tf_op jit(solution)/shard_map/ppermute | solution.py:24
  295.3 13.7 %collective-permute-start.40 = (f32[8,256]{1,0:T(8,128)}, f32[8,256]{1,0:T(8,128)S(1)}, u32[]{:S(2)}, u32[]{:S(2)}) collective-permute-start(f32[8,256]{1,0:T(8,128)} %get-tuple-element.118.refs_0_), channel_id=1, source_target_pairs={{0,1},{1,2},{2,3},{3,0},{4,5},{5,6},{6,7},{7,4},{8,9},{9,10},{10,1... | collective-permute-start | bytes 24584 | tf_op jit(solution)/shard_map/ppermute | solution.py:24
  295.5 13.5 %collective-permute-start.41 = (f32[8,256]{1,0:T(8,128)}, f32[8,256]{1,0:T(8,128)S(1)}, u32[]{:S(2)}, u32[]{:S(2)}) collective-permute-start(f32[8,256]{1,0:T(8,128)} %get-tuple-element.118.refs_0_), channel_id=1, source_target_pairs={{0,2},{1,3},{2,0},{3,1},{4,6},{5,7},{6,4},{7,5},{8,10},{9,11},{10,... | collective-permute-start | bytes 24584 | tf_op jit(solution)/shard_map/ppermute | solution.py:24
  302.9 19.7 %collective-permute-start.31 = (bf16[256,768]{1,0:T(8,128)(2,1)}, bf16[256,768]{1,0:T(8,128)(2,1)S(1)}, u32[]{:S(2)}, u32[]{:S(2)}) collective-permute-start(bf16[256,768]{1,0:T(8,128)(2,1)} %add_share.16), channel_id=1, source_target_pairs={{0,1},{1,2},{2,3},{3,0},{4,5},{5,6},{6,7},{7,4},{8,9},{9,10},{10,1... | collective-permute-start | bytes 1179656 | tf_op jit(solution)/shard_map/ppermute | solution.py:24
  312.0 16.3 %collective-permute-start.43 = (bf16[256,768]{1,0:T(8,128)(2,1)}, bf16[256,768]{1,0:T(8,128)(2,1)S(1)}, u32[]{:S(2)}, u32[]{:S(2)}) collective-permute-start(bf16[256,768]{1,0:T(8,128)(2,1)} %normalize.4), channel_id=1, source_target_pairs={{0,4},{4,8},{8,12},{12,16},{16,20},{20,24},{24,28},{28,0},{1,5},{5... | collective-permute-start | bytes 1179656 | tf_op jit(solution)/shard_map/ppermute | solution.py:24
  321.8 13.8 %collective-permute-start.39 = (bf16[256,768]{1,0:T(8,128)(2,1)S(1)}, bf16[256,768]{1,0:T(8,128)(2,1)S(1)}, u32[]{:S(2)}, u32[]{:S(2)}) collective-permute-start(bf16[256,768]{1,0:T(8,128)(2,1)S(1)} %collective-permute-done.38.refs_1_), channel_id=1, source_target_pairs={{0,1},{1,2},{2,3},{3,0},{4,5},{5,6},{6,7},{7,4},{8,9},{9,10},{10,1... | collective-permute-start | bytes 1179656 | tf_op jit(solution)/shard_map/ppermute | solution.py:24
  325.4 18.6 %collective-permute-start.32 = (bf16[256,768]{1,0:T(8,128)(2,1)}, bf16[256,768]{1,0:T(8,128)(2,1)S(1)}, u32[]{:S(2)}, u32[]{:S(2)}) collective-permute-start(bf16[256,768]{1,0:T(8,128)(2,1)} %add_share.17), channel_id=1, source_target_pairs={{0,1},{1,2},{2,3},{3,0},{4,5},{5,6},{6,7},{7,4},{8,9},{9,10},{10,1... | collective-permute-start | bytes 1179656 | tf_op jit(solution)/shard_map/ppermute | solution.py:24
  335.5 17.0 %collective-permute-start.44 = (bf16[256,768]{1,0:T(8,128)(2,1)S(1)}, bf16[256,768]{1,0:T(8,128)(2,1)S(1)}, u32[]{:S(2)}, u32[]{:S(2)}) collective-permute-start(bf16[256,768]{1,0:T(8,128)(2,1)S(1)} %collective-permute-done.39.refs_2_), channel_id=1, source_target_pairs={{0,1},{1,2},{2,3},{3,0},{4,5},{5,6},{6,7},{7,4},{8,9},{9,10},{10,1... | collective-permute-start | bytes 1179656 | tf_op jit(solution)/shard_map/ppermute | solution.py:24
  335.5 24.8 %collective-permute-start.45 = (bf16[256,768]{1,0:T(8,128)(2,1)S(1)}, bf16[256,768]{1,0:T(8,128)(2,1)S(1)}, u32[]{:S(2)}, u32[]{:S(2)}) collective-permute-start(bf16[256,768]{1,0:T(8,128)(2,1)S(1)} %collective-permute-done.43.refs_0_), channel_id=1, source_target_pairs={{0,1},{1,2},{2,3},{3,0},{4,5},{5,6},{6,7},{7,4},{8,9},{9,10},{10,1... | collective-permute-start | bytes 1179656 | tf_op jit(solution)/shard_map/ppermute | solution.py:24
  347.5 12.9 %collective-permute-start.47 = (f32[8,256]{1,0:T(8,128)}, f32[8,256]{1,0:T(8,128)S(1)}, u32[]{:S(2)}, u32[]{:S(2)}) collective-permute-start(f32[8,256]{1,0:T(8,128)} %get-tuple-element.126.refs_0_), channel_id=1, source_target_pairs={{0,1},{1,2},{2,3},{3,0},{4,5},{5,6},{6,7},{7,4},{8,9},{9,10},{10,1... | collective-permute-start | bytes 24584 | tf_op jit(solution)/shard_map/ppermute | solution.py:24
  347.5 13.1 %collective-permute-start.48 = (f32[8,256]{1,0:T(8,128)}, f32[8,256]{1,0:T(8,128)S(1)}, u32[]{:S(2)}, u32[]{:S(2)}) collective-permute-start(f32[8,256]{1,0:T(8,128)} %get-tuple-element.126.refs_0_), channel_id=1, source_target_pairs={{0,2},{1,3},{2,0},{3,1},{4,6},{5,7},{6,4},{7,5},{8,10},{9,11},{10,... | collective-permute-start | bytes 24584 | tf_op jit(solution)/shard_map/ppermute | solution.py:24
  347.7 12.9 %collective-permute-start.49 = (f32[8,256]{1,0:T(8,128)}, f32[8,256]{1,0:T(8,128)S(1)}, u32[]{:S(2)}, u32[]{:S(2)}) collective-permute-start(f32[8,256]{1,0:T(8,128)} %get-tuple-element.126.refs_0_), channel_id=1, source_target_pairs={{0,3},{1,0},{2,1},{3,2},{4,7},{5,4},{6,5},{7,6},{8,11},{9,8},{10,9... | collective-permute-start | bytes 24584 | tf_op jit(solution)/shard_map/ppermute | solution.py:24
  360.3 16.7 %collective-permute-start.46 = (bf16[256,768]{1,0:T(8,128)(2,1)S(1)}, bf16[256,768]{1,0:T(8,128)(2,1)S(1)}, u32[]{:S(2)}, u32[]{:S(2)}) collective-permute-start(bf16[256,768]{1,0:T(8,128)(2,1)S(1)} %collective-permute-done.45.refs_1_), channel_id=1, source_target_pairs={{0,1},{1,2},{2,3},{3,0},{4,5},{5,6},{6,7},{7,4},{8,9},{9,10},{10,1... | collective-permute-start | bytes 1179656 | tf_op jit(solution)/shard_map/ppermute | solution.py:24
  363.5 13.5 %collective-permute-start.50 = (bf16[256,768]{1,0:T(8,128)(2,1)}, bf16[256,768]{1,0:T(8,128)(2,1)S(1)}, u32[]{:S(2)}, u32[]{:S(2)}) collective-permute-start(bf16[256,768]{1,0:T(8,128)(2,1)} %normalize.5), channel_id=1, source_target_pairs={{0,4},{4,8},{8,12},{12,16},{16,20},{20,24},{24,28},{28,0},{1,5},{5... | collective-permute-start | bytes 1179656 | tf_op jit(solution)/shard_map/ppermute | solution.py:24
  374.1 22.6 %collective-permute-start.53 = (bf16[256,1536]{1,0:T(8,128)(2,1)}, bf16[256,1536]{1,0:T(8,128)(2,1)S(1)}, u32[]{:S(2)}, u32[]{:S(2)}) collective-permute-start(bf16[256,1536]{1,0:T(8,128)(2,1)} %get-tuple-element.139.refs_3_.refs_14_), channel_id=1, source_target_pairs={{0,8},{4,12},{8,0},{12,4},{16,24},{20,28},{24,16},{28,20},{1,9},{5... | collective-permute-start | bytes 2359304 | tf_op jit(solution)/shard_map/ppermute | solution.py:24
  378.2 18.5 %collective-permute-start.52 = (bf16[256,768]{1,0:T(8,128)(2,1)S(1)}, bf16[256,768]{1,0:T(8,128)(2,1)S(1)}, u32[]{:S(2)}, u32[]{:S(2)}) collective-permute-start(bf16[256,768]{1,0:T(8,128)(2,1)S(1)} %collective-permute-done.50.refs_0_), channel_id=1, source_target_pairs={{0,1},{1,2},{2,3},{3,0},{4,5},{5,6},{6,7},{7,4},{8,9},{9,10},{10,1... | collective-permute-start | bytes 1179656 | tf_op jit(solution)/shard_map/ppermute | solution.py:24
  396.7 15.0 %collective-permute-start.54 = (bf16[256,768]{1,0:T(8,128)(2,1)S(1)}, bf16[256,768]{1,0:T(8,128)(2,1)S(1)}, u32[]{:S(2)}, u32[]{:S(2)}) collective-permute-start(bf16[256,768]{1,0:T(8,128)(2,1)S(1)} %collective-permute-done.52.refs_1_), channel_id=1, source_target_pairs={{0,1},{1,2},{2,3},{3,0},{4,5},{5,6},{6,7},{7,4},{8,9},{9,10},{10,1... | collective-permute-start | bytes 1179656 | tf_op jit(solution)/shard_map/ppermute | solution.py:24
  396.7 27.5 %collective-permute-start.56 = (bf16[256,1536]{1,0:T(8,128)(2,1)S(1)}, bf16[256,1536]{1,0:T(8,128)(2,1)S(1)}, u32[]{:S(2)}, u32[]{:S(2)}) collective-permute-start(bf16[256,1536]{1,0:T(8,128)(2,1)S(1)} %collective-permute-done.53.refs_5_.refs_16_), channel_id=1, source_target_pairs={{0,16},{4,20},{24,8},{28,12},{1,17},{5,21},{25,9},{29,13},{2,18},{... | collective-permute-start | bytes 2359304 | tf_op jit(solution)/shard_map/ppermute | solution.py:24
  426.0 23.2 %collective-permute-start.58 = (bf16[768,1536]{1,0:T(8,128)(2,1)}, bf16[768,1536]{1,0:T(8,128)(2,1)S(1)}, u32[]{:S(2)}, u32[]{:S(2)}) collective-permute-start(bf16[768,1536]{1,0:T(8,128)(2,1)} %pad_maximum_fusion.3), channel_id=1, source_target_pairs={{0,4},{4,0},{8,12},{12,8},{16,20},{20,16},{24,28},{28,24},{1,5},{5... | collective-permute-start | bytes 7077896 | tf_op jit(solution)/shard_map/ppermute | solution.py:24
  426.0 20.0 %collective-permute-start.57 = (bf16[256,1536]{1,0:T(8,128)(2,1)S(1)}, bf16[256,1536]{1,0:T(8,128)(2,1)S(1)}, u32[]{:S(2)}, u32[]{:S(2)}) collective-permute-start(bf16[256,1536]{1,0:T(8,128)(2,1)S(1)} %copy-done.15), channel_id=1, source_target_pairs={{0,8},{4,12},{8,0},{12,4},{16,24},{20,28},{24,16},{28,20},{1,9},{5... | collective-permute-start | bytes 2359304 | tf_op jit(solution)/shard_map/ppermute | solution.py:24
  426.1 21.5 %collective-permute-start.59 = (bf16[256,1536]{1,0:T(8,128)(2,1)S(1)}, bf16[256,1536]{1,0:T(8,128)(2,1)S(1)}, u32[]{:S(2)}, u32[]{:S(2)}) collective-permute-start(bf16[256,1536]{1,0:T(8,128)(2,1)S(1)} %copy-done.13), channel_id=1, source_target_pairs={{4,16},{12,24},{16,4},{24,12},{5,17},{13,25},{17,5},{25,13},{6,18}... | collective-permute-start | bytes 2359304 | tf_op jit(solution)/shard_map/ppermute | solution.py:24
  426.8 22.4 %collective-permute-start.60 = (bf16[256,1536]{1,0:T(8,128)(2,1)S(1)}, bf16[256,1536]{1,0:T(8,128)(2,1)S(1)}, u32[]{:S(2)}, u32[]{:S(2)}) collective-permute-start(bf16[256,1536]{1,0:T(8,128)(2,1)S(1)} %copy-done.15), channel_id=1, source_target_pairs={{4,16},{12,24},{16,4},{24,12},{5,17},{13,25},{17,5},{25,13},{6,18}... | collective-permute-start | bytes 2359304 | tf_op jit(solution)/shard_map/ppermute | solution.py:24
  446.0 24.2 %collective-permute-start.61 = (bf16[256,1536]{1,0:T(8,128)(2,1)S(1)}, bf16[256,1536]{1,0:T(8,128)(2,1)S(1)}, u32[]{:S(2)}, u32[]{:S(2)}) collective-permute-start(bf16[256,1536]{1,0:T(8,128)(2,1)S(1)} %collective-permute-done.57.refs_11_.refs_22_), channel_id=1, source_target_pairs={{0,16},{4,20},{24,8},{28,12},{1,17},{5,21},{25,9},{29,13},{2,18},{... | collective-permute-start | bytes 2359304 | tf_op jit(solution)/shard_map/ppermute | solution.py:24
  447.3 22.8 %collective-permute-start.62 = (bf16[256,1536]{1,0:T(8,128)(2,1)}, bf16[256,1536]{1,0:T(8,128)(2,1)S(1)}, u32[]{:S(2)}, u32[]{:S(2)}) collective-permute-start(bf16[256,1536]{1,0:T(8,128)(2,1)} %get-tuple-element.143.refs_13_.refs_24_), channel_id=1, source_target_pairs={{0,8},{4,12},{8,0},{12,4},{16,24},{20,28},{24,16},{28,20},{1,9},{5... | collective-permute-start | bytes 2359304 | tf_op jit(solution)/shard_map/ppermute | solution.py:24
  447.6 22.6 %collective-permute-start.63 = (bf16[256,1536]{1,0:T(8,128)(2,1)}, bf16[256,1536]{1,0:T(8,128)(2,1)}, u32[]{:S(2)}, u32[]{:S(2)}) collective-permute-start(bf16[256,1536]{1,0:T(8,128)(2,1)} %get-tuple-element.143.refs_13_.refs_24_), channel_id=1, source_target_pairs={{4,16},{12,24},{16,4},{24,12},{5,17},{13,25},{17,5},{25,13},{6,18}... | collective-permute-start | bytes 2359304 | tf_op jit(solution)/shard_map/ppermute | solution.py:24
  475.2 20.6 %collective-permute-start.65 = (bf16[256,1536]{1,0:T(8,128)(2,1)S(1)}, bf16[256,1536]{1,0:T(8,128)(2,1)S(1)}, u32[]{:S(2)}, u32[]{:S(2)}) collective-permute-start(bf16[256,1536]{1,0:T(8,128)(2,1)S(1)} %collective-permute-done.62.refs_4_.refs_10_), channel_id=1, source_target_pairs={{0,16},{4,20},{24,8},{28,12},{1,17},{5,21},{25,9},{29,13},{2,18},{... | collective-permute-start | bytes 2359304 | tf_op jit(solution)/shard_map/ppermute | solution.py:24
  518.1 14.0 %collective-permute-start.72 = (bf16[256,768]{1,0:T(8,128)(2,1)}, bf16[256,768]{1,0:T(8,128)(2,1)S(1)}, u32[]{:S(2)}, u32[]{:S(2)}) collective-permute-start(bf16[256,768]{1,0:T(8,128)(2,1)} %get-tuple-element.154), channel_id=1, source_target_pairs={{0,1},{1,2},{2,3},{3,0},{4,5},{5,6},{6,7},{7,4},{8,9},{9,10},{10,1... | collective-permute-start | bytes 1179656 | tf_op jit(solution)/shard_map/ppermute | solution.py:24
  518.1 22.4 %collective-permute-start.76 = (bf16[256,768]{1,0:T(8,128)(2,1)}, bf16[256,768]{1,0:T(8,128)(2,1)S(1)}, u32[]{:S(2)}, u32[]{:S(2)}) collective-permute-start(bf16[256,768]{1,0:T(8,128)(2,1)} %get-tuple-element.156), channel_id=1, source_target_pairs={{0,1},{1,2},{2,3},{3,0},{4,5},{5,6},{6,7},{7,4},{8,9},{9,10},{10,1... | collective-permute-start | bytes 1179656 | tf_op jit(solution)/shard_map/ppermute | solution.py:24
  520.1 28.8 %collective-permute-start.68 = (bf16[256,768]{1,0:T(8,128)(2,1)}, bf16[256,768]{1,0:T(8,128)(2,1)S(1)}, u32[]{:S(2)}, u32[]{:S(2)}) collective-permute-start(bf16[256,768]{1,0:T(8,128)(2,1)} %get-tuple-element.152), channel_id=1, source_target_pairs={{0,1},{1,2},{2,3},{3,0},{4,5},{5,6},{6,7},{7,4},{8,9},{9,10},{10,1... | collective-permute-start | bytes 1179656 | tf_op jit(solution)/shard_map/ppermute | solution.py:24
  534.8 22.6 %collective-permute-start.73 = (bf16[256,768]{1,0:T(8,128)(2,1)}, bf16[256,768]{1,0:T(8,128)(2,1)S(1)}, u32[]{:S(2)}, u32[]{:S(2)}) collective-permute-start(bf16[256,768]{1,0:T(8,128)(2,1)} %add_share.20), channel_id=1, source_target_pairs={{0,1},{1,2},{2,3},{3,0},{4,5},{5,6},{6,7},{7,4},{8,9},{9,10},{10,1... | collective-permute-start | bytes 1179656 | tf_op jit(solution)/shard_map/ppermute | solution.py:24
  534.8 42.1 %collective-permute-start.67 = (f32[256,768]{1,0:T(8,128)S(1)}, f32[256,768]{1,0:T(8,128)S(1)}, u32[]{:S(2)}, u32[]{:S(2)}) collective-permute-start(f32[256,768]{1,0:T(8,128)S(1)} %copy-done.29), channel_id=1, source_target_pairs={{0,4},{4,8},{8,12},{12,16},{16,20},{20,24},{24,28},{28,0},{1,5},{5... | collective-permute-start | bytes 2359304 | tf_op jit(solution)/shard_map/ppermute | solution.py:24
  534.8 42.1 %collective-permute-start.71 = (f32[256,768]{1,0:T(8,128)S(1)}, f32[256,768]{1,0:T(8,128)S(1)}, u32[]{:S(2)}, u32[]{:S(2)}) collective-permute-start(f32[256,768]{1,0:T(8,128)S(1)} %copy-done.30), channel_id=1, source_target_pairs={{0,4},{4,8},{8,12},{12,16},{16,20},{20,24},{24,28},{28,0},{1,5},{5... | collective-permute-start | bytes 2359304 | tf_op jit(solution)/shard_map/ppermute | solution.py:24
  543.2 22.5 %collective-permute-start.77 = (bf16[256,768]{1,0:T(8,128)(2,1)}, bf16[256,768]{1,0:T(8,128)(2,1)S(1)}, u32[]{:S(2)}, u32[]{:S(2)}) collective-permute-start(bf16[256,768]{1,0:T(8,128)(2,1)} %add_share.22), channel_id=1, source_target_pairs={{0,1},{1,2},{2,3},{3,0},{4,5},{5,6},{6,7},{7,4},{8,9},{9,10},{10,1... | collective-permute-start | bytes 1179656 | tf_op jit(solution)/shard_map/ppermute | solution.py:24
  551.6 22.6 %collective-permute-start.69 = (bf16[256,768]{1,0:T(8,128)(2,1)}, bf16[256,768]{1,0:T(8,128)(2,1)S(1)}, u32[]{:S(2)}, u32[]{:S(2)}) collective-permute-start(bf16[256,768]{1,0:T(8,128)(2,1)} %add_share.18), channel_id=1, source_target_pairs={{0,1},{1,2},{2,3},{3,0},{4,5},{5,6},{6,7},{7,4},{8,9},{9,10},{10,1... | collective-permute-start | bytes 1179656 | tf_op jit(solution)/shard_map/ppermute | solution.py:24
  557.4 19.6 %collective-permute-start.75 = (f32[256,768]{1,0:T(8,128)S(1)}, f32[256,768]{1,0:T(8,128)S(1)}, u32[]{:S(2)}, u32[]{:S(2)}) collective-permute-start(f32[256,768]{1,0:T(8,128)S(1)} %copy-done.31), channel_id=1, source_target_pairs={{0,4},{4,8},{8,12},{12,16},{16,20},{20,24},{24,28},{28,0},{1,5},{5... | collective-permute-start | bytes 2359304 | tf_op jit(solution)/shard_map/ppermute | solution.py:24
  565.8 16.9 %collective-permute-start.74 = (bf16[256,768]{1,0:T(8,128)(2,1)}, bf16[256,768]{1,0:T(8,128)(2,1)S(1)}, u32[]{:S(2)}, u32[]{:S(2)}) collective-permute-start(bf16[256,768]{1,0:T(8,128)(2,1)} %add_share.21), channel_id=1, source_target_pairs={{0,1},{1,2},{2,3},{3,0},{4,5},{5,6},{6,7},{7,4},{8,9},{9,10},{10,1... | collective-permute-start | bytes 1179656 | tf_op jit(solution)/shard_map/ppermute | solution.py:24
  574.2 16.9 %collective-permute-start.78 = (bf16[256,768]{1,0:T(8,128)(2,1)}, bf16[256,768]{1,0:T(8,128)(2,1)S(1)}, u32[]{:S(2)}, u32[]{:S(2)}) collective-permute-start(bf16[256,768]{1,0:T(8,128)(2,1)} %add_share.23), channel_id=1, source_target_pairs={{0,1},{1,2},{2,3},{3,0},{4,5},{5,6},{6,7},{7,4},{8,9},{9,10},{10,1... | collective-permute-start | bytes 1179656 | tf_op jit(solution)/shard_map/ppermute | solution.py:24
  576.9 21.8 %collective-permute-start.70 = (bf16[256,768]{1,0:T(8,128)(2,1)}, bf16[256,768]{1,0:T(8,128)(2,1)S(1)}, u32[]{:S(2)}, u32[]{:S(2)}) collective-permute-start(bf16[256,768]{1,0:T(8,128)(2,1)} %add_share.19), channel_id=1, source_target_pairs={{0,1},{1,2},{2,3},{3,0},{4,5},{5,6},{6,7},{7,4},{8,9},{9,10},{10,1... | collective-permute-start | bytes 1179656 | tf_op jit(solution)/shard_map/ppermute | solution.py:24
  (97 other events, 1020.1 us)
